TPU v7x, 128 devices: a whole 4x4x4 slice. The times are simulated.
128 devices in a mesh: ctx: 64 (over x, z, y), fsdp: 2 (over core).
Axes of the slice: x: 4, y: 4, z: 4, core: 2. Of those that a mesh axis runs over, the one named last changes fastest.
Arguments:
- tokens: bfloat16 [2, 16384, 640], P('fsdp', 'ctx'), may hold values from -6 to 6
- positions: int32 [2, 16384], P('fsdp'), may hold values from 0 to 20479, as said below
- gain_attn: bfloat16 [640], P('fsdp'), may hold values from 0.25 to 1.75
- w_query: bfloat16 [640, 1024], P(None, 'fsdp'), may hold values from -0.25 to 0.25
- w_key: bfloat16 [640, 256], P(None, 'fsdp'), may hold values from -0.25 to 0.25
- w_value: bfloat16 [640, 256], P(None, 'fsdp'), may hold values from -0.25 to 0.25
- w_out: bfloat16 [1024, 640], P('fsdp'), may hold values from -1 to 1
- gain_ffn: bfloat16 [640], P('fsdp'), may hold values from 0.25 to 1.75
- w_gate: bfloat16 [640, 2048], P(None, 'fsdp'), may hold values from -0.25 to 0.25
- w_up: bfloat16 [640, 2048], P(None, 'fsdp'), may hold values from -0.25 to 0.25
- w_down: bfloat16 [2048, 640], P('fsdp'), may hold values from -0.125 to 0.125
- grad_out: bfloat16 [2, 16384, 640], P('fsdp', 'ctx'), may hold values from -6 to 6
Outputs:
- output: bfloat16 [2, 16384, 640], P('fsdp', 'ctx')
- grad_tokens: float32 [2, 16384, 640], P('fsdp', 'ctx')
- grad_gain_attn: float32 [640], P('fsdp')
- grad_w_query: float32 [640, 1024], P(None, 'fsdp')
- grad_w_key: float32 [640, 256], P(None, 'fsdp')
- grad_w_value: float32 [640, 256], P(None, 'fsdp')
- grad_w_out: float32 [1024, 640], P('fsdp')
- grad_gain_ffn: float32 [640], P('fsdp')
- grad_w_gate: float32 [640, 2048], P(None, 'fsdp')
- grad_w_up: float32 [640, 2048], P(None, 'fsdp')
- grad_w_down: float32 [2048, 640], P('fsdp')
Inputs may be any that keep to these rules, and one draw needn't show every extreme that they name: Along each sequence the positions start at 0 and rise by 1 or 2 from each token to the next, by 2 at exactly 4096 of the steps.
All inputs are finite; a program needn't handle non-finite values.
Results may differ from a plain program's by a relative error of at most 0.018.
Values may be sent and summed in bfloat16 or wider, within the bound.
No kernel may reach another device: no remote copies, remote signals or barrier semaphores. Data moves between devices by JAX's collectives and lax.ppermute only.
A program may use at most 128 MiB of HBM per device.

v0:
```python
import functools

import jax
import jax.numpy as jnp
from jax import lax
from jax.experimental import pallas as pl
from jax.experimental.pallas import tpu as pltpu
from jax.sharding import PartitionSpec as P

D = 640
HEADS = 4
HEAD = 256
FF = 2048
WINDOW = 512
HALF = HEAD // 2
MINE = 2 * HEAD

epsilon = 1e-06
rope_base = 10000.0
neg_fill = -1e30
score_scale = HEAD ** (-0.5)
gelu_c = 0.7978845608028654
gelu_k = 0.044715

F32 = jnp.float32
BF16 = jnp.bfloat16
MIB = 1024 * 1024


def swap(x):
    return lax.ppermute(x, "fsdp", [(0, 1), (1, 0)])


def chip_pairs(move):
    pairs = []
    for x in range(4):
        for z in range(4):
            for y in range(4):
                for c in range(2):
                    tx, tz, ty = move(x, z, y, c)
                    target = (((tx % 4) * 4 + tz % 4) * 4 + ty % 4) * 2 + c
                    pairs.append((((x * 4 + z) * 4 + y) * 2 + c, target))
    return pairs


def shift_first(by):
    return chip_pairs(lambda x, z, y, c: (x + by, z, y) if c == 0 else (x, z, y + by))


def shift_second(by):
    return chip_pairs(lambda x, z, y, c: (x, z, y + by) if c == 0 else (x + by, z, y))


def shift_z(by):
    return chip_pairs(lambda x, z, y, c: (x, z + by, y))


def after(x, *done):
    return lax.optimization_barrier((x, *done))[0]


def pair_first(z):
    return z ^ 1


def pair_second(z):
    return 3 - z


def swap_z(x, step):
    return lax.ppermute(
        x, ("ctx", "fsdp"),
        chip_pairs(lambda x, z, y, c: (x, (pair_first, pair_second)[c ^ step](z), y)),
    )


def swap_first(v, step):
    pair = (pair_first, pair_second)[step]
    return lax.ppermute(
        v, ("ctx", "fsdp"),
        chip_pairs(lambda x, z, y, c: (pair(x), z, y) if c == 0 else (x, z, pair(y))),
    )


def to_peers(parts, shift):
    return [
        lax.ppermute(part, ("ctx", "fsdp"), shift(by)) for part, by in zip(parts, (2, 1, -1))
    ]


def passed_along(shard, by):
    peers = lax.axis_size("ctx")
    pairs = [(i, i + by) for i in range(peers) if 0 <= i + by < peers]
    return lax.ppermute(shard, "ctx", pairs)


def dot(a, b):
    return lax.dot_general(a, b, (((1,), (0,)), ((), ())), preferred_element_type=F32)


def dot_nt(a, b):
    return lax.dot_general(a, b, (((1,), (1,)), ((), ())), preferred_element_type=F32)


def dot_tn(a, b):
    return lax.dot_general(a, b, (((0,), (0,)), ((), ())), preferred_element_type=F32)


def call(name, body, outs, ins, us, scalars=0, scratch=(), extra=8):
    smem = pl.BlockSpec(memory_space=pltpu.SMEM)
    whole = pl.BlockSpec(memory_space=pltpu.VMEM)
    shapes = [jax.ShapeDtypeStruct(s, t) for s, t in outs]
    held = sum(x.size * x.dtype.itemsize for x in [*ins, *shapes])
    return pl.pallas_call(
        body,
        out_shape=shapes,
        in_specs=[smem] * scalars
        + [whole] * (len(ins) - scalars),
        out_specs=[whole] * len(outs),
        scratch_shapes=scratch,
        compiler_params=pltpu.CompilerParams(vmem_limit_bytes=held + extra * MIB),
        cost_estimate=pl.CostEstimate(
            flops=int(us * 1.1e9), bytes_accessed=1024, transcendentals=0
        ),
        name=name,
    )(*ins)


def inv_rms(x):
    return lax.rsqrt(jnp.mean(x * x, axis=-1, keepdims=True) + epsilon)


def rotate_pair(a, b, c, s):
    return a * c - b * s, b * c + a * s


def allowed_pairs(pos_row):
    keys = pos_row[...].astype(F32)
    own = jnp.broadcast_to(keys[:, 512:], (128, 256)).T[:, :1]
    distance = own - keys
    return (distance >= 0) & (distance < WINDOW)


def query_body(
    where, tok, gain, wq_m, wq_o, wk_m, wk_o, wv_m, wv_o, wo, cos, sin,
    normed, query, wkv, wide, wo_near,
):
    x = tok[...].astype(F32)
    wide[...] = x
    wo_near[...] = wo[...]
    n = (x * inv_rms(x) * gain[...]).astype(BF16)
    normed[...] = n
    c, s = cos[512:, :], sin[512:, :]
    for half, w in enumerate((wq_m, wq_o)):
        raw = dot(n, w[...])
        for head in range(2):
            a = raw[:, head * HEAD : head * HEAD + HALF]
            b = raw[:, head * HEAD + HALF : (head + 1) * HEAD]
            ra, rb = rotate_pair(a, b, c, s)
            at = half * MINE + head * HEAD
            query[:, at : at + HALF] = (ra * score_scale).astype(BF16)
            query[:, at + HALF : at + HEAD] = (rb * score_scale).astype(BF16)
    for which, (a, b, c, d) in enumerate(((wk_m, wk_o, wv_m, wv_o), (wk_o, wk_m, wv_o, wv_m))):

        @pl.when(where[0] == which)
        def _(parts=(a, b, c, d)):
            for i, part in enumerate(parts):
                wkv[:, i * HALF : (i + 1) * HALF] = part[...]


def attend_body(
    far_two, far_one, normed, wide, query, wkv, gain, wo_m, wo_o, gain_two, cos, sin, pos_row,
    normed_all, query_kept, kv, ctx_m, ctx_o, lse, after, normed_two,
):
    query_kept[...] = query[...]
    normed_all[512:, :] = normed[...]
    for i, far in enumerate((far_two, far_one)):
        x = far[...].astype(F32)
        normed_all[i * 256 : (i + 1) * 256, :] = (x * inv_rms(x) * gain[...]).astype(BF16)
    raw = dot(normed_all[...], wkv[...])
    ka, kb = rotate_pair(raw[:, :HALF], raw[:, HALF:HEAD], cos[...], sin[...])
    kv[:, :HALF] = ka.astype(BF16)
    kv[:, HALF:HEAD] = kb.astype(BF16)
    kv[:, HEAD:] = raw[:, HEAD:].astype(BF16)
    ok = allowed_pairs(pos_row)
    for head in range(HEADS):
        cols = slice(head * HEAD, (head + 1) * HEAD)
        scores = jnp.where(ok, dot_nt(query[:, cols], kv[:, :HEAD]), neg_fill)
        top = jnp.max(scores, axis=-1, keepdims=True)
        exps = jnp.exp(scores - top)
        total = jnp.sum(exps, axis=-1, keepdims=True)
        lse[:, head * 128 : (head + 1) * 128] = jnp.broadcast_to(top + jnp.log(total), (256, 128))
        probs = (exps * (1.0 / total)).astype(BF16)
        context = (ctx_m, ctx_o)[head // 2]
        at = head % 2 * HEAD
        context[:, at : at + HEAD] = dot(probs, kv[:, HEAD:]).astype(BF16)
    h = wide[...] + (dot(ctx_m[...], wo_m[...]) + dot(ctx_o[...], wo_o[...]))
    after[...] = h
    normed_two[...] = (h * inv_rms(h) * gain_two[...]).astype(BF16)


FFN_STEP = 512


def ffn_half(n, y, wg, wu, wd, hid, dg, du):
    total = None
    grad_n = None
    for at in range(0, FF // 2, FFN_STEP):
        cols = slice(at, at + FFN_STEP)
        gate = dot(n, wg[:, cols])
        up = dot(n, wu[:, cols])
        grad_hidden = dot_nt(y, wd[cols, :])
        square = gate * gate
        t = jnp.tanh(gelu_c * gate * (1.0 + gelu_k * square))
        one_t = 0.5 + 0.5 * t
        act = gate * one_t
        slope = one_t + 0.5 * gate * (1.0 - t * t) * (gelu_c * (1.0 + 3.0 * gelu_k * square))
        hidden = (act * up).astype(BF16)
        grad_gate = (grad_hidden * up * slope).astype(BF16)
        grad_up = (grad_hidden * act).astype(BF16)
        hid[:, cols] = hidden
        dg[:, cols] = grad_gate
        du[:, cols] = grad_up
        part = dot(hidden, wd[cols, :])
        total = part if total is None else total + part
        part = dot_nt(grad_gate, wg[:, cols]) + dot_nt(grad_up, wu[:, cols])
        grad_n = part if grad_n is None else grad_n + part
    return total, grad_n


def ffn_other_body(normed_two, gy, wg, wu, wd, hid, dg, du, total, grad_n):
    total[...], grad_n[...] = ffn_half(normed_two[...], gy[...], wg, wu, wd, hid, dg, du)


def ffn_body(
    after, normed_two, gain_two, gy, wg, wu, wd, total_o, grad_n_o,
    out, hid, dg, du, grad_after, grad_after_low, grad_gain,
):
    y = gy[...]
    total, grad_n = ffn_half(normed_two[...], y, wg, wu, wd, hid, dg, du)
    grad_n = grad_n + grad_n_o[...]
    h = after[...]
    out[...] = (h + (total + total_o[...])).astype(BF16)
    r = inv_rms(h)
    dn = grad_n * gain_two[...]
    grad_gain[...] = jnp.sum(grad_n * h * r, axis=0, keepdims=True)
    ga = y.astype(F32) + r * dn - h * (r * r * r * jnp.mean(dn * h, axis=-1, keepdims=True))
    grad_after[...] = ga
    grad_after_low[...] = ga.astype(BF16)


ORDER = (0, 2, 1, 3)
F_ROWS = 3840
A_ROWS = 1664


def place(i, by):
    return lax.rem(i + by, 4)


def z_places(core, z):
    one = z + 1 - 2 * lax.rem(z, 2)
    other = 3 - z
    first = jnp.where(core == 0, one, other)
    second = jnp.where(core == 0, other, one)
    return z, second, first, 2 - z + 2 * lax.rem(z, 2)


def ffn_grads_body(
    where, hid_m, hid_r, dg_m, dg_r, du_m, du_r, n, n_r, gy, gy_r, out_0, out_1, out_2, out_3, turned
):
    first = where[1]
    turned[:, :256] = n[...].T
    turned[:, 256:] = n_r[...].T
    for out, by in zip((out_0, out_1, out_2, out_3), ORDER):
        j = place(first, by)
        cols = pl.ds(pl.multiple_of(j * 256, 256), 256)
        for at, left, right in ((0, dg_m, dg_r), (1280, du_m, du_r)):
            g = dot(turned[:, :256], left[:, cols]) + dot(turned[:, 256:], right[:, cols])
            out[at : at + 640, :] = g[:, :128].astype(BF16)
            out[at + 640 : at + 1280, :] = g[:, 128:].astype(BF16)
        g = dot_tn(hid_m[:, cols], gy[...]) + dot_tn(hid_r[:, cols], gy_r[...])
        for b in range(5):
            out[2560 + b * 256 : 2816 + b * 256, :] = g[:, b * 128 : (b + 1) * 128].astype(BF16)


def attend_grad_body(
    where, query, kv, lse, ga_low, wo_m, wo_o, cos, sin, pos_row,
    dq_m, dq_o, dkv, dkv_m, packed,
):
    dkv_o = packed.at[512:, :]
    ok = allowed_pairs(pos_row)
    ga = ga_low[...]
    grad_k = None
    grad_v = None
    c, s = cos[512:, :], sin[512:, :]
    for half, wo, dq in ((1, wo_o, dq_o), (0, wo_m, dq_m)):
        grad_context = dot_nt(ga, wo[...]).astype(BF16)
        for head in range(2):
            cols = slice(half * MINE + head * HEAD, half * MINE + (head + 1) * HEAD)
            q = query[:, cols]
            gc = grad_context[:, head * HEAD : (head + 1) * HEAD]
            which = half * 2 + head
            scores = jnp.where(ok, dot_nt(q, kv[:, :HEAD]), neg_fill)
            probs = jnp.exp(scores - lse[:, which * 128 : which * 128 + 1])
            part = dot_tn(probs.astype(BF16), gc)
            grad_v = part if grad_v is None else grad_v + part
            grad_probs = dot_nt(gc, kv[:, HEAD:])
            row_dot = jnp.sum(grad_probs * probs, axis=-1, keepdims=True)
            grad_scores = (probs * (grad_probs - row_dot)).astype(BF16)
            gq = dot(grad_scores, kv[:, :HEAD]) * score_scale
            a, b = rotate_pair(gq[:, :HALF], gq[:, HALF:], c, -s)
            dq[:, head * HEAD : head * HEAD + HALF] = a.astype(BF16)
            dq[:, head * HEAD + HALF : (head + 1) * HEAD] = b.astype(BF16)
            part = dot_tn(grad_scores, q)
            grad_k = part if grad_k is None else grad_k + part
    a, b = rotate_pair(grad_k[:, :HALF], grad_k[:, HALF:], cos[...], -sin[...])
    packed[:256, :] = dq_o[:, :HEAD]
    packed[256:512, :] = dq_o[:, HEAD:]
    dkv[:, :HALF] = a.astype(BF16)
    dkv[:, HALF:HEAD] = b.astype(BF16)
    dkv[:, HEAD:] = grad_v.astype(BF16)
    even = where[0] == 0
    dkv_m[:, :HALF] = jnp.where(even, a, b).astype(BF16)
    dkv_o[:, :HALF] = jnp.where(even, b, a).astype(BF16)
    va, vb = grad_v[:, :HALF], grad_v[:, HALF:]
    dkv_m[:, HALF:] = jnp.where(even, va, vb).astype(BF16)
    dkv_o[:, HALF:] = jnp.where(even, vb, va).astype(BF16)


def attend_grads_body(
    where, n, n_r, dq_m, dkv_m, packed, ctx, ctx_r, ga, ga_r, wq, wk, wv,
    gain, gain_two_grad, out_0, out_1, out_2, out_3, turned,
):
    turned[:, :768] = n[...].T
    turned[:, 768:] = n_r[...].T
    gk = dot(turned[:, :768], dkv_m[...]) + dot(turned[:, 768:], packed[512:, :])
    weighed = gk[:, :HALF] * wk[...].astype(F32) + gk[:, HALF:] * wv[...].astype(F32)
    gk = gk.astype(BF16)
    for out, j in zip((out_0, out_1, out_2, out_3), z_places(where[0], where[3])):
        cols = pl.ds(pl.multiple_of(j * 128, 128), 128)
        rows = pl.ds(pl.multiple_of(j // 2 * 256, 256), 256)
        half = pl.ds(pl.multiple_of(j % 2 * 128, 128), 128)
        g = dot(turned[:, 512:768], dq_m[:, cols]) + dot(turned[:, 1280:], packed[rows, half])
        weighed = weighed + g * wq[:, cols].astype(F32)
        out[:640, :] = g.astype(BF16)
        g = dot_tn(ctx[:, cols], ga[...]) + dot_tn(ctx_r[:, cols], ga_r[...])
        for b in range(5):
            out[960 + b * 128 : 1088 + b * 128, :] = g[:, b * 128 : (b + 1) * 128].astype(BF16)
        for at in range(4):

            @pl.when(j == at)
            def _(out=out, at=at):
                out[640:800, :] = gk[at * 160 : (at + 1) * 160, :HALF]
                out[800:960, :] = gk[at * 160 : (at + 1) * 160, HALF:]

    by_row = jnp.broadcast_to(jnp.sum(weighed, axis=1, keepdims=True), (640, 128))
    one = by_row.T[:1, :] / gain[...]
    two = gain_two_grad[...]
    rows = [v[:, b * 128 : (b + 1) * 128] for v in (one, two) for b in range(5)]
    block = jnp.concatenate([*rows, jnp.zeros((6, 128), F32)], axis=0).astype(BF16)
    for out in (out_0, out_1, out_2, out_3):
        out[1600:1616, :] = block
        out[1616:, :] = jnp.zeros((48, 128), BF16)


def token_grad_body(
    tok, gain, grad_after, dq_m, dq_o, dkv, back_one, back_two, wq_m, wq_o, wkv, out
):
    back = back_one[...].astype(F32) + back_two[...].astype(F32)
    own = (dkv[512:, :].astype(F32) + back).astype(BF16)
    gn = dot_nt(dq_m[...], wq_m[...]) + dot_nt(dq_o[...], wq_o[...]) + dot_nt(own, wkv[...])
    x = tok[...].astype(F32)
    r = inv_rms(x)
    dm = gn * gain[...]
    out[...] = grad_after[...] + r * dm - x * (
        r * r * r * jnp.mean(dm * x, axis=-1, keepdims=True)
    )


def add_low(*terms):
    total = terms[0].astype(F32)
    for term in terms[1:]:
        total = total + term.astype(F32)
    return total.astype(BF16)


F_PART, A_PART = F_ROWS // 4, A_ROWS // 4
PART = F_PART + A_PART


def split_sum_body(
    where, own, r_two, r_one, r_minus, a_own, a_one, a_last, out_0, out_1, out_2, out_3
):
    for out, by in zip((out_0, out_1, out_2, out_3), ORDER):
        j = place(where[2], by)
        at = pl.ds(pl.multiple_of(j * F_PART, F_PART), F_PART)
        total = (own[at, :].astype(F32) + r_two[at, :].astype(F32)) + (
            r_one[at, :].astype(F32) + r_minus[at, :].astype(F32)
        )
        out[:F_PART, :] = total.astype(BF16)
        at = pl.ds(pl.multiple_of(j * A_PART, A_PART), A_PART)
        total = a_own[at, :].astype(F32) + a_one[at, :].astype(F32) + a_last[at, :].astype(F32)
        out[F_PART:, :] = total.astype(BF16)


def sum_four(own, r_two, r_one, r_minus):
    total = (own.astype(F32) + r_two.astype(F32)) + (r_one.astype(F32) + r_minus.astype(F32))
    return total.astype(BF16)


def join_body(where, own, r_two, r_one, r_minus, f_out, a_out):
    for ref, by in ((own, 0), (r_two, 2), (r_one, 3), (r_minus, 1)):
        j = place(where[2], by)
        f_out[pl.ds(pl.multiple_of(j * F_PART, F_PART), F_PART), :] = ref[:F_PART, :]
        a_out[pl.ds(pl.multiple_of(j * A_PART, A_PART), A_PART), :] = ref[F_PART:, :]


def ffn_spread_body(by, fresh, where, piece, *refs):
    gate, up, down, gate_wide, up_wide, down_wide, sems = refs if fresh else refs[3:]
    j = place(where[1], by)
    copies = []
    cols = pl.ds(pl.multiple_of(j * 256, 256), 256)
    for i, (at, wide, target) in enumerate(((0, gate_wide, gate), (1280, up_wide, up))):
        for b in range(2):
            wide[:, b * 128 : (b + 1) * 128] = piece[
                at + b * 640 : at + (b + 1) * 640, :
            ].astype(F32)
        copies.append(pltpu.make_async_copy(wide, target.at[:, cols], sems.at[i]))
        copies[-1].start()
    for b in range(5):
        down_wide[:, b * 128 : (b + 1) * 128] = piece[2560 + b * 256 : 2816 + b * 256, :].astype(F32)
    copies.append(pltpu.make_async_copy(down_wide, down.at[cols, :], sems.at[2]))
    copies[-1].start()
    for copy in copies:
        copy.wait()


def ffn_spread(where, pieces):
    outs = [jax.ShapeDtypeStruct(s, F32) for s in ((D, FF // 2), (D, FF // 2), (FF // 2, D))]
    anywhere = pl.BlockSpec(memory_space=pl.ANY)
    shards = []
    for piece, by in zip(pieces, (0, 2, 3, 1)):
        shards = pl.pallas_call(
            functools.partial(ffn_spread_body, by, not shards),
            out_shape=outs,
            in_specs=[
                pl.BlockSpec(memory_space=pltpu.SMEM), pl.BlockSpec(memory_space=pltpu.VMEM),
                *[anywhere] * len(shards),
            ],
            out_specs=[anywhere] * 3,
            input_output_aliases={2 + i: i for i in range(len(shards))},
            scratch_shapes=[
                pltpu.VMEM((D, 256), F32), pltpu.VMEM((D, 256), F32), pltpu.VMEM((256, D), F32),
                pltpu.SemaphoreType.DMA((3,)),
            ],
            compiler_params=pltpu.CompilerParams(vmem_limit_bytes=8 * MIB),
            cost_estimate=pl.CostEstimate(flops=1024, bytes_accessed=1024, transcendentals=0),
            name="f_spread",
        )(where, piece, *shards)
    return shards


def attend_spread_body(where, own, r_two, r_one, r_minus, query, key, value, out, gains):
    for ref, by in ((own, 0), (r_two, 2), (r_one, 3), (r_minus, 1)):
        j = place(where[3], by)
        query[:, pl.ds(pl.multiple_of(j * 128, 128), 128)] = ref[:640, :].astype(F32)
        rows = pl.ds(pl.multiple_of(j * 160, 160), 160)
        key[rows, :] = ref[640:800, :].astype(F32)
        value[rows, :] = ref[800:960, :].astype(F32)
        rows = pl.ds(pl.multiple_of(j * 128, 128), 128)
        for b in range(5):
            out[rows, b * 128 : (b + 1) * 128] = ref[960 + b * 128 : 1088 + b * 128, :].astype(F32)
    gains[...] = own[1600:1616, :].astype(F32)


def local(
    tokens, positions, gain_attn, w_query, w_key, w_value, w_out, gain_ffn, w_gate, w_up, w_down,
    grad_out,
):
    tok = tokens[0]
    gy = grad_out[0]
    rows = tok.shape[0]
    ctx = lax.axis_index("ctx")
    core = lax.axis_index("fsdp")
    x_at, y_at = ctx // 16, ctx % 4
    where = jnp.stack(
        [core, jnp.where(core == 0, x_at, y_at), jnp.where(core == 0, y_at, x_at), ctx // 4 % 4]
    ).astype(jnp.int32)
    even = core == 0

    far_one = passed_along(tok, 1)
    far_two = passed_along(tok, 2)
    gains = jnp.concatenate([gain_attn, gain_ffn]).reshape(1, D)
    gains_other = swap(gains)
    key_other, value_other = swap(w_key), swap(w_value)
    query_other = swap(after(w_query, gains_other))
    out_other = swap(after(w_out, key_other))

    low = jnp.where(even, gains, gains_other)
    high = jnp.where(even, gains_other, gains)
    half_d = D // 2
    gain_one = jnp.concatenate([low[:, :half_d], high[:, :half_d]], axis=1).astype(F32)
    gain_two = jnp.concatenate([low[:, half_d:], high[:, half_d:]], axis=1).astype(F32)
    seq_pos = positions[0]
    key_pos = lax.dynamic_slice_in_dim(
        jnp.concatenate([jnp.full((2 * rows,), -2 * WINDOW, jnp.int32), seq_pos]), ctx * rows,
        3 * rows,
    )
    pos_row = key_pos.reshape(1, 3 * rows)
    frequency = rope_base ** (-(jnp.arange(HALF, dtype=F32) * 2.0 / HEAD))
    angles = key_pos.astype(F32)[:, None] * frequency[None, :]
    cos, sin = jnp.cos(angles), jnp.sin(angles)

    gy_r = swap(after(gy, value_other))
    normed, query, wkv, wide, wo_near = call(
        "query", query_body,
        [
            ((rows, D), BF16), ((rows, HEADS * HEAD), BF16), ((D, 2 * HEAD), BF16),
            ((rows, D), F32), ((MINE, D), BF16),
        ],
        [
            where, after(tok, gain_two, pos_row), gain_one, w_query, query_other, w_key,
            key_other, w_value, value_other, w_out, cos, sin,
        ],
        us=6, scalars=1,
    )
    first = (normed, far_one, far_two, out_other, gy_r)
    gate_other = swap(after(w_gate, *first))
    up_other = swap(after(w_up, *first))
    down_other = swap(after(w_down, *first))
    normed_all, query, kv, ctx_m, ctx_o, lse, after_attn, normed_two = call(
        "attend", attend_body,
        [
            ((3 * rows, D), BF16), ((rows, HEADS * HEAD), BF16), ((3 * rows, 2 * HEAD), BF16),
            ((rows, MINE), BF16), ((rows, MINE), BF16), ((rows, 512), F32), ((rows, D), F32),
            ((rows, D), BF16),
        ],
        [
            far_two, far_one, normed, wide, query, wkv, gain_one, wo_near, out_other, gain_two,
            cos, sin, pos_row,
        ],
        us=5,
    )
    normed_two_r = swap(normed_two)
    ctx_r, normed_r = swap(ctx_o), swap(normed_all)
    half_ffn = [((rows, FF // 2), BF16)] * 3
    hid_o, dg_o, du_o, total_o, grad_n_o = call(
        "ffn_other", ffn_other_body, [*half_ffn, ((rows, D), F32), ((rows, D), F32)],
        [normed_two, gy, gate_other, up_other, down_other],
        us=5,
    )
    gain_two = after(gain_two, normed_two_r, ctx_r, normed_r)
    hid_r, dg_r, du_r = swap(hid_o), swap(dg_o), swap(du_o)
    out, hid_m, dg_m, du_m, grad_after, ga_low, grad_gain_two = call(
        "ffn", ffn_body,
        [((rows, D), BF16), *half_ffn, ((rows, D), F32), ((rows, D), BF16), ((1, D), F32)],
        [after_attn, normed_two, gain_two, gy, w_gate, w_up, w_down, total_o, grad_n_o],
        us=4,
    )
    ga_r = swap(ga_low)
    dq_m, dq_o, dkv, dkv_m, packed = call(
        "attend_grad", attend_grad_body,
        [
            ((rows, MINE), BF16), ((rows, MINE), BF16), ((3 * rows, 2 * HEAD), BF16),
            ((3 * rows, HEAD), BF16), ((5 * rows, HEAD), BF16),
        ],
        [
            where, query, kv, lse, ga_low, w_out, out_other, cos, sin, pos_row,
        ],
        us=0, scalars=1,
    )
    packed_r = swap(packed)
    f_chunks = call(
        "ffn_grads", ffn_grads_body, [((F_ROWS, 128), BF16)] * 4,
        [where, after(hid_m, packed), hid_r, dg_m, dg_r, du_m, du_r, normed_two, normed_two_r, gy, gy_r],
        scalars=1, scratch=[pltpu.VMEM((D, 512), BF16)],
        us=3,
    )
    f_got = to_peers(f_chunks[1:], shift_first)

    a_chunks = call(
        "attend_grads", attend_grads_body, [((A_ROWS, 128), BF16)] * 4,
        [
            where, normed_all, normed_r, after(dq_m, f_chunks[0]), dkv_m, packed_r, ctx_m, ctx_r, ga_low, ga_r,
            w_query, w_key, w_value, gain_one, grad_gain_two,
        ],
        us=0, scalars=1, scratch=[pltpu.VMEM((D, 6 * rows), BF16)],
    )
    a_own, a_next, a_far_own, a_far_next = a_chunks
    a_next_r, a_own_r = swap_z(a_far_next, 0), swap_z(a_far_own, 0)
    a_last_r = swap_z(add_low(a_next, a_next_r), 1)
    parts = call(
        "split", split_sum_body, [((PART, 128), BF16)] * 4,
        [where, after(f_chunks[0], a_own), *f_got, a_own, a_own_r, a_last_r], us=0, scalars=1,
    )
    got = [parts[0], *to_peers(parts[1:], shift_second)]
    f_two = sum_four(*[part[:F_PART] for part in got])
    a_two = sum_four(*[part[F_PART:] for part in got])
    f_pair = add_low(f_two, swap_z(f_two, 0))
    a_pair = add_low(a_two, swap_first(a_two, 0))
    f_three = add_low(f_pair, swap_z(f_pair, 1))
    a_three = add_low(a_pair, swap_first(a_pair, 1))
    back_two = passed_along(after(dkv[:rows], f_two), -2)
    back_one = passed_along(after(dkv[rows : 2 * rows], f_two), -1)
    own = after(jnp.concatenate([f_three, a_three]), back_one, back_two)
    f_whole, a_whole = call(
        "join", join_body, [((F_ROWS, 128), BF16), ((A_ROWS, 128), BF16)],
        [where, own, *to_peers([own] * 3, shift_second)], us=0, scalars=1,
    )
    f_sums = [f_whole, *to_peers([f_whole] * 3, shift_first)]
    a_sums = [a_whole, *to_peers([a_whole] * 3, shift_z)]
    grad_tokens = call(
        "token_grad", token_grad_body, [((rows, D), F32)],
        [
            tok, gain_one, grad_after, dq_m, dq_o, dkv, back_one, back_two, w_query, query_other,
            wkv,
        ],
        us=2,
    )[0]

    g_query, g_key, g_value, g_out, g_gains = call(
        "a_spread", attend_spread_body,
        [((D, MINE), F32), ((D, HALF), F32), ((D, HALF), F32), ((MINE, D), F32), ((16, 128), F32)],
        [where, *a_sums], scalars=1,
        us=2.5,
    )
    g_gate, g_up, g_down = ffn_spread(where, f_sums)
    g_gains = (g_gains + swap(g_gains))[:10].reshape(2, D)
    g_gains = jnp.where(even, g_gains[:, :half_d], g_gains[:, half_d:])
    return (
        out[None], grad_tokens[None], g_gains[0], g_query, g_key, g_value, g_out, g_gains[1],
        g_gate, g_up, g_down,
    )


def solution(mesh):
    tokens = P("fsdp", "ctx", None)
    columns, rows = P(None, "fsdp"), P("fsdp", None)
    in_specs = (
        tokens, P("fsdp", None), P("fsdp"), columns, columns, columns, rows, P("fsdp"), columns,
        columns, rows, tokens,
    )
    out_specs = (
        tokens, tokens, P("fsdp"), columns, columns, columns, rows, P("fsdp"), columns, columns,
        rows,
    )
    return jax.shard_map(local, mesh=mesh, in_specs=in_specs, out_specs=out_specs, check_vma=False)
```

profile of v0, /device:TPU:0, one launch (start us, length us, event | category | flops | bytes accessed | tf_op | source)
XLA Modules:
  0.0 170.7 jit_solution(14503264765496691835)
XLA Ops:
  0.6 5.2 %collective-permute-start = (bf16[256,640]{1,0:T(8,128)(2,1)}, bf16[256,640]{1,0:T(8,128)(2,1)S(1)}, u32[]{:S(2)}, u32[]{:S(2)}) collective-permute-start(bf16[256,640]{1,0:T(8,128)(2,1)} %bitcast.13), channel_id=1, source_target_pairs={{0,4},{2,6},{4,8},{6,10},{8,12},{10,14},{12,16},{14,18},{16,20},{1... | collective-permute-start | bytes 983048 | tf_op jit(solution)/shard_map/ppermute | solution.py:94
  5.9 2.6 %collective-permute-start.1 = (bf16[256,640]{1,0:T(8,128)(2,1)}, bf16[256,640]{1,0:T(8,128)(2,1)S(1)}, u32[]{:S(2)}, u32[]{:S(2)}) collective-permute-start(bf16[256,640]{1,0:T(8,128)(2,1)} %bitcast.14), channel_id=1, source_target_pairs={{0,2},{2,4},{4,6},{6,8},{8,10},{10,12},{12,14},{14,16},{16,18},{18... | collective-permute-start | bytes 983048 | tf_op jit(solution)/shard_map/ppermute | solution.py:94
  22.1 3.2 %attend.1 = (bf16[768,640]{1,0:T(8,128)(2,1)S(1)}, bf16[256,1024]{1,0:T(8,128)(2,1)S(1)}, bf16[768,512]{1,0:T(8,128)(2,1)S(1)}, bf16[256,512]{1,0:T(8,128)(2,1)S...) custom-call(bf16[256,640]{1,0:T(8,128)(2,1)S(1)} %collective-permute, ...), custom_call_target="tpu_custom_call" | custom-call | flops 5500000256 | bytes 1024 | tf_op jit(solution)/shard_map/attend/pallas_call | solution.py:114
  25.9 3.8 %collective-permute-done.8.ctx_r = bf16[256,512]{1,0:T(8,128)(2,1)S(1)} collective-permute-done((bf16[256,512]{1,0:T(8,128)(2,1)S(1)}, bf16[256,512]{1,0:T(8,128)(2,1)S(1)}, u32[]{:S(2)}, u32[]{:S(2)}) %collective-permute-start.8) | collective-permute-done | bytes 262176 | tf_op jit(solution)/shard_map/ppermute | solution.py:31
  31.4 3.1 %ffn_other.1 = (bf16[256,1024]{1,0:T(8,128)(2,1)S(1)}, bf16[256,1024]{1,0:T(8,128)(2,1)S(1)}, bf16[256,1024]{1,0:T(8,128)(2,1)S(1)}, f32[256,640]{1,0:T(8,128)S(1)}, f32[256,640]{1,0:T(8,128)S(1)}) custom-call(bf16[256,640]{1,0:T(8,128)(2,1)S(1)} %get-tuple-element.95.normed_two.n, bf16[256,640]{1,0:T(8,128)(2,1)S(1)} %bitcast.10, ...), custom_call_target="tpu_custom_call" | custom-call | flops 5500000256 | bytes 1024 | tf_op jit(solution)/shard_map/ffn_other/pallas_call | solution.py:114
  35.5 4.1 %ffn.1 = (bf16[256,640]{1,0:T(8,128)(2,1)}, bf16[256,1024]{1,0:T(8,128)(2,1)S(1)}, bf16[256,1024]{1,0:T(8,128)(2,1)S(1)}, bf16[256,1024]{1,0:T(8,128)(2,1)S(1)},...) custom-call(f32[256,640]{1,0:T(8,128)S(1)} %get-tuple-element.94.after, ...), custom_call_target="tpu_custom_call" | custom-call | flops 4400000000 | bytes 1024 | tf_op jit(solution)/shard_map/ffn/pallas_call | solution.py:114
  39.6 4.4 %attend_grad.1 = (bf16[256,512]{1,0:T(8,128)(2,1)S(1)}, bf16[256,512]{1,0:T(8,128)(2,1)S(1)}, bf16[768,512]{1,0:T(8,128)(2,1)S(1)}, bf16[768,256]{1,0:T(8,128)(2,1)S(1)}, bf16[1280,256]{1,0:T(8,128)(2,1)S(1)}) custom-call(s32[4]{0:T(128)S(1)} %pad_add_fusion.where, bf16[256,1024]{1,0:T(8,128)(2,1)S(1)} %get-tuple-element.107.query, ...), custom_call_target="tpu_custom_call" | custom-call | bytes 1024 | tf_op jit(solution)/shard_map/attend_grad/pallas_call | solution.py:114
  44.7 2.9 %ffn_grads.1 = (bf16[3840,128]{1,0:T(8,128)(2,1)S(1)}, bf16[3840,128]{1,0:T(8,128)(2,1)S(1)}, bf16[3840,128]{1,0:T(8,128)(2,1)S(1)}, bf16[3840,128]{1,0:T(8,128)(2,1)S(1)}) custom-call(s32[4]{0:T(128)S(1)} %pad_add_fusion.where, bf16[256,1024]{1,0:T(8,128)(2,1)S(1)} %get-tuple-element.116.hid_m, bf16[256,1024]{1,0:T(8,128)(2,1)S(1)} %collective-permute-done.14.hid_r, ...), custom_call_target="tpu_custom_call" | custom-call | flops 3300000000 | bytes 1024 | tf_op jit(solution)/shard_map/ffn_grads/pallas_call | solution.py:114
  47.7 4.0 %attend_grads.1 = (bf16[1664,128]{1,0:T(8,128)(2,1)S(1)}, bf16[1664,128]{1,0:T(8,128)(2,1)S(1)}, bf16[1664,128]{1,0:T(8,128)(2,1)S(1)}, bf16[1664,128]{1,0:T(8,128)(2,1)S(1)}) custom-call(s32[4]{0:T(128)S(1)} %pad_add_fusion.where, bf16[768,640]{1,0:T(8,128)(2,1)S(1)} %get-tuple-element.97.n, bf16[768,640]{1,0:T(8,128)(2,1)S(1)} %collective-permute-done.9.n_r, ...), custom_call_target="tpu_custom_call" | custom-call | bytes 1024 | tf_op jit(solution)/shard_map/attend_grads/pallas_call | solution.py:114
  51.6 2.6 %collective-permute-start.23 = (bf16[1664,128]{1,0:T(8,128)(2,1)S(1)}, bf16[1664,128]{1,0:T(8,128)(2,1)S(1)}, u32[]{:S(2)}, u32[]{:S(2)}) collective-permute-start(bf16[1664,128]{1,0:T(8,128)(2,1)S(1)} %get-tuple-element.134), channel_id=1, source_target_pairs={{0,8},{1,25},{2,10},{3,27},{4,12},{5,29},{6,14},{7,31},{8,0},{9,17... | collective-permute-start | bytes 1277960 | tf_op jit(solution)/shard_map/ppermute | solution.py:71
  54.2 4.0 %collective-permute-start.19 = (bf16[3840,128]{1,0:T(8,128)(2,1)S(1)}, bf16[3840,128]{1,0:T(8,128)(2,1)S(1)}, u32[]{:S(2)}, u32[]{:S(2)}) collective-permute-start(bf16[3840,128]{1,0:T(8,128)(2,1)S(1)} %get-tuple-element.129), channel_id=1, source_target_pairs={{0,64},{1,5},{2,66},{3,7},{4,68},{5,1},{6,70},{7,3},{8,72},{9,13},... | collective-permute-start | bytes 2949128 | tf_op jit(solution)/shard_map/ppermute | solution.py:87
  58.9 2.6 %collective-permute-start.21 = (bf16[3840,128]{1,0:T(8,128)(2,1)S(1)}, bf16[3840,128]{1,0:T(8,128)(2,1)S(1)}, u32[]{:S(2)}, u32[]{:S(2)}) collective-permute-start(bf16[3840,128]{1,0:T(8,128)(2,1)S(1)} %get-tuple-element.131), channel_id=1, source_target_pairs={{0,96},{1,7},{2,98},{3,1},{4,100},{5,3},{6,102},{7,5},{8,104},{9,1... | collective-permute-start | bytes 2949128 | tf_op jit(solution)/shard_map/ppermute | solution.py:87
  64.8 9.2 %collective-permute-done.22.a_one = bf16[1664,128]{1,0:T(8,128)(2,1)S(1)} collective-permute-done((bf16[1664,128]{1,0:T(8,128)(2,1)S(1)}, bf16[1664,128]{1,0:T(8,128)(2,1)S(1)}, u32[]{:S(2)}, u32[]{:S(2)}) %collective-permute-start.22) | collective-permute-done | bytes 426016 | tf_op jit(solution)/shard_map/ppermute | solution.py:71
  74.0 6.8 %collective-permute-done.20.r_one = bf16[3840,128]{1,0:T(8,128)(2,1)S(1)} collective-permute-done((bf16[3840,128]{1,0:T(8,128)(2,1)S(1)}, bf16[3840,128]{1,0:T(8,128)(2,1)S(1)}, u32[]{:S(2)}, u32[]{:S(2)}) %collective-permute-start.20) | collective-permute-done | bytes 983072 | tf_op jit(solution)/shard_map/ppermute | solution.py:87
  87.6 4.2 %collective-permute-done.25 = bf16[1376,128]{1,0:T(8,128)(2,1)S(1)} collective-permute-done((bf16[1376,128]{1,0:T(8,128)(2,1)S(1)}, bf16[1376,128]{1,0:T(8,128)(2,1)S(1)}, u32[]{:S(2)}, u32[]{:S(2)}) %collective-permute-start.25) | collective-permute-done | bytes 352288 | tf_op jit(solution)/shard_map/ppermute | solution.py:87
  91.7 3.7 %collective-permute-done.26 = bf16[1376,128]{1,0:T(8,128)(2,1)S(1)} collective-permute-done((bf16[1376,128]{1,0:T(8,128)(2,1)S(1)}, bf16[1376,128]{1,0:T(8,128)(2,1)S(1)}, u32[]{:S(2)}, u32[]{:S(2)}) %collective-permute-start.26) | collective-permute-done | bytes 352288 | tf_op jit(solution)/shard_map/ppermute | solution.py:87
  100.3 2.7 %collective-permute-start.33 = (bf16[416,128]{1,0:T(8,128)(2,1)S(1)}, bf16[416,128]{1,0:T(8,128)(2,1)S(1)}, u32[]{:S(2)}, u32[]{:S(2)}) collective-permute-start(bf16[416,128]{1,0:T(8,128)(2,1)S(1)} %add_convert_fusion.5), channel_id=1, source_target_pairs={{0,96},{1,7},{2,98},{3,5},{4,100},{5,3},{6,102},{7,1},{8,104},{9,1... | collective-permute-start | bytes 319496 | tf_op jit(solution)/shard_map/ppermute | solution.py:79
  108.1 2.8 %collective-permute-done.31 = bf16[960,128]{1,0:T(8,128)(2,1)S(1)} collective-permute-done((bf16[960,128]{1,0:T(8,128)(2,1)S(1)}, bf16[960,128]{1,0:T(8,128)(2,1)S(1)}, u32[]{:S(2)}, u32[]{:S(2)}) %collective-permute-start.31) | collective-permute-done | bytes 245792 | tf_op jit(solution)/shard_map/ppermute | solution.py:71
  111.0 4.2 %collective-permute-done.29.back_two = bf16[256,512]{1,0:T(8,128)(2,1)S(1)} collective-permute-done((bf16[256,512]{1,0:T(8,128)(2,1)S(1)}, bf16[256,512]{1,0:T(8,128)(2,1)S(1)}, u32[]{:S(2)}, u32[]{:S(2)}) %collective-permute-start.29) | collective-permute-done | bytes 262176 | tf_op jit(solution)/shard_map/ppermute | solution.py:94
  115.2 3.6 %collective-permute-done.28.back_one = bf16[256,512]{1,0:T(8,128)(2,1)S(1)} collective-permute-done((bf16[256,512]{1,0:T(8,128)(2,1)S(1)}, bf16[256,512]{1,0:T(8,128)(2,1)S(1)}, u32[]{:S(2)}, u32[]{:S(2)}) %collective-permute-start.28) | collective-permute-done | bytes 262176 | tf_op jit(solution)/shard_map/ppermute | solution.py:94
  118.8 2.3 %collective-permute-start.34 = (bf16[1376,128]{1,0:T(8,128)(2,1)S(1)}, bf16[1376,128]{1,0:T(8,128)(2,1)S(1)}, u32[]{:S(2)}, u32[]{:S(2)}) collective-permute-start(bf16[1376,128]{1,0:T(8,128)(2,1)S(1)} %pad_maximum_fusion.own), channel_id=1, source_target_pairs={{0,4},{1,65},{2,6},{3,67},{4,0},{5,69},{6,2},{7,71},{8,12},{9,73},... | collective-permute-start | bytes 1056776 | tf_op jit(solution)/shard_map/ppermute | solution.py:87
  121.1 2.3 %collective-permute-start.35 = (bf16[1376,128]{1,0:T(8,128)(2,1)S(1)}, bf16[1376,128]{1,0:T(8,128)(2,1)S(1)}, u32[]{:S(2)}, u32[]{:S(2)}) collective-permute-start(bf16[1376,128]{1,0:T(8,128)(2,1)S(1)} %pad_maximum_fusion.own), channel_id=1, source_target_pairs={{0,2},{1,33},{2,4},{3,35},{4,6},{5,37},{6,0},{7,39},{8,10},{9,41},... | collective-permute-start | bytes 1056776 | tf_op jit(solution)/shard_map/ppermute | solution.py:87
  124.4 3.4 %collective-permute-done.34.r_two = bf16[1376,128]{1,0:T(8,128)(2,1)S(1)} collective-permute-done((bf16[1376,128]{1,0:T(8,128)(2,1)S(1)}, bf16[1376,128]{1,0:T(8,128)(2,1)S(1)}, u32[]{:S(2)}, u32[]{:S(2)}) %collective-permute-start.34) | collective-permute-done | bytes 352288 | tf_op jit(solution)/shard_map/ppermute | solution.py:87
  127.7 3.7 %collective-permute-done.35.r_one = bf16[1376,128]{1,0:T(8,128)(2,1)S(1)} collective-permute-done((bf16[1376,128]{1,0:T(8,128)(2,1)S(1)}, bf16[1376,128]{1,0:T(8,128)(2,1)S(1)}, u32[]{:S(2)}, u32[]{:S(2)}) %collective-permute-start.35) | collective-permute-done | bytes 352288 | tf_op jit(solution)/shard_map/ppermute | solution.py:87
  133.2 2.6 %collective-permute-start.37 = (bf16[1664,128]{1,0:T(8,128)(2,1)S(1)}, bf16[1664,128]{1,0:T(8,128)(2,1)S(1)}, u32[]{:S(2)}, u32[]{:S(2)}) collective-permute-start(bf16[1664,128]{1,0:T(8,128)(2,1)S(1)} %get-tuple-element.142.own), channel_id=1, source_target_pairs={{0,16},{1,17},{2,18},{3,19},{4,20},{5,21},{6,22},{7,23},{8,24},{9,... | collective-permute-start | bytes 1277960 | tf_op jit(solution)/shard_map/ppermute | solution.py:87
  135.7 4.9 %collective-permute-start.38 = (bf16[1664,128]{1,0:T(8,128)(2,1)S(1)}, bf16[1664,128]{1,0:T(8,128)(2,1)S(1)}, u32[]{:S(2)}, u32[]{:S(2)}) collective-permute-start(bf16[1664,128]{1,0:T(8,128)(2,1)S(1)} %get-tuple-element.142.own), channel_id=1, source_target_pairs={{0,8},{1,9},{2,10},{3,11},{4,12},{5,13},{6,14},{7,15},{8,16},{9,17... | collective-permute-start | bytes 1277960 | tf_op jit(solution)/shard_map/ppermute | solution.py:87
  141.6 5.9 %collective-permute-done.37.r_two = bf16[1664,128]{1,0:T(8,128)(2,1)S(1)} collective-permute-done((bf16[1664,128]{1,0:T(8,128)(2,1)S(1)}, bf16[1664,128]{1,0:T(8,128)(2,1)S(1)}, u32[]{:S(2)}, u32[]{:S(2)}) %collective-permute-start.37) | collective-permute-done | bytes 426016 | tf_op jit(solution)/shard_map/ppermute | solution.py:87
  147.5 2.7 %collective-permute-start.41 = (bf16[3840,128]{1,0:T(8,128)(2,1)S(1)}, bf16[3840,128]{1,0:T(8,128)(2,1)S(1)}, u32[]{:S(2)}, u32[]{:S(2)}) collective-permute-start(bf16[3840,128]{1,0:T(8,128)(2,1)S(1)} %get-tuple-element.148.piece), channel_id=1, source_target_pairs={{0,96},{1,7},{2,98},{3,1},{4,100},{5,3},{6,102},{7,5},{8,104},{9,1... | collective-permute-start | bytes 2949128 | tf_op jit(solution)/shard_map/ppermute | solution.py:87
  150.3 2.1 %collective-permute-done.38.r_one = bf16[1664,128]{1,0:T(8,128)(2,1)S(1)} collective-permute-done((bf16[1664,128]{1,0:T(8,128)(2,1)S(1)}, bf16[1664,128]{1,0:T(8,128)(2,1)S(1)}, u32[]{:S(2)}, u32[]{:S(2)}) %collective-permute-start.38) | collective-permute-done | bytes 426016 | tf_op jit(solution)/shard_map/ppermute | solution.py:87
  152.4 2.5 %a_spread.1 = (f32[640,512]{1,0:T(8,128)}, f32[640,128]{1,0:T(8,128)}, f32[640,128]{1,0:T(8,128)}, f32[512,640]{1,0:T(8,128)}, f32[16,128]{1,0:T(8,128)S(1)}) custom-call(s32[4]{0:T(128)S(1)} %pad_add_fusion.where, bf16[1664,128]{1,0:T(8,128)(2,1)S(1)} %get-tuple-element.142.own, bf16[1664,128]{1,0:T(8,128)(2,1)S(1)} %collective-permute-done.37.r_two, ...), custom_call_target="tpu_custom_call" | custom-call | flops 2750000128 | bytes 1024 | tf_op jit(solution)/shard_map/a_spread/pallas_call | solution.py:114
  159.3 2.5 %f_spread.5 = (f32[640,1024]{1,0:T(8,128)}, f32[640,1024]{1,0:T(8,128)}, f32[1024,640]{1,0:T(8,128)}) custom-call(s32[4]{0:T(128)S(1)} %pad_add_fusion.where, bf16[3840,128]{1,0:T(8,128)(2,1)} %collective-permute-done.43.piece, f32[640,1024]{1,0:T(8,128)} %get-tuple-element.149.refs_0_, ...), custom_call_target="tpu_custom_call", output_to_operand_aliasing={{0}: (2, {}), {1}: (3, {}), {2}: (4, {})} | custom-call | flops 1024 | bytes 1024 | tf_op jit(solution)/shard_map/f_spread/pallas_call | solution.py:444
  161.9 4.9 %collective-permute-done.42.piece = bf16[3840,128]{1,0:T(8,128)(2,1)S(1)} collective-permute-done((bf16[3840,128]{1,0:T(8,128)(2,1)S(1)}, bf16[3840,128]{1,0:T(8,128)(2,1)S(1)}, u32[]{:S(2)}, u32[]{:S(2)}) %collective-permute-start.42) | collective-permute-done | bytes 983072 | tf_op jit(solution)/shard_map/ppermute | solution.py:87
  (123 shorter events, 49.9 us)
Async XLA Ops:
  0.6 20.4 %collective-permute-start = (bf16[256,640]{1,0:T(8,128)(2,1)}, bf16[256,640]{1,0:T(8,128)(2,1)S(1)}, u32[]{:S(2)}, u32[]{:S(2)}) collective-permute-start(bf16[256,640]{1,0:T(8,128)(2,1)} %bitcast.13), channel_id=1, source_target_pairs={{0,4},{2,6},{4,8},{6,10},{8,12},{10,14},{12,16},{14,18},{16,20},{1... | collective-permute-start | bytes 983048 | tf_op jit(solution)/shard_map/ppermute | solution.py:94
  5.9 15.2 %collective-permute-start.1 = (bf16[256,640]{1,0:T(8,128)(2,1)}, bf16[256,640]{1,0:T(8,128)(2,1)S(1)}, u32[]{:S(2)}, u32[]{:S(2)}) collective-permute-start(bf16[256,640]{1,0:T(8,128)(2,1)} %bitcast.14), channel_id=1, source_target_pairs={{0,2},{2,4},{4,6},{6,8},{8,10},{10,12},{12,14},{14,16},{16,18},{18... | collective-permute-start | bytes 983048 | tf_op jit(solution)/shard_map/ppermute | solution.py:94
  12.9 8.2 %collective-permute-start.6 = (bf16[512,640]{1,0:T(8,128)(2,1)}, bf16[512,640]{1,0:T(8,128)(2,1)S(1)}, u32[]{:S(2)}, u32[]{:S(2)}) collective-permute-start(bf16[512,640]{1,0:T(8,128)(2,1)} %wo_m.1), channel_id=1, source_target_pairs={{0,1},{1,0},{2,3},{3,2},{4,5},{5,4},{6,7},{7,6},{8,9},{9,8},{10,11... | collective-permute-start | bytes 1966088 | tf_op jit(solution)/shard_map/ppermute | solution.py:31
  13.1 8.0 %collective-permute-start.10 = (bf16[256,640]{1,0:T(8,128)(2,1)}, bf16[256,640]{1,0:T(8,128)(2,1)S(1)}, u32[]{:S(2)}, u32[]{:S(2)}) collective-permute-start(bf16[256,640]{1,0:T(8,128)(2,1)} %bitcast.9), channel_id=1, source_target_pairs={{0,1},{1,0},{2,3},{3,2},{4,5},{5,4},{6,7},{7,6},{8,9},{9,8},{10,11... | collective-permute-start | bytes 983048 | tf_op jit(solution)/shard_map/ppermute | solution.py:31
  21.1 10.3 %collective-permute-start.11 = (bf16[640,1024]{1,0:T(8,128)(2,1)S(1)}, bf16[640,1024]{1,0:T(8,128)(2,1)S(1)}, u32[]{:S(2)}, u32[]{:S(2)}) collective-permute-start(bf16[640,1024]{1,0:T(8,128)(2,1)S(1)} %copy-done.8), channel_id=1, source_target_pairs={{0,1},{1,0},{2,3},{3,2},{4,5},{5,4},{6,7},{7,6},{8,9},{9,8},{10,11... | collective-permute-start | bytes 3932168 | tf_op jit(solution)/shard_map/ppermute | solution.py:31
  21.5 9.8 %collective-permute-start.12 = (bf16[640,1024]{1,0:T(8,128)(2,1)S(1)}, bf16[640,1024]{1,0:T(8,128)(2,1)S(1)}, u32[]{:S(2)}, u32[]{:S(2)}) collective-permute-start(bf16[640,1024]{1,0:T(8,128)(2,1)S(1)} %copy-done.9), channel_id=1, source_target_pairs={{0,1},{1,0},{2,3},{3,2},{4,5},{5,4},{6,7},{7,6},{8,9},{9,8},{10,11... | collective-permute-start | bytes 3932168 | tf_op jit(solution)/shard_map/ppermute | solution.py:31
  21.7 9.6 %collective-permute-start.13 = (bf16[1024,640]{1,0:T(8,128)(2,1)S(1)}, bf16[1024,640]{1,0:T(8,128)(2,1)S(1)}, u32[]{:S(2)}, u32[]{:S(2)}) collective-permute-start(bf16[1024,640]{1,0:T(8,128)(2,1)S(1)} %copy-done.10), channel_id=1, source_target_pairs={{0,1},{1,0},{2,3},{3,2},{4,5},{5,4},{6,7},{7,6},{8,9},{9,8},{10,11... | collective-permute-start | bytes 3932168 | tf_op jit(solution)/shard_map/ppermute | solution.py:31
  34.5 10.1 %collective-permute-start.14 = (bf16[256,1024]{1,0:T(8,128)(2,1)S(1)}, bf16[256,1024]{1,0:T(8,128)(2,1)S(1)}, u32[]{:S(2)}, u32[]{:S(2)}) collective-permute-start(bf16[256,1024]{1,0:T(8,128)(2,1)S(1)} %get-tuple-element.117), channel_id=1, source_target_pairs={{0,1},{1,0},{2,3},{3,2},{4,5},{5,4},{6,7},{7,6},{8,9},{9,8},{10,11... | collective-permute-start | bytes 1572872 | tf_op jit(solution)/shard_map/ppermute | solution.py:31
  35.0 9.7 %collective-permute-start.15 = (bf16[256,1024]{1,0:T(8,128)(2,1)S(1)}, bf16[256,1024]{1,0:T(8,128)(2,1)S(1)}, u32[]{:S(2)}, u32[]{:S(2)}) collective-permute-start(bf16[256,1024]{1,0:T(8,128)(2,1)S(1)} %get-tuple-element.119), channel_id=1, source_target_pairs={{0,1},{1,0},{2,3},{3,2},{4,5},{5,4},{6,7},{7,6},{8,9},{9,8},{10,11... | collective-permute-start | bytes 1572872 | tf_op jit(solution)/shard_map/ppermute | solution.py:31
  35.2 9.4 %collective-permute-start.16 = (bf16[256,1024]{1,0:T(8,128)(2,1)S(1)}, bf16[256,1024]{1,0:T(8,128)(2,1)S(1)}, u32[]{:S(2)}, u32[]{:S(2)}) collective-permute-start(bf16[256,1024]{1,0:T(8,128)(2,1)S(1)} %get-tuple-element.121), channel_id=1, source_target_pairs={{0,1},{1,0},{2,3},{3,2},{4,5},{5,4},{6,7},{7,6},{8,9},{9,8},{10,11... | collective-permute-start | bytes 1572872 | tf_op jit(solution)/shard_map/ppermute | solution.py:31
  51.6 11.8 %collective-permute-start.23 = (bf16[1664,128]{1,0:T(8,128)(2,1)S(1)}, bf16[1664,128]{1,0:T(8,128)(2,1)S(1)}, u32[]{:S(2)}, u32[]{:S(2)}) collective-permute-start(bf16[1664,128]{1,0:T(8,128)(2,1)S(1)} %get-tuple-element.134), channel_id=1, source_target_pairs={{0,8},{1,25},{2,10},{3,27},{4,12},{5,29},{6,14},{7,31},{8,0},{9,17... | collective-permute-start | bytes 1277960 | tf_op jit(solution)/shard_map/ppermute | solution.py:71
  54.2 19.8 %collective-permute-start.19 = (bf16[3840,128]{1,0:T(8,128)(2,1)S(1)}, bf16[3840,128]{1,0:T(8,128)(2,1)S(1)}, u32[]{:S(2)}, u32[]{:S(2)}) collective-permute-start(bf16[3840,128]{1,0:T(8,128)(2,1)S(1)} %get-tuple-element.129), channel_id=1, source_target_pairs={{0,64},{1,5},{2,66},{3,7},{4,68},{5,1},{6,70},{7,3},{8,72},{9,13},... | collective-permute-start | bytes 2949128 | tf_op jit(solution)/shard_map/ppermute | solution.py:87
  58.2 22.6 %collective-permute-start.20 = (bf16[3840,128]{1,0:T(8,128)(2,1)S(1)}, bf16[3840,128]{1,0:T(8,128)(2,1)S(1)}, u32[]{:S(2)}, u32[]{:S(2)}) collective-permute-start(bf16[3840,128]{1,0:T(8,128)(2,1)S(1)} %get-tuple-element.130), channel_id=1, source_target_pairs={{0,32},{1,3},{2,34},{3,5},{4,36},{5,7},{6,38},{7,1},{8,40},{9,11},... | collective-permute-start | bytes 2949128 | tf_op jit(solution)/shard_map/ppermute | solution.py:87
  58.9 22.6 %collective-permute-start.21 = (bf16[3840,128]{1,0:T(8,128)(2,1)S(1)}, bf16[3840,128]{1,0:T(8,128)(2,1)S(1)}, u32[]{:S(2)}, u32[]{:S(2)}) collective-permute-start(bf16[3840,128]{1,0:T(8,128)(2,1)S(1)} %get-tuple-element.131), channel_id=1, source_target_pairs={{0,96},{1,7},{2,98},{3,1},{4,100},{5,3},{6,102},{7,5},{8,104},{9,1... | collective-permute-start | bytes 2949128 | tf_op jit(solution)/shard_map/ppermute | solution.py:87
  61.5 12.5 %collective-permute-start.22 = (bf16[1664,128]{1,0:T(8,128)(2,1)S(1)}, bf16[1664,128]{1,0:T(8,128)(2,1)S(1)}, u32[]{:S(2)}, u32[]{:S(2)}) collective-permute-start(bf16[1664,128]{1,0:T(8,128)(2,1)S(1)} %get-tuple-element.132), channel_id=1, source_target_pairs={{0,8},{1,25},{2,10},{3,27},{4,12},{5,29},{6,14},{7,31},{8,0},{9,17... | collective-permute-start | bytes 1277960 | tf_op jit(solution)/shard_map/ppermute | solution.py:71
  63.5 10.5 %collective-permute-start.24 = (bf16[1664,128]{1,0:T(8,128)(2,1)S(1)}, bf16[1664,128]{1,0:T(8,128)(2,1)S(1)}, u32[]{:S(2)}, u32[]{:S(2)}) collective-permute-start(bf16[1664,128]{1,0:T(8,128)(2,1)S(1)} %add_convert_fusion), channel_id=1, source_target_pairs={{0,24},{1,9},{2,26},{3,11},{4,28},{5,13},{6,30},{7,15},{8,16},{9,1... | collective-permute-start | bytes 1277960 | tf_op jit(solution)/shard_map/ppermute | solution.py:71
  82.7 9.0 %collective-permute-start.25 = (bf16[1376,128]{1,0:T(8,128)(2,1)S(1)}, bf16[1376,128]{1,0:T(8,128)(2,1)S(1)}, u32[]{:S(2)}, u32[]{:S(2)}) collective-permute-start(bf16[1376,128]{1,0:T(8,128)(2,1)S(1)} %get-tuple-element.136), channel_id=1, source_target_pairs={{0,4},{1,65},{2,6},{3,67},{4,0},{5,69},{6,2},{7,71},{8,12},{9,73},... | collective-permute-start | bytes 1056776 | tf_op jit(solution)/shard_map/ppermute | solution.py:87
  84.3 11.1 %collective-permute-start.26 = (bf16[1376,128]{1,0:T(8,128)(2,1)S(1)}, bf16[1376,128]{1,0:T(8,128)(2,1)S(1)}, u32[]{:S(2)}, u32[]{:S(2)}) collective-permute-start(bf16[1376,128]{1,0:T(8,128)(2,1)S(1)} %get-tuple-element.137), channel_id=1, source_target_pairs={{0,2},{1,33},{2,4},{3,35},{4,6},{5,37},{6,0},{7,39},{8,10},{9,41},... | collective-permute-start | bytes 1056776 | tf_op jit(solution)/shard_map/ppermute | solution.py:87
  85.9 9.5 %collective-permute-start.27 = (bf16[1376,128]{1,0:T(8,128)(2,1)S(1)}, bf16[1376,128]{1,0:T(8,128)(2,1)S(1)}, u32[]{:S(2)}, u32[]{:S(2)}) collective-permute-start(bf16[1376,128]{1,0:T(8,128)(2,1)S(1)} %get-tuple-element.138), channel_id=1, source_target_pairs={{0,6},{1,97},{2,0},{3,99},{4,2},{5,101},{6,4},{7,103},{8,14},{9,10... | collective-permute-start | bytes 1056776 | tf_op jit(solution)/shard_map/ppermute | solution.py:87
  100.3 7.7 %collective-permute-start.33 = (bf16[416,128]{1,0:T(8,128)(2,1)S(1)}, bf16[416,128]{1,0:T(8,128)(2,1)S(1)}, u32[]{:S(2)}, u32[]{:S(2)}) collective-permute-start(bf16[416,128]{1,0:T(8,128)(2,1)S(1)} %add_convert_fusion.5), channel_id=1, source_target_pairs={{0,96},{1,7},{2,98},{3,5},{4,100},{5,3},{6,102},{7,1},{8,104},{9,1... | collective-permute-start | bytes 319496 | tf_op jit(solution)/shard_map/ppermute | solution.py:79
  103.4 7.5 %collective-permute-start.31 = (bf16[960,128]{1,0:T(8,128)(2,1)S(1)}, bf16[960,128]{1,0:T(8,128)(2,1)S(1)}, u32[]{:S(2)}, u32[]{:S(2)}) collective-permute-start(bf16[960,128]{1,0:T(8,128)(2,1)S(1)} %add_convert_fusion.2), channel_id=1, source_target_pairs={{0,24},{1,9},{2,26},{3,11},{4,28},{5,13},{6,30},{7,15},{8,16},{9,1... | collective-permute-start | bytes 737288 | tf_op jit(solution)/shard_map/ppermute | solution.py:71
  105.4 9.8 %collective-permute-start.29 = (bf16[256,512]{1,0:T(8,128)(2,1)S(1)}, bf16[256,512]{1,0:T(8,128)(2,1)S(1)}, u32[]{:S(2)}, u32[]{:S(2)}) collective-permute-start(bf16[256,512]{1,0:T(8,128)(2,1)S(1)} %get-tuple-element.140), channel_id=1, source_target_pairs={{4,0},{6,2},{8,4},{10,6},{12,8},{14,10},{16,12},{18,14},{20,16},{2... | collective-permute-start | bytes 786440 | tf_op jit(solution)/shard_map/ppermute | solution.py:94
  106.7 12.0 %collective-permute-start.28 = (bf16[256,512]{1,0:T(8,128)(2,1)S(1)}, bf16[256,512]{1,0:T(8,128)(2,1)S(1)}, u32[]{:S(2)}, u32[]{:S(2)}) collective-permute-start(bf16[256,512]{1,0:T(8,128)(2,1)S(1)} %get-tuple-element.139), channel_id=1, source_target_pairs={{2,0},{4,2},{6,4},{8,6},{10,8},{12,10},{14,12},{16,14},{18,16},{20... | collective-permute-start | bytes 786440 | tf_op jit(solution)/shard_map/ppermute | solution.py:94
  118.8 8.9 %collective-permute-start.34 = (bf16[1376,128]{1,0:T(8,128)(2,1)S(1)}, bf16[1376,128]{1,0:T(8,128)(2,1)S(1)}, u32[]{:S(2)}, u32[]{:S(2)}) collective-permute-start(bf16[1376,128]{1,0:T(8,128)(2,1)S(1)} %pad_maximum_fusion.own), channel_id=1, source_target_pairs={{0,4},{1,65},{2,6},{3,67},{4,0},{5,69},{6,2},{7,71},{8,12},{9,73},... | collective-permute-start | bytes 1056776 | tf_op jit(solution)/shard_map/ppermute | solution.py:87
  121.1 10.3 %collective-permute-start.35 = (bf16[1376,128]{1,0:T(8,128)(2,1)S(1)}, bf16[1376,128]{1,0:T(8,128)(2,1)S(1)}, u32[]{:S(2)}, u32[]{:S(2)}) collective-permute-start(bf16[1376,128]{1,0:T(8,128)(2,1)S(1)} %pad_maximum_fusion.own), channel_id=1, source_target_pairs={{0,2},{1,33},{2,4},{3,35},{4,6},{5,37},{6,0},{7,39},{8,10},{9,41},... | collective-permute-start | bytes 1056776 | tf_op jit(solution)/shard_map/ppermute | solution.py:87
  123.4 9.1 %collective-permute-start.36 = (bf16[1376,128]{1,0:T(8,128)(2,1)S(1)}, bf16[1376,128]{1,0:T(8,128)(2,1)S(1)}, u32[]{:S(2)}, u32[]{:S(2)}) collective-permute-start(bf16[1376,128]{1,0:T(8,128)(2,1)S(1)} %pad_maximum_fusion.own), channel_id=1, source_target_pairs={{0,6},{1,97},{2,0},{3,99},{4,2},{5,101},{6,4},{7,103},{8,14},{9,10... | collective-permute-start | bytes 1056776 | tf_op jit(solution)/shard_map/ppermute | solution.py:87
  133.2 14.3 %collective-permute-start.37 = (bf16[1664,128]{1,0:T(8,128)(2,1)S(1)}, bf16[1664,128]{1,0:T(8,128)(2,1)S(1)}, u32[]{:S(2)}, u32[]{:S(2)}) collective-permute-start(bf16[1664,128]{1,0:T(8,128)(2,1)S(1)} %get-tuple-element.142.own), channel_id=1, source_target_pairs={{0,16},{1,17},{2,18},{3,19},{4,20},{5,21},{6,22},{7,23},{8,24},{9,... | collective-permute-start | bytes 1277960 | tf_op jit(solution)/shard_map/ppermute | solution.py:87
  135.7 16.6 %collective-permute-start.38 = (bf16[1664,128]{1,0:T(8,128)(2,1)S(1)}, bf16[1664,128]{1,0:T(8,128)(2,1)S(1)}, u32[]{:S(2)}, u32[]{:S(2)}) collective-permute-start(bf16[1664,128]{1,0:T(8,128)(2,1)S(1)} %get-tuple-element.142.own), channel_id=1, source_target_pairs={{0,8},{1,9},{2,10},{3,11},{4,12},{5,13},{6,14},{7,15},{8,16},{9,17... | collective-permute-start | bytes 1277960 | tf_op jit(solution)/shard_map/ppermute | solution.py:87
  140.6 11.8 %collective-permute-start.39 = (bf16[1664,128]{1,0:T(8,128)(2,1)S(1)}, bf16[1664,128]{1,0:T(8,128)(2,1)S(1)}, u32[]{:S(2)}, u32[]{:S(2)}) collective-permute-start(bf16[1664,128]{1,0:T(8,128)(2,1)S(1)} %get-tuple-element.142.own), channel_id=1, source_target_pairs={{0,24},{1,25},{2,26},{3,27},{4,28},{5,29},{6,30},{7,31},{8,0},{9,1... | collective-permute-start | bytes 1277960 | tf_op jit(solution)/shard_map/ppermute | solution.py:87
  140.6 18.7 %collective-permute-start.43 = (bf16[3840,128]{1,0:T(8,128)(2,1)S(1)}, bf16[3840,128]{1,0:T(8,128)(2,1)}, u32[]{:S(2)}, u32[]{:S(2)}) collective-permute-start(bf16[3840,128]{1,0:T(8,128)(2,1)S(1)} %get-tuple-element.148.piece), channel_id=1, source_target_pairs={{0,64},{1,5},{2,66},{3,7},{4,68},{5,1},{6,70},{7,3},{8,72},{9,13},... | collective-permute-start | bytes 2949128 | tf_op jit(solution)/shard_map/ppermute | solution.py:87
  141.6 25.2 %collective-permute-start.42 = (bf16[3840,128]{1,0:T(8,128)(2,1)S(1)}, bf16[3840,128]{1,0:T(8,128)(2,1)S(1)}, u32[]{:S(2)}, u32[]{:S(2)}) collective-permute-start(bf16[3840,128]{1,0:T(8,128)(2,1)S(1)} %get-tuple-element.148.piece), channel_id=1, source_target_pairs={{0,32},{1,3},{2,34},{3,5},{4,36},{5,7},{6,38},{7,1},{8,40},{9,11},... | collective-permute-start | bytes 2949128 | tf_op jit(solution)/shard_map/ppermute | solution.py:87
  147.5 21.1 %collective-permute-start.41 = (bf16[3840,128]{1,0:T(8,128)(2,1)S(1)}, bf16[3840,128]{1,0:T(8,128)(2,1)S(1)}, u32[]{:S(2)}, u32[]{:S(2)}) collective-permute-start(bf16[3840,128]{1,0:T(8,128)(2,1)S(1)} %get-tuple-element.148.piece), channel_id=1, source_target_pairs={{0,96},{1,7},{2,98},{3,1},{4,100},{5,3},{6,102},{7,5},{8,104},{9,1... | collective-permute-start | bytes 2949128 | tf_op jit(solution)/shard_map/ppermute | solution.py:87
  (26 other events, 92.7 us)
where the time goes:
time: 171 us
  waiting for transfers between devices  64.2 us (38%)
  starting transfers between devices  58.2 us (34%)
  Pallas kernels  37.5 us (22%)
  local copies, waits for them, and re-layouts  5.77 us (3%)
  other arithmetic  3.84 us (2%)
    ppermute x15, waiting for transfers between devices, to_peers(): lax.ppermute(part, ('ctx', 'fsdp'), shift(by))  36.5 us
    pallas_call x11, Pallas kernels, call(): pl.pallas_call(body, out_shape=shapes, in_specs=[smem] * scalars + [whole...  29.3 us
    ppermute x15, starting transfers between devices, to_peers(): lax.ppermute(part, ('ctx', 'fsdp'), shift(by))  28.8 us
    ppermute x5, waiting for transfers between devices, swap_z(): lax.ppermute(x, ('ctx', 'fsdp'), chip_pairs(lambda x, z, y, c: (x, (pair_...  12.4 us
    ppermute x4, starting transfers between devices, passed_along(): return lax.ppermute(shard, 'ctx', pairs)  10.4 us
    ppermute x5, starting transfers between devices, swap_z(): lax.ppermute(x, ('ctx', 'fsdp'), chip_pairs(lambda x, z, y, c: (x, (pair_...  9.57 us
    pallas_call x4, Pallas kernels, ffn_spread(): pl.pallas_call(functools.partial(ffn_spread_body, by, not shards), out_sh...  8.19 us
    ppermute x4, waiting for transfers between devices, passed_along(): return lax.ppermute(shard, 'ctx', pairs)  7.77 us
  transfers between devices with their start and end apart: 44, of which 19 were waited for; matrix products, arithmetic and copies ran while one was open for 3% of the time, Pallas kernels for 16%

commit v1 on v0

--- a/solution.py
+++ b/solution.py
@@ -44,33 +44,37 @@
 
 
 def shift_first(by):
-    return chip_pairs(lambda x, z, y, c: (x + by, z, y) if c == 0 else (x, z, y + by))
+    return chip_pairs(lambda x, z, y, c: (x + by, z, y) if c == 0 else (x, z + by, y))
 
 
 def shift_second(by):
-    return chip_pairs(lambda x, z, y, c: (x, z, y + by) if c == 0 else (x + by, z, y))
-
-
-def shift_z(by):
-    return chip_pairs(lambda x, z, y, c: (x, z + by, y))
+    return chip_pairs(lambda x, z, y, c: (x, z + by, y) if c == 0 else (x + by, z, y))
+
+
+def shift_y(by):
+    return chip_pairs(lambda x, z, y, c: (x, z, y + by))
+
+
+def shift_apart(by):
+    return chip_pairs(lambda x, z, y, c: (x, z, y + by - 2 * by * c))
 
 
 def after(x, *done):
     return lax.optimization_barrier((x, *done))[0]
 
 
-def pair_first(z):
-    return z ^ 1
-
-
-def pair_second(z):
-    return 3 - z
-
-
-def swap_z(x, step):
+def pair_first(v):
+    return v ^ 1
+
+
+def pair_second(v):
+    return 3 - v
+
+
+def swap_y(v, step):
     return lax.ppermute(
-        x, ("ctx", "fsdp"),
-        chip_pairs(lambda x, z, y, c: (x, (pair_first, pair_second)[c ^ step](z), y)),
+        v, ("ctx", "fsdp"),
+        chip_pairs(lambda x, z, y, c: (x, z, (pair_first, pair_second)[c ^ step](y))),
     )
 
 
@@ -78,7 +82,7 @@
     pair = (pair_first, pair_second)[step]
     return lax.ppermute(
         v, ("ctx", "fsdp"),
-        chip_pairs(lambda x, z, y, c: (pair(x), z, y) if c == 0 else (x, z, pair(y))),
+        chip_pairs(lambda x, z, y, c: (pair(x), z, y) if c == 0 else (x, pair(z), y)),
     )
 
 
@@ -258,12 +262,12 @@
     return lax.rem(i + by, 4)
 
 
-def z_places(core, z):
-    one = z + 1 - 2 * lax.rem(z, 2)
-    other = 3 - z
+def y_places(core, y):
+    one = y + 1 - 2 * lax.rem(y, 2)
+    other = 3 - y
     first = jnp.where(core == 0, one, other)
     second = jnp.where(core == 0, other, one)
-    return z, second, first, 2 - z + 2 * lax.rem(z, 2)
+    return y, second, first, 2 - y + 2 * lax.rem(y, 2)
 
 
 def ffn_grads_body(
@@ -286,7 +290,7 @@
 
 def attend_grad_body(
     where, query, kv, lse, ga_low, wo_m, wo_o, cos, sin, pos_row,
-    dq_m, dq_o, dkv, dkv_m, packed,
+    dq_m, dq_o, dkv, back_two, back_one, dkv_m, packed,
 ):
     dkv_o = packed.at[512:, :]
     ok = allowed_pairs(pos_row)
@@ -317,9 +321,11 @@
     a, b = rotate_pair(grad_k[:, :HALF], grad_k[:, HALF:], cos[...], -sin[...])
     packed[:256, :] = dq_o[:, :HEAD]
     packed[256:512, :] = dq_o[:, HEAD:]
-    dkv[:, :HALF] = a.astype(BF16)
-    dkv[:, HALF:HEAD] = b.astype(BF16)
-    dkv[:, HEAD:] = grad_v.astype(BF16)
+    for rows, out in ((0, back_two), (256, back_one), (512, dkv)):
+        rows = slice(rows, rows + 256)
+        out[:, :HALF] = a[rows, :].astype(BF16)
+        out[:, HALF:HEAD] = b[rows, :].astype(BF16)
+        out[:, HEAD:] = grad_v[rows, :].astype(BF16)
     even = where[0] == 0
     dkv_m[:, :HALF] = jnp.where(even, a, b).astype(BF16)
     dkv_o[:, :HALF] = jnp.where(even, b, a).astype(BF16)
@@ -337,7 +343,7 @@
     gk = dot(turned[:, :768], dkv_m[...]) + dot(turned[:, 768:], packed[512:, :])
     weighed = gk[:, :HALF] * wk[...].astype(F32) + gk[:, HALF:] * wv[...].astype(F32)
     gk = gk.astype(BF16)
-    for out, j in zip((out_0, out_1, out_2, out_3), z_places(where[0], where[3])):
+    for out, j in zip((out_0, out_1, out_2, out_3), y_places(where[0], where[3])):
         cols = pl.ds(pl.multiple_of(j * 128, 128), 128)
         rows = pl.ds(pl.multiple_of(j // 2 * 256, 256), 256)
         half = pl.ds(pl.multiple_of(j % 2 * 128, 128), 128)
@@ -368,7 +374,7 @@
     tok, gain, grad_after, dq_m, dq_o, dkv, back_one, back_two, wq_m, wq_o, wkv, out
 ):
     back = back_one[...].astype(F32) + back_two[...].astype(F32)
-    own = (dkv[512:, :].astype(F32) + back).astype(BF16)
+    own = (dkv[...].astype(F32) + back).astype(BF16)
     gn = dot_nt(dq_m[...], wq_m[...]) + dot_nt(dq_o[...], wq_o[...]) + dot_nt(own, wkv[...])
     x = tok[...].astype(F32)
     r = inv_rms(x)
@@ -409,69 +415,85 @@
     return total.astype(BF16)
 
 
-def join_body(where, own, r_two, r_one, r_minus, f_out, a_out):
+def join_body(where, own, r_two, r_one, r_minus, _, f_out, a_out, small):
     for ref, by in ((own, 0), (r_two, 2), (r_one, 3), (r_minus, 1)):
         j = place(where[2], by)
         f_out[pl.ds(pl.multiple_of(j * F_PART, F_PART), F_PART), :] = ref[:F_PART, :]
         a_out[pl.ds(pl.multiple_of(j * A_PART, A_PART), A_PART), :] = ref[F_PART:, :]
-
-
-def ffn_spread_body(by, fresh, where, piece, *refs):
-    gate, up, down, gate_wide, up_wide, down_wide, sems = refs if fresh else refs[3:]
-    j = place(where[1], by)
+    small[...] = a_out[1600:1616, :]
+
+
+SHARDS = ((D, FF // 2), (D, FF // 2), (FF // 2, D), (D, MINE), (D, HALF), (D, HALF), (MINE, D))
+F_WIDE = ((D, 256), (D, 256), (256, D))
+A_WIDE = ((D, 128), (160, 128), (160, 128), (128, D))
+
+
+def spread_body(f_places, a_places, fresh, where, *refs):
+    f_count, a_count = len(f_places), len(a_places)
+    f_pieces, a_pieces = refs[:f_count], refs[f_count : f_count + a_count]
+    refs = refs[f_count + a_count + (0 if fresh else len(SHARDS)) :]
+    gate, up, down, query, key, value, out = refs[:7]
+    sems = refs[-1]
+    f_wide, a_wide = refs[7:10], refs[10:14]
     copies = []
-    cols = pl.ds(pl.multiple_of(j * 256, 256), 256)
-    for i, (at, wide, target) in enumerate(((0, gate_wide, gate), (1280, up_wide, up))):
-        for b in range(2):
-            wide[:, b * 128 : (b + 1) * 128] = piece[
-                at + b * 640 : at + (b + 1) * 640, :
-            ].astype(F32)
-        copies.append(pltpu.make_async_copy(wide, target.at[:, cols], sems.at[i]))
+
+    def send(source, target):
+        copies.append(pltpu.make_async_copy(source, target, sems.at[len(copies)]))
         copies[-1].start()
-    for b in range(5):
-        down_wide[:, b * 128 : (b + 1) * 128] = piece[2560 + b * 256 : 2816 + b * 256, :].astype(F32)
-    copies.append(pltpu.make_async_copy(down_wide, down.at[cols, :], sems.at[2]))
-    copies[-1].start()
+
+    for i, (piece, by) in enumerate(zip(f_pieces, f_places)):
+        j = place(where[1], by)
+        cols = pl.ds(pl.multiple_of(j * 256, 256), 256)
+        for at, wide, target in ((0, f_wide[0], gate), (1280, f_wide[1], up)):
+            for b in range(2):
+                wide[i, :, b * 128 : (b + 1) * 128] = piece[
+                    at + b * 640 : at + (b + 1) * 640, :
+                ].astype(F32)
+            send(wide.at[i], target.at[:, cols])
+        for b in range(5):
+            at = 2560 + b * 256
+            f_wide[2][i, :, b * 128 : (b + 1) * 128] = piece[at : at + 256, :].astype(F32)
+        send(f_wide[2].at[i], down.at[cols, :])
+    for i, (piece, (by, apart)) in enumerate(zip(a_pieces, a_places)):
+        j = place(where[3], by + apart * where[0])
+        block = pl.ds(pl.multiple_of(j * 128, 128), 128)
+        rows = pl.ds(pl.multiple_of(j * 160, 32), 160)
+        a_wide[0][i] = piece[:640, :].astype(F32)
+        send(a_wide[0].at[i], query.at[:, block])
+        a_wide[1][i] = piece[640:800, :].astype(F32)
+        send(a_wide[1].at[i], key.at[rows, :])
+        a_wide[2][i] = piece[800:960, :].astype(F32)
+        send(a_wide[2].at[i], value.at[rows, :])
+        for b in range(5):
+            at = 960 + b * 128
+            a_wide[3][i, :, b * 128 : (b + 1) * 128] = piece[at : at + 128, :].astype(F32)
+        send(a_wide[3].at[i], out.at[block, :])
     for copy in copies:
         copy.wait()
 
 
-def ffn_spread(where, pieces):
-    outs = [jax.ShapeDtypeStruct(s, F32) for s in ((D, FF // 2), (D, FF // 2), (FF // 2, D))]
+def spread(where, f_pieces, f_places, a_pieces, a_places, shards):
+    f_count, a_count = len(f_pieces), len(a_pieces)
     anywhere = pl.BlockSpec(memory_space=pl.ANY)
-    shards = []
-    for piece, by in zip(pieces, (0, 2, 3, 1)):
-        shards = pl.pallas_call(
-            functools.partial(ffn_spread_body, by, not shards),
-            out_shape=outs,
-            in_specs=[
-                pl.BlockSpec(memory_space=pltpu.SMEM), pl.BlockSpec(memory_space=pltpu.VMEM),
-                *[anywhere] * len(shards),
-            ],
-            out_specs=[anywhere] * 3,
-            input_output_aliases={2 + i: i for i in range(len(shards))},
-            scratch_shapes=[
-                pltpu.VMEM((D, 256), F32), pltpu.VMEM((D, 256), F32), pltpu.VMEM((256, D), F32),
-                pltpu.SemaphoreType.DMA((3,)),
-            ],
-            compiler_params=pltpu.CompilerParams(vmem_limit_bytes=8 * MIB),
-            cost_estimate=pl.CostEstimate(flops=1024, bytes_accessed=1024, transcendentals=0),
-            name="f_spread",
-        )(where, piece, *shards)
-    return shards
-
-
-def attend_spread_body(where, own, r_two, r_one, r_minus, query, key, value, out, gains):
-    for ref, by in ((own, 0), (r_two, 2), (r_one, 3), (r_minus, 1)):
-        j = place(where[3], by)
-        query[:, pl.ds(pl.multiple_of(j * 128, 128), 128)] = ref[:640, :].astype(F32)
-        rows = pl.ds(pl.multiple_of(j * 160, 160), 160)
-        key[rows, :] = ref[640:800, :].astype(F32)
-        value[rows, :] = ref[800:960, :].astype(F32)
-        rows = pl.ds(pl.multiple_of(j * 128, 128), 128)
-        for b in range(5):
-            out[rows, b * 128 : (b + 1) * 128] = ref[960 + b * 128 : 1088 + b * 128, :].astype(F32)
-    gains[...] = own[1600:1616, :].astype(F32)
+    return pl.pallas_call(
+        functools.partial(spread_body, f_places, a_places, not shards),
+        out_shape=[jax.ShapeDtypeStruct(s, F32) for s in SHARDS],
+        in_specs=[
+            pl.BlockSpec(memory_space=pltpu.SMEM),
+            *[pl.BlockSpec(memory_space=pltpu.VMEM)] * (f_count + a_count),
+            *[anywhere] * len(shards),
+        ],
+        out_specs=[anywhere] * len(SHARDS),
+        input_output_aliases={1 + f_count + a_count + i: i for i in range(len(shards))},
+        scratch_shapes=[
+            *[pltpu.VMEM((f_count, *s), F32) for s in F_WIDE],
+            *[pltpu.VMEM((max(a_count, 1), *s), F32) for s in A_WIDE],
+            pltpu.SemaphoreType.DMA((3 * f_count + 4 * a_count,)),
+        ],
+        compiler_params=pltpu.CompilerParams(vmem_limit_bytes=20 * MIB),
+        cost_estimate=pl.CostEstimate(flops=1024, bytes_accessed=1024, transcendentals=0),
+        name="spread",
+    )(where, *f_pieces, *a_pieces, *shards)
 
 
 def local(
@@ -483,9 +505,9 @@
     rows = tok.shape[0]
     ctx = lax.axis_index("ctx")
     core = lax.axis_index("fsdp")
-    x_at, y_at = ctx // 16, ctx % 4
+    x_at, z_at, y_at = ctx // 16, ctx // 4 % 4, ctx % 4
     where = jnp.stack(
-        [core, jnp.where(core == 0, x_at, y_at), jnp.where(core == 0, y_at, x_at), ctx // 4 % 4]
+        [core, jnp.where(core == 0, x_at, z_at), jnp.where(core == 0, z_at, x_at), y_at]
     ).astype(jnp.int32)
     even = core == 0
 
@@ -543,15 +565,15 @@
         us=5,
     )
     normed_two_r = swap(normed_two)
-    ctx_r, normed_r = swap(ctx_o), swap(normed_all)
     half_ffn = [((rows, FF // 2), BF16)] * 3
     hid_o, dg_o, du_o, total_o, grad_n_o = call(
         "ffn_other", ffn_other_body, [*half_ffn, ((rows, D), F32), ((rows, D), F32)],
         [normed_two, gy, gate_other, up_other, down_other],
         us=5,
     )
-    gain_two = after(gain_two, normed_two_r, ctx_r, normed_r)
+    gain_two = after(gain_two, normed_two_r)
     hid_r, dg_r, du_r = swap(hid_o), swap(dg_o), swap(du_o)
+    ctx_r, normed_r = swap(after(ctx_o, hid_o)), swap(after(normed_all, hid_o))
     out, hid_m, dg_m, du_m, grad_after, ga_low, grad_gain_two = call(
         "ffn", ffn_body,
         [((rows, D), BF16), *half_ffn, ((rows, D), F32), ((rows, D), BF16), ((1, D), F32)],
@@ -559,10 +581,10 @@
         us=4,
     )
     ga_r = swap(ga_low)
-    dq_m, dq_o, dkv, dkv_m, packed = call(
+    dq_m, dq_o, dkv, back_two, back_one, dkv_m, packed = call(
         "attend_grad", attend_grad_body,
         [
-            ((rows, MINE), BF16), ((rows, MINE), BF16), ((3 * rows, 2 * HEAD), BF16),
+            ((rows, MINE), BF16), ((rows, MINE), BF16), *[((rows, 2 * HEAD), BF16)] * 3,
             ((3 * rows, HEAD), BF16), ((5 * rows, HEAD), BF16),
         ],
         [
@@ -588,8 +610,8 @@
         us=0, scalars=1, scratch=[pltpu.VMEM((D, 6 * rows), BF16)],
     )
     a_own, a_next, a_far_own, a_far_next = a_chunks
-    a_next_r, a_own_r = swap_z(a_far_next, 0), swap_z(a_far_own, 0)
-    a_last_r = swap_z(add_low(a_next, a_next_r), 1)
+    a_next_r, a_own_r = swap_y(a_far_next, 0), swap_y(a_far_own, 0)
+    a_last_r = swap_y(add_low(a_next, a_next_r), 1)
     parts = call(
         "split", split_sum_body, [((PART, 128), BF16)] * 4,
         [where, after(f_chunks[0], a_own), *f_got, a_own, a_own_r, a_last_r], us=0, scalars=1,
@@ -597,19 +619,25 @@
     got = [parts[0], *to_peers(parts[1:], shift_second)]
     f_two = sum_four(*[part[:F_PART] for part in got])
     a_two = sum_four(*[part[F_PART:] for part in got])
-    f_pair = add_low(f_two, swap_z(f_two, 0))
+    f_pair = add_low(f_two, swap_y(f_two, 0))
     a_pair = add_low(a_two, swap_first(a_two, 0))
-    f_three = add_low(f_pair, swap_z(f_pair, 1))
-    a_three = add_low(a_pair, swap_first(a_pair, 1))
-    back_two = passed_along(after(dkv[:rows], f_two), -2)
-    back_one = passed_along(after(dkv[rows : 2 * rows], f_two), -1)
-    own = after(jnp.concatenate([f_three, a_three]), back_one, back_two)
-    f_whole, a_whole = call(
-        "join", join_body, [((F_ROWS, 128), BF16), ((A_ROWS, 128), BF16)],
-        [where, own, *to_peers([own] * 3, shift_second)], us=0, scalars=1,
-    )
-    f_sums = [f_whole, *to_peers([f_whole] * 3, shift_first)]
-    a_sums = [a_whole, *to_peers([a_whole] * 3, shift_z)]
+    f_three = add_low(f_pair, swap_y(f_pair, 1))
+    back_two = passed_along(after(back_two, f_two), -2)
+    back_one = passed_along(after(back_one, f_two), -1)
+    turn = swap(after(swap(after(grad_gain_two, back_one, back_two)), f_pair))
+    a_three = add_low(a_pair, swap_first(after(a_pair, f_pair), 1))
+    own, turn = lax.optimization_barrier((jnp.concatenate([f_three, a_three]), turn))
+    f_whole, a_whole, small = call(
+        "join", join_body,
+        [((F_ROWS, 128), BF16), ((A_ROWS, 128), BF16), ((16, 128), BF16)],
+        [where, own, *to_peers([own] * 3, shift_second), turn], us=0, scalars=1,
+    )
+    small_r = swap(small)
+    everywhere = ("ctx", "fsdp")
+    f_send, a_send = after(f_whole, small_r), after(a_whole, small_r)
+    f_got = to_peers([f_send] * 3, shift_first)
+    a_two = lax.ppermute(a_send, everywhere, shift_y(2))
+    a_one = lax.ppermute(a_send, everywhere, shift_apart(1))
     grad_tokens = call(
         "token_grad", token_grad_body, [((rows, D), F32)],
         [
@@ -619,14 +647,13 @@
         us=2,
     )[0]
 
-    g_query, g_key, g_value, g_out, g_gains = call(
-        "a_spread", attend_spread_body,
-        [((D, MINE), F32), ((D, HALF), F32), ((D, HALF), F32), ((MINE, D), F32), ((16, 128), F32)],
-        [where, *a_sums], scalars=1,
-        us=2.5,
-    )
-    g_gate, g_up, g_down = ffn_spread(where, f_sums)
-    g_gains = (g_gains + swap(g_gains))[:10].reshape(2, D)
+    shards = spread(where, [after(f_whole, grad_tokens)], (0,), [a_whole], ((0, 0),), [])
+    a_other = lax.ppermute(after(a_send, f_got[0]), everywhere, shift_apart(-1))
+    shards = spread(where, f_got[:1], (2,), [], (), shards)
+    g_gate, g_up, g_down, g_query, g_key, g_value, g_out = spread(
+        where, f_got[1:], (3, 1), [a_two, a_one, a_other], ((2, 0), (3, -2), (1, 2)), shards
+    )
+    g_gains = (after(small, g_key).astype(F32) + small_r.astype(F32))[:10].reshape(2, D)
     g_gains = jnp.where(even, g_gains[:, :half_d], g_gains[:, half_d:])
     return (
         out[None], grad_tokens[None], g_gains[0], g_query, g_key, g_value, g_out, g_gains[1],

time: 171 us -> 162 us (0.947)
  waiting for transfers between devices: 64.2 us -> 57.8 us
  Pallas kernels: 37.5 us -> 33.7 us
    ppermute x15 -> x12, waiting for transfers between devices: 36.5 us -> 27.9 us  [to_peers(): lax.ppermute(part, ('ctx', 'fsdp'), shift(by))]
    ppermute x5 -> x8, waiting for transfers between devices: 12.4 us -> 17.9 us  [the longest x5 15.2 us: swap_y(): lax.ppermute(v, ('ctx', 'fsdp'), chip_pairs(lambda x, z, y, c: (x, z, (pa...]
    pallas_call x11 -> x10, Pallas kernels: 29.3 us -> 26.2 us  [call(): pl.pallas_call(body, out_shape=shapes, in_specs=[smem] * scalars + [whole...]
    ppermute x4, waiting for transfers between devices: 7.77 us -> 5.46 us  [passed_along(): return lax.ppermute(shard, 'ctx', pairs)]
    ppermute x5 -> x8, starting transfers between devices: 9.57 us -> 11.6 us  [the longest x5 6.24 us: swap_y(): lax.ppermute(v, ('ctx', 'fsdp'), chip_pairs(lambda x, z, y, c: (x, z, (pa...]
    ppermute x15 -> x12, starting transfers between devices: 28.8 us -> 26.8 us  [to_peers(): lax.ppermute(part, ('ctx', 'fsdp'), shift(by))]
    pallas_call x4 -> x3, Pallas kernels: 8.19 us -> 7.48 us  [spread(): pl.pallas_call(functools.partial(spread_body, f_places, a_places, not sha...]
    ppermute x18 -> x20, waiting for transfers between devices: 6.21 us -> 6.61 us  [swap(): return lax.ppermute(x, 'fsdp', [(0, 1), (1, 0)])]
  transfers between devices with their start and end apart: 44 -> 46, of which waited for: 19 -> 18; matrix products, arithmetic and copies ran while one was open for 3% -> 2% of each run, Pallas kernels for 16% -> 13%
where the time goes in v1:
time: 162 us; the launch traced here: 160 us
  starting transfers between devices  58.4 us (36%)
  waiting for transfers between devices  57.8 us (36%)
  Pallas kernels  33.7 us (21%)
  local copies, waits for them, and re-layouts  5.73 us (4%)
  other arithmetic  3.84 us (2%)
    ppermute x12, waiting for transfers between devices, to_peers(): lax.ppermute(part, ('ctx', 'fsdp'), shift(by))  27.9 us
    ppermute x12, starting transfers between devices, to_peers(): lax.ppermute(part, ('ctx', 'fsdp'), shift(by))  26.8 us
    pallas_call x10, Pallas kernels, call(): pl.pallas_call(body, out_shape=shapes, in_specs=[smem] * scalars + [whole...  26.2 us
    ppermute x5, waiting for transfers between devices, swap_y(): lax.ppermute(v, ('ctx', 'fsdp'), chip_pairs(lambda x, z, y, c: (x, z, (pa...  15.2 us
    ppermute x4, starting transfers between devices, passed_along(): return lax.ppermute(shard, 'ctx', pairs)  10.4 us
    pallas_call x3, Pallas kernels, spread(): pl.pallas_call(functools.partial(spread_body, f_places, a_places, not sha...  7.48 us
    ppermute x20, waiting for transfers between devices, swap(): return lax.ppermute(x, 'fsdp', [(0, 1), (1, 0)])  6.61 us
    ppermute x5, starting transfers between devices, swap_y(): lax.ppermute(v, ('ctx', 'fsdp'), chip_pairs(lambda x, z, y, c: (x, z, (pa...  6.24 us
  transfers between devices with their start and end apart: 46, of which 18 were waited for; matrix products, arithmetic and copies ran while one was open for 2% of the time, Pallas kernels for 13%

profile of v1, /device:TPU:0, one launch (start us, length us, event | category | flops | bytes accessed | tf_op | source)
XLA Modules:
  0.0 160.5 jit_solution(4927969257624825218)
XLA Ops:
  0.6 5.2 %collective-permute-start = (bf16[256,640]{1,0:T(8,128)(2,1)}, bf16[256,640]{1,0:T(8,128)(2,1)S(1)}, u32[]{:S(2)}, u32[]{:S(2)}) collective-permute-start(bf16[256,640]{1,0:T(8,128)(2,1)} %bitcast.13), channel_id=1, source_target_pairs={{0,4},{2,6},{4,8},{6,10},{8,12},{10,14},{12,16},{14,18},{16,20},{1... | collective-permute-start | bytes 983048 | tf_op jit(solution)/shard_map/ppermute | solution.py:98
  5.9 2.6 %collective-permute-start.1 = (bf16[256,640]{1,0:T(8,128)(2,1)}, bf16[256,640]{1,0:T(8,128)(2,1)S(1)}, u32[]{:S(2)}, u32[]{:S(2)}) collective-permute-start(bf16[256,640]{1,0:T(8,128)(2,1)} %bitcast.14), channel_id=1, source_target_pairs={{0,2},{2,4},{4,6},{6,8},{8,10},{10,12},{12,14},{14,16},{16,18},{18... | collective-permute-start | bytes 983048 | tf_op jit(solution)/shard_map/ppermute | solution.py:98
  22.1 3.2 %attend.1 = (bf16[768,640]{1,0:T(8,128)(2,1)S(1)}, bf16[256,1024]{1,0:T(8,128)(2,1)S(1)}, bf16[768,512]{1,0:T(8,128)(2,1)S(1)}, bf16[256,512]{1,0:T(8,128)(2,1)S...) custom-call(bf16[256,640]{1,0:T(8,128)(2,1)S(1)} %collective-permute, ...), custom_call_target="tpu_custom_call" | custom-call | flops 5500000256 | bytes 1024 | tf_op jit(solution)/shard_map/attend/pallas_call | solution.py:118
  25.5 2.9 %collective-permute-done.7.n_r = bf16[256,640]{1,0:T(8,128)(2,1)S(1)} collective-permute-done((bf16[256,640]{1,0:T(8,128)(2,1)S(1)}, bf16[256,640]{1,0:T(8,128)(2,1)S(1)}, u32[]{:S(2)}, u32[]{:S(2)}) %collective-permute-start.7) | collective-permute-done | bytes 327712 | tf_op jit(solution)/shard_map/ppermute | solution.py:31
  28.4 3.0 %ffn_other.1 = (bf16[256,1024]{1,0:T(8,128)(2,1)S(1)}, bf16[256,1024]{1,0:T(8,128)(2,1)S(1)}, bf16[256,1024]{1,0:T(8,128)(2,1)S(1)}, f32[256,640]{1,0:T(8,128)S(1)}, f32[256,640]{1,0:T(8,128)S(1)}) custom-call(bf16[256,640]{1,0:T(8,128)(2,1)S(1)} %get-tuple-element.113.normed_two.n, bf16[256,640]{1,0:T(8,128)(2,1)S(1)} %bitcast.10, ...), custom_call_target="tpu_custom_call" | custom-call | flops 5500000256 | bytes 1024 | tf_op jit(solution)/shard_map/ffn_other/pallas_call | solution.py:118
  32.5 3.9 %ffn.1 = (bf16[256,640]{1,0:T(8,128)(2,1)}, bf16[256,1024]{1,0:T(8,128)(2,1)S(1)}, bf16[256,1024]{1,0:T(8,128)(2,1)S(1)}, bf16[256,1024]{1,0:T(8,128)(2,1)S(1)},...) custom-call(f32[256,640]{1,0:T(8,128)S(1)} %get-tuple-element.112.after, ...), custom_call_target="tpu_custom_call" | custom-call | flops 4400000000 | bytes 1024 | tf_op jit(solution)/shard_map/ffn/pallas_call | solution.py:118
  36.4 4.4 %attend_grad.1 = (bf16[256,512]{1,0:T(8,128)(2,1)S(1)}, bf16[256,512]{1,0:T(8,128)(2,1)S(1)}, bf16[256,512]{1,0:T(8,128)(2,1)S(1)}, bf16[256,512]{1,0:T(8,128)(2...) custom-call(s32[4]{0:T(128)S(1)} %pad_add_fusion.where, ...), custom_call_target="tpu_custom_call" | custom-call | bytes 1024 | tf_op jit(solution)/shard_map/attend_grad/pallas_call | solution.py:118
  41.8 2.9 %ffn_grads.1 = (bf16[3840,128]{1,0:T(8,128)(2,1)S(1)}, bf16[3840,128]{1,0:T(8,128)(2,1)S(1)}, bf16[3840,128]{1,0:T(8,128)(2,1)S(1)}, bf16[3840,128]{1,0:T(8,128)(2,1)S(1)}) custom-call(s32[4]{0:T(128)S(1)} %pad_add_fusion.where, bf16[256,1024]{1,0:T(8,128)(2,1)S(1)} %get-tuple-element.133.hid_m, bf16[256,1024]{1,0:T(8,128)(2,1)S(1)} %collective-permute-done.12.hid_r, ...), custom_call_target="tpu_custom_call" | custom-call | flops 3300000000 | bytes 1024 | tf_op jit(solution)/shard_map/ffn_grads/pallas_call | solution.py:118
  44.8 3.8 %attend_grads.1 = (bf16[1664,128]{1,0:T(8,128)(2,1)S(1)}, bf16[1664,128]{1,0:T(8,128)(2,1)S(1)}, bf16[1664,128]{1,0:T(8,128)(2,1)S(1)}, bf16[1664,128]{1,0:T(8,128)(2,1)S(1)}) custom-call(s32[4]{0:T(128)S(1)} %pad_add_fusion.where, bf16[768,640]{1,0:T(8,128)(2,1)S(1)} %get-tuple-element.141.n, bf16[768,640]{1,0:T(8,128)(2,1)S(1)} %collective-permute-done.15.n_r, ...), custom_call_target="tpu_custom_call" | custom-call | bytes 1024 | tf_op jit(solution)/shard_map/attend_grads/pallas_call | solution.py:118
  50.2 5.1 %collective-permute-start.19 = (bf16[3840,128]{1,0:T(8,128)(2,1)S(1)}, bf16[3840,128]{1,0:T(8,128)(2,1)S(1)}, u32[]{:S(2)}, u32[]{:S(2)}) collective-permute-start(bf16[3840,128]{1,0:T(8,128)(2,1)S(1)} %get-tuple-element.150), channel_id=1, source_target_pairs={{0,64},{1,17},{2,66},{3,19},{4,68},{5,21},{6,70},{7,23},{8,72},{9,... | collective-permute-start | bytes 2949128 | tf_op jit(solution)/shard_map/ppermute | solution.py:91
  55.9 2.6 %collective-permute-start.21 = (bf16[3840,128]{1,0:T(8,128)(2,1)S(1)}, bf16[3840,128]{1,0:T(8,128)(2,1)S(1)}, u32[]{:S(2)}, u32[]{:S(2)}) collective-permute-start(bf16[3840,128]{1,0:T(8,128)(2,1)S(1)} %get-tuple-element.152), channel_id=1, source_target_pairs={{0,96},{1,25},{2,98},{3,27},{4,100},{5,29},{6,102},{7,31},{8,104},... | collective-permute-start | bytes 2949128 | tf_op jit(solution)/shard_map/ppermute | solution.py:91
  61.3 9.4 %collective-permute-done.22.a_one = bf16[1664,128]{1,0:T(8,128)(2,1)S(1)} collective-permute-done((bf16[1664,128]{1,0:T(8,128)(2,1)S(1)}, bf16[1664,128]{1,0:T(8,128)(2,1)S(1)}, u32[]{:S(2)}, u32[]{:S(2)}) %collective-permute-start.22) | collective-permute-done | bytes 426016 | tf_op jit(solution)/shard_map/ppermute | solution.py:75
  70.7 7.2 %collective-permute-done.20.r_one = bf16[3840,128]{1,0:T(8,128)(2,1)S(1)} collective-permute-done((bf16[3840,128]{1,0:T(8,128)(2,1)S(1)}, bf16[3840,128]{1,0:T(8,128)(2,1)S(1)}, u32[]{:S(2)}, u32[]{:S(2)}) %collective-permute-start.20) | collective-permute-done | bytes 983072 | tf_op jit(solution)/shard_map/ppermute | solution.py:91
  82.6 2.2 %collective-permute-start.27 = (bf16[1376,128]{1,0:T(8,128)(2,1)S(1)}, bf16[1376,128]{1,0:T(8,128)(2,1)S(1)}, u32[]{:S(2)}, u32[]{:S(2)}) collective-permute-start(bf16[1376,128]{1,0:T(8,128)(2,1)S(1)} %get-tuple-element.159), channel_id=1, source_target_pairs={{0,24},{1,97},{2,26},{3,99},{4,28},{5,101},{6,30},{7,103},{8,0},{9... | collective-permute-start | bytes 1056776 | tf_op jit(solution)/shard_map/ppermute | solution.py:91
  84.8 4.0 %collective-permute-done.25 = bf16[1376,128]{1,0:T(8,128)(2,1)S(1)} collective-permute-done((bf16[1376,128]{1,0:T(8,128)(2,1)S(1)}, bf16[1376,128]{1,0:T(8,128)(2,1)S(1)}, u32[]{:S(2)}, u32[]{:S(2)}) %collective-permute-start.25) | collective-permute-done | bytes 352288 | tf_op jit(solution)/shard_map/ppermute | solution.py:91
  88.8 3.7 %collective-permute-done.26 = bf16[1376,128]{1,0:T(8,128)(2,1)S(1)} collective-permute-done((bf16[1376,128]{1,0:T(8,128)(2,1)S(1)}, bf16[1376,128]{1,0:T(8,128)(2,1)S(1)}, u32[]{:S(2)}, u32[]{:S(2)}) %collective-permute-start.26) | collective-permute-done | bytes 352288 | tf_op jit(solution)/shard_map/ppermute | solution.py:91
  94.1 2.0 %collective-permute-start.30 = (bf16[960,128]{1,0:T(8,128)(2,1)S(1)}, bf16[960,128]{1,0:T(8,128)(2,1)S(1)}, u32[]{:S(2)}, u32[]{:S(2)}) collective-permute-start(bf16[960,128]{1,0:T(8,128)(2,1)S(1)} %add_convert_fusion.3), channel_id=1, source_target_pairs={{0,2},{1,7},{2,0},{3,5},{4,6},{5,3},{6,4},{7,1},{8,10},{9,15},{10,... | collective-permute-start | bytes 737288 | tf_op jit(solution)/shard_map/ppermute | solution.py:75
  98.8 5.2 %collective-permute-done.30 = bf16[960,128]{1,0:T(8,128)(2,1)S(1)} collective-permute-done((bf16[960,128]{1,0:T(8,128)(2,1)S(1)}, bf16[960,128]{1,0:T(8,128)(2,1)S(1)}, u32[]{:S(2)}, u32[]{:S(2)}) %collective-permute-start.30) | collective-permute-done | bytes 245792 | tf_op jit(solution)/shard_map/ppermute | solution.py:75
  104.1 2.9 %collective-permute-start.33 = (bf16[416,128]{1,0:T(8,128)(2,1)S(1)}, bf16[416,128]{1,0:T(8,128)(2,1)S(1)}, u32[]{:S(2)}, u32[]{:S(2)}) collective-permute-start(bf16[416,128]{1,0:T(8,128)(2,1)S(1)} %add_convert_fusion.5), channel_id=1, source_target_pairs={{0,96},{1,25},{2,98},{3,27},{4,100},{5,29},{6,102},{7,31},{8,104},... | collective-permute-start | bytes 319496 | tf_op jit(solution)/shard_map/ppermute | solution.py:83
  108.8 3.7 %collective-permute-done.28.back_one = bf16[256,512]{1,0:T(8,128)(2,1)S(1)} collective-permute-done((bf16[256,512]{1,0:T(8,128)(2,1)S(1)}, bf16[256,512]{1,0:T(8,128)(2,1)S(1)}, u32[]{:S(2)}, u32[]{:S(2)}) %collective-permute-start.28) | collective-permute-done | bytes 262176 | tf_op jit(solution)/shard_map/ppermute | solution.py:98
  114.8 3.7 %collective-permute-start.36 = (bf16[1376,128]{1,0:T(8,128)(2,1)S(1)}, bf16[1376,128]{1,0:T(8,128)(2,1)S(1)}, u32[]{:S(2)}, u32[]{:S(2)}) collective-permute-start(bf16[1376,128]{1,0:T(8,128)(2,1)S(1)} %pad_maximum_fusion.own), channel_id=1, source_target_pairs={{0,16},{1,65},{2,18},{3,67},{4,20},{5,69},{6,22},{7,71},{8,24},{9,... | collective-permute-start | bytes 1056776 | tf_op jit(solution)/shard_map/ppermute | solution.py:91
  118.4 3.2 %collective-permute-start.38 = (bf16[1376,128]{1,0:T(8,128)(2,1)S(1)}, bf16[1376,128]{1,0:T(8,128)(2,1)S(1)}, u32[]{:S(2)}, u32[]{:S(2)}) collective-permute-start(bf16[1376,128]{1,0:T(8,128)(2,1)S(1)} %pad_maximum_fusion.own), channel_id=1, source_target_pairs={{0,24},{1,97},{2,26},{3,99},{4,28},{5,101},{6,30},{7,103},{8,0},{9... | collective-permute-start | bytes 1056776 | tf_op jit(solution)/shard_map/ppermute | solution.py:91
  121.7 2.1 %collective-permute-done.36.r_two = bf16[1376,128]{1,0:T(8,128)(2,1)S(1)} collective-permute-done((bf16[1376,128]{1,0:T(8,128)(2,1)S(1)}, bf16[1376,128]{1,0:T(8,128)(2,1)S(1)}, u32[]{:S(2)}, u32[]{:S(2)}) %collective-permute-start.36) | collective-permute-done | bytes 352288 | tf_op jit(solution)/shard_map/ppermute | solution.py:91
  123.8 3.7 %collective-permute-done.37.r_one = bf16[1376,128]{1,0:T(8,128)(2,1)S(1)} collective-permute-done((bf16[1376,128]{1,0:T(8,128)(2,1)S(1)}, bf16[1376,128]{1,0:T(8,128)(2,1)S(1)}, u32[]{:S(2)}, u32[]{:S(2)}) %collective-permute-start.37) | collective-permute-done | bytes 352288 | tf_op jit(solution)/shard_map/ppermute | solution.py:91
  129.4 3.3 %collective-permute-start.44 = (bf16[3840,128]{1,0:T(8,128)(2,1)S(1)}, bf16[3840,128]{1,0:T(8,128)(2,1)S(1)}, u32[]{:S(2)}, u32[]{:S(2)}) collective-permute-start(bf16[3840,128]{1,0:T(8,128)(2,1)S(1)} %get-tuple-element.174.refs_0_), channel_id=1, source_target_pairs={{0,64},{1,17},{2,66},{3,19},{4,68},{5,21},{6,70},{7,23},{8,72},{9,... | collective-permute-start | bytes 2949128 | tf_op jit(solution)/shard_map/ppermute | solution.py:91
  132.7 3.2 %collective-permute-start.41 = (bf16[3840,128]{1,0:T(8,128)(2,1)S(1)}, bf16[3840,128]{1,0:T(8,128)(2,1)S(1)}, u32[]{:S(2)}, u32[]{:S(2)}) collective-permute-start(bf16[3840,128]{1,0:T(8,128)(2,1)S(1)} %get-tuple-element.174.refs_0_), channel_id=1, source_target_pairs={{0,96},{1,25},{2,98},{3,27},{4,100},{5,29},{6,102},{7,31},{8,104},... | collective-permute-start | bytes 2949128 | tf_op jit(solution)/shard_map/ppermute | solution.py:91
  136.0 2.7 %collective-permute-start.42 = (bf16[1664,128]{1,0:T(8,128)(2,1)S(1)}, bf16[1664,128]{1,0:T(8,128)(2,1)S(1)}, u32[]{:S(2)}, u32[]{:S(2)}) collective-permute-start(bf16[1664,128]{1,0:T(8,128)(2,1)S(1)} %get-tuple-element.173.refs_1_), channel_id=1, source_target_pairs={{0,4},{1,5},{2,6},{3,7},{4,0},{5,1},{6,2},{7,3},{8,12},{9,13},{10,... | collective-permute-start | bytes 1277960 | tf_op jit(solution)/shard_map/ppermute | solution.py:639
  138.7 6.4 %collective-permute-done.44.refs_0_ = bf16[3840,128]{1,0:T(8,128)(2,1)S(1)} collective-permute-done((bf16[3840,128]{1,0:T(8,128)(2,1)S(1)}, bf16[3840,128]{1,0:T(8,128)(2,1)S(1)}, u32[]{:S(2)}, u32[]{:S(2)}) %collective-permute-start.44) | collective-permute-done | bytes 983072 | tf_op jit(solution)/shard_map/ppermute | solution.py:91
  145.1 2.6 %collective-permute-start.45 = (bf16[1664,128]{1,0:T(8,128)(2,1)S(1)}, bf16[1664,128]{1,0:T(8,128)(2,1)S(1)}, u32[]{:S(2)}, u32[]{:S(2)}) collective-permute-start(bf16[1664,128]{1,0:T(8,128)(2,1)S(1)} %get-tuple-element.173.refs_1_), channel_id=1, source_target_pairs={{0,6},{1,3},{2,0},{3,5},{4,2},{5,7},{6,4},{7,1},{8,14},{9,11},{10,... | collective-permute-start | bytes 1277960 | tf_op jit(solution)/shard_map/ppermute | solution.py:651
  149.5 2.2 %spread.3 = (f32[640,1024]{1,0:T(8,128)}, f32[640,1024]{1,0:T(8,128)}, f32[1024,640]{1,0:T(8,128)}, f32[640,512]{1,0:T(8,128)}, f32[640,128]{1,0:T(8,128)}, /*index=5*/f32[640,128]{1,0:T(8,128)}, f32[512,640]{1,0:T(8,128)}) custom-call(s32[4]{0:T(128)S(1)} %pad_add_fusion.where, bf16[3840,128]{1,0:T(8,128)(2,1)S(1)} %get-tuple-element.174.refs_0_, ...), custom_call_target="tpu_custom_call" | custom-call | flops 1024 | bytes 1024 | tf_op jit(solution)/shard_map/spread/pallas_call | solution.py:478
  153.6 2.7 %collective-permute-done.43.refs_3_ = bf16[1664,128]{1,0:T(8,128)(2,1)S(1)} collective-permute-done((bf16[1664,128]{1,0:T(8,128)(2,1)S(1)}, bf16[1664,128]{1,0:T(8,128)(2,1)S(1)}, u32[]{:S(2)}, u32[]{:S(2)}) %collective-permute-start.43) | collective-permute-done | bytes 426016 | tf_op jit(solution)/shard_map/ppermute | solution.py:640
  156.4 3.4 %spread.5 = (f32[640,1024]{1,0:T(8,128)}, f32[640,1024]{1,0:T(8,128)}, f32[1024,640]{1,0:T(8,128)}, f32[640,512]{1,0:T(8,128)}, f32[640,128]{1,0:T(8,128)}, /*index=5*/f32[640,128]{1,0:T(8,128)}, f32[512,640]{1,0:T(8,128)}) custom-call(s32[4]{0:T(128)S(1)} %pad_add_fusion.where, ...), custom_call_target="tpu_custom_call", output_to_operand_aliasing={{0}: (6, {}), {1}: (7, {}), {2}: (8, {}), {3}: (9, {}), {4}... | custom-call | flops 1024 | bytes 1024 | tf_op jit(solution)/shard_map/spread/pallas_call | solution.py:478
  (124 shorter events, 40.2 us)
Async XLA Ops:
  0.6 20.4 %collective-permute-start = (bf16[256,640]{1,0:T(8,128)(2,1)}, bf16[256,640]{1,0:T(8,128)(2,1)S(1)}, u32[]{:S(2)}, u32[]{:S(2)}) collective-permute-start(bf16[256,640]{1,0:T(8,128)(2,1)} %bitcast.13), channel_id=1, source_target_pairs={{0,4},{2,6},{4,8},{6,10},{8,12},{10,14},{12,16},{14,18},{16,20},{1... | collective-permute-start | bytes 983048 | tf_op jit(solution)/shard_map/ppermute | solution.py:98
  5.9 15.2 %collective-permute-start.1 = (bf16[256,640]{1,0:T(8,128)(2,1)}, bf16[256,640]{1,0:T(8,128)(2,1)S(1)}, u32[]{:S(2)}, u32[]{:S(2)}) collective-permute-start(bf16[256,640]{1,0:T(8,128)(2,1)} %bitcast.14), channel_id=1, source_target_pairs={{0,2},{2,4},{4,6},{6,8},{8,10},{10,12},{12,14},{14,16},{16,18},{18... | collective-permute-start | bytes 983048 | tf_op jit(solution)/shard_map/ppermute | solution.py:98
  12.9 8.2 %collective-permute-start.6 = (bf16[512,640]{1,0:T(8,128)(2,1)}, bf16[512,640]{1,0:T(8,128)(2,1)S(1)}, u32[]{:S(2)}, u32[]{:S(2)}) collective-permute-start(bf16[512,640]{1,0:T(8,128)(2,1)} %wo_m.1), channel_id=1, source_target_pairs={{0,1},{1,0},{2,3},{3,2},{4,5},{5,4},{6,7},{7,6},{8,9},{9,8},{10,11... | collective-permute-start | bytes 1966088 | tf_op jit(solution)/shard_map/ppermute | solution.py:31
  13.1 8.0 %collective-permute-start.8 = (bf16[256,640]{1,0:T(8,128)(2,1)}, bf16[256,640]{1,0:T(8,128)(2,1)S(1)}, u32[]{:S(2)}, u32[]{:S(2)}) collective-permute-start(bf16[256,640]{1,0:T(8,128)(2,1)} %bitcast.9), channel_id=1, source_target_pairs={{0,1},{1,0},{2,3},{3,2},{4,5},{5,4},{6,7},{7,6},{8,9},{9,8},{10,11... | collective-permute-start | bytes 983048 | tf_op jit(solution)/shard_map/ppermute | solution.py:31
  21.1 7.3 %collective-permute-start.10 = (bf16[640,1024]{1,0:T(8,128)(2,1)S(1)}, bf16[640,1024]{1,0:T(8,128)(2,1)S(1)}, u32[]{:S(2)}, u32[]{:S(2)}) collective-permute-start(bf16[640,1024]{1,0:T(8,128)(2,1)S(1)} %copy-done.9), channel_id=1, source_target_pairs={{0,1},{1,0},{2,3},{3,2},{4,5},{5,4},{6,7},{7,6},{8,9},{9,8},{10,11... | collective-permute-start | bytes 3932168 | tf_op jit(solution)/shard_map/ppermute | solution.py:31
  31.4 9.9 %collective-permute-start.12 = (bf16[256,1024]{1,0:T(8,128)(2,1)S(1)}, bf16[256,1024]{1,0:T(8,128)(2,1)S(1)}, u32[]{:S(2)}, u32[]{:S(2)}) collective-permute-start(bf16[256,1024]{1,0:T(8,128)(2,1)S(1)} %get-tuple-element.134), channel_id=1, source_target_pairs={{0,1},{1,0},{2,3},{3,2},{4,5},{5,4},{6,7},{7,6},{8,9},{9,8},{10,11... | collective-permute-start | bytes 1572872 | tf_op jit(solution)/shard_map/ppermute | solution.py:31
  31.9 9.6 %collective-permute-start.13 = (bf16[256,1024]{1,0:T(8,128)(2,1)S(1)}, bf16[256,1024]{1,0:T(8,128)(2,1)S(1)}, u32[]{:S(2)}, u32[]{:S(2)}) collective-permute-start(bf16[256,1024]{1,0:T(8,128)(2,1)S(1)} %get-tuple-element.136), channel_id=1, source_target_pairs={{0,1},{1,0},{2,3},{3,2},{4,5},{5,4},{6,7},{7,6},{8,9},{9,8},{10,11... | collective-permute-start | bytes 1572872 | tf_op jit(solution)/shard_map/ppermute | solution.py:31
  32.0 9.8 %collective-permute-start.14 = (bf16[256,1024]{1,0:T(8,128)(2,1)S(1)}, bf16[256,1024]{1,0:T(8,128)(2,1)S(1)}, u32[]{:S(2)}, u32[]{:S(2)}) collective-permute-start(bf16[256,1024]{1,0:T(8,128)(2,1)S(1)} %get-tuple-element.138), channel_id=1, source_target_pairs={{0,1},{1,0},{2,3},{3,2},{4,5},{5,4},{6,7},{7,6},{8,9},{9,8},{10,11... | collective-permute-start | bytes 1572872 | tf_op jit(solution)/shard_map/ppermute | solution.py:31
  32.4 12.4 %collective-permute-start.15 = (bf16[768,640]{1,0:T(8,128)(2,1)S(1)}, bf16[768,640]{1,0:T(8,128)(2,1)S(1)}, u32[]{:S(2)}, u32[]{:S(2)}) collective-permute-start(bf16[768,640]{1,0:T(8,128)(2,1)S(1)} %get-tuple-element.141.n), channel_id=1, source_target_pairs={{0,1},{1,0},{2,3},{3,2},{4,5},{5,4},{6,7},{7,6},{8,9},{9,8},{10,11... | collective-permute-start | bytes 2949128 | tf_op jit(solution)/shard_map/ppermute | solution.py:31
  48.6 11.8 %collective-permute-start.23 = (bf16[1664,128]{1,0:T(8,128)(2,1)S(1)}, bf16[1664,128]{1,0:T(8,128)(2,1)S(1)}, u32[]{:S(2)}, u32[]{:S(2)}) collective-permute-start(bf16[1664,128]{1,0:T(8,128)(2,1)S(1)} %get-tuple-element.155), channel_id=1, source_target_pairs={{0,2},{1,7},{2,0},{3,5},{4,6},{5,3},{6,4},{7,1},{8,10},{9,15},{10,... | collective-permute-start | bytes 1277960 | tf_op jit(solution)/shard_map/ppermute | solution.py:75
  50.2 20.5 %collective-permute-start.19 = (bf16[3840,128]{1,0:T(8,128)(2,1)S(1)}, bf16[3840,128]{1,0:T(8,128)(2,1)S(1)}, u32[]{:S(2)}, u32[]{:S(2)}) collective-permute-start(bf16[3840,128]{1,0:T(8,128)(2,1)S(1)} %get-tuple-element.150), channel_id=1, source_target_pairs={{0,64},{1,17},{2,66},{3,19},{4,68},{5,21},{6,70},{7,23},{8,72},{9,... | collective-permute-start | bytes 2949128 | tf_op jit(solution)/shard_map/ppermute | solution.py:91
  55.3 22.6 %collective-permute-start.20 = (bf16[3840,128]{1,0:T(8,128)(2,1)S(1)}, bf16[3840,128]{1,0:T(8,128)(2,1)S(1)}, u32[]{:S(2)}, u32[]{:S(2)}) collective-permute-start(bf16[3840,128]{1,0:T(8,128)(2,1)S(1)} %get-tuple-element.151), channel_id=1, source_target_pairs={{0,32},{1,9},{2,34},{3,11},{4,36},{5,13},{6,38},{7,15},{8,40},{9,1... | collective-permute-start | bytes 2949128 | tf_op jit(solution)/shard_map/ppermute | solution.py:91
  55.9 22.6 %collective-permute-start.21 = (bf16[3840,128]{1,0:T(8,128)(2,1)S(1)}, bf16[3840,128]{1,0:T(8,128)(2,1)S(1)}, u32[]{:S(2)}, u32[]{:S(2)}) collective-permute-start(bf16[3840,128]{1,0:T(8,128)(2,1)S(1)} %get-tuple-element.152), channel_id=1, source_target_pairs={{0,96},{1,25},{2,98},{3,27},{4,100},{5,29},{6,102},{7,31},{8,104},... | collective-permute-start | bytes 2949128 | tf_op jit(solution)/shard_map/ppermute | solution.py:91
  58.5 12.2 %collective-permute-start.22 = (bf16[1664,128]{1,0:T(8,128)(2,1)S(1)}, bf16[1664,128]{1,0:T(8,128)(2,1)S(1)}, u32[]{:S(2)}, u32[]{:S(2)}) collective-permute-start(bf16[1664,128]{1,0:T(8,128)(2,1)S(1)} %get-tuple-element.153), channel_id=1, source_target_pairs={{0,2},{1,7},{2,0},{3,5},{4,6},{5,3},{6,4},{7,1},{8,10},{9,15},{10,... | collective-permute-start | bytes 1277960 | tf_op jit(solution)/shard_map/ppermute | solution.py:75
  60.6 18.0 %collective-permute-start.24 = (bf16[1664,128]{1,0:T(8,128)(2,1)S(1)}, bf16[1664,128]{1,0:T(8,128)(2,1)S(1)}, u32[]{:S(2)}, u32[]{:S(2)}) collective-permute-start(bf16[1664,128]{1,0:T(8,128)(2,1)S(1)} %add_convert_fusion), channel_id=1, source_target_pairs={{0,6},{1,3},{2,4},{3,1},{4,2},{5,7},{6,0},{7,5},{8,14},{9,11},{10,... | collective-permute-start | bytes 1277960 | tf_op jit(solution)/shard_map/ppermute | solution.py:75
  79.8 9.0 %collective-permute-start.25 = (bf16[1376,128]{1,0:T(8,128)(2,1)S(1)}, bf16[1376,128]{1,0:T(8,128)(2,1)S(1)}, u32[]{:S(2)}, u32[]{:S(2)}) collective-permute-start(bf16[1376,128]{1,0:T(8,128)(2,1)S(1)} %get-tuple-element.157), channel_id=1, source_target_pairs={{0,16},{1,65},{2,18},{3,67},{4,20},{5,69},{6,22},{7,71},{8,24},{9,... | collective-permute-start | bytes 1056776 | tf_op jit(solution)/shard_map/ppermute | solution.py:91
  81.6 10.9 %collective-permute-start.26 = (bf16[1376,128]{1,0:T(8,128)(2,1)S(1)}, bf16[1376,128]{1,0:T(8,128)(2,1)S(1)}, u32[]{:S(2)}, u32[]{:S(2)}) collective-permute-start(bf16[1376,128]{1,0:T(8,128)(2,1)S(1)} %get-tuple-element.158), channel_id=1, source_target_pairs={{0,8},{1,33},{2,10},{3,35},{4,12},{5,37},{6,14},{7,39},{8,16},{9,4... | collective-permute-start | bytes 1056776 | tf_op jit(solution)/shard_map/ppermute | solution.py:91
  82.6 9.9 %collective-permute-start.27 = (bf16[1376,128]{1,0:T(8,128)(2,1)S(1)}, bf16[1376,128]{1,0:T(8,128)(2,1)S(1)}, u32[]{:S(2)}, u32[]{:S(2)}) collective-permute-start(bf16[1376,128]{1,0:T(8,128)(2,1)S(1)} %get-tuple-element.159), channel_id=1, source_target_pairs={{0,24},{1,97},{2,26},{3,99},{4,28},{5,101},{6,30},{7,103},{8,0},{9... | collective-permute-start | bytes 1056776 | tf_op jit(solution)/shard_map/ppermute | solution.py:91
  94.1 9.9 %collective-permute-start.30 = (bf16[960,128]{1,0:T(8,128)(2,1)S(1)}, bf16[960,128]{1,0:T(8,128)(2,1)S(1)}, u32[]{:S(2)}, u32[]{:S(2)}) collective-permute-start(bf16[960,128]{1,0:T(8,128)(2,1)S(1)} %add_convert_fusion.3), channel_id=1, source_target_pairs={{0,2},{1,7},{2,0},{3,5},{4,6},{5,3},{6,4},{7,1},{8,10},{9,15},{10,... | collective-permute-start | bytes 737288 | tf_op jit(solution)/shard_map/ppermute | solution.py:75
  96.1 12.6 %collective-permute-start.29 = (bf16[256,512]{1,0:T(8,128)(2,1)S(1)}, bf16[256,512]{1,0:T(8,128)(2,1)S(1)}, u32[]{:S(2)}, u32[]{:S(2)}) collective-permute-start(bf16[256,512]{1,0:T(8,128)(2,1)S(1)} %get-tuple-element.162), channel_id=1, source_target_pairs={{4,0},{6,2},{8,4},{10,6},{12,8},{14,10},{16,12},{18,14},{20,16},{2... | collective-permute-start | bytes 786440 | tf_op jit(solution)/shard_map/ppermute | solution.py:98
  97.4 15.0 %collective-permute-start.28 = (bf16[256,512]{1,0:T(8,128)(2,1)S(1)}, bf16[256,512]{1,0:T(8,128)(2,1)S(1)}, u32[]{:S(2)}, u32[]{:S(2)}) collective-permute-start(bf16[256,512]{1,0:T(8,128)(2,1)S(1)} %get-tuple-element.160), channel_id=1, source_target_pairs={{2,0},{4,2},{6,4},{8,6},{10,8},{12,10},{14,12},{16,14},{18,16},{20... | collective-permute-start | bytes 786440 | tf_op jit(solution)/shard_map/ppermute | solution.py:98
  104.1 9.7 %collective-permute-start.33 = (bf16[416,128]{1,0:T(8,128)(2,1)S(1)}, bf16[416,128]{1,0:T(8,128)(2,1)S(1)}, u32[]{:S(2)}, u32[]{:S(2)}) collective-permute-start(bf16[416,128]{1,0:T(8,128)(2,1)S(1)} %add_convert_fusion.5), channel_id=1, source_target_pairs={{0,96},{1,25},{2,98},{3,27},{4,100},{5,29},{6,102},{7,31},{8,104},... | collective-permute-start | bytes 319496 | tf_op jit(solution)/shard_map/ppermute | solution.py:83
  107.0 7.4 %collective-permute-start.31 = (bf16[960,128]{1,0:T(8,128)(2,1)S(1)}, bf16[960,128]{1,0:T(8,128)(2,1)S(1)}, u32[]{:S(2)}, u32[]{:S(2)}) collective-permute-start(bf16[960,128]{1,0:T(8,128)(2,1)S(1)} %add_convert_fusion.2), channel_id=1, source_target_pairs={{0,6},{1,3},{2,4},{3,1},{4,2},{5,7},{6,0},{7,5},{8,14},{9,11},{10,... | collective-permute-start | bytes 737288 | tf_op jit(solution)/shard_map/ppermute | solution.py:75
  114.8 9.0 %collective-permute-start.36 = (bf16[1376,128]{1,0:T(8,128)(2,1)S(1)}, bf16[1376,128]{1,0:T(8,128)(2,1)S(1)}, u32[]{:S(2)}, u32[]{:S(2)}) collective-permute-start(bf16[1376,128]{1,0:T(8,128)(2,1)S(1)} %pad_maximum_fusion.own), channel_id=1, source_target_pairs={{0,16},{1,65},{2,18},{3,67},{4,20},{5,69},{6,22},{7,71},{8,24},{9,... | collective-permute-start | bytes 1056776 | tf_op jit(solution)/shard_map/ppermute | solution.py:91
  118.4 9.1 %collective-permute-start.37 = (bf16[1376,128]{1,0:T(8,128)(2,1)S(1)}, bf16[1376,128]{1,0:T(8,128)(2,1)S(1)}, u32[]{:S(2)}, u32[]{:S(2)}) collective-permute-start(bf16[1376,128]{1,0:T(8,128)(2,1)S(1)} %pad_maximum_fusion.own), channel_id=1, source_target_pairs={{0,8},{1,33},{2,10},{3,35},{4,12},{5,37},{6,14},{7,39},{8,16},{9,4... | collective-permute-start | bytes 1056776 | tf_op jit(solution)/shard_map/ppermute | solution.py:91
  118.4 9.1 %collective-permute-start.38 = (bf16[1376,128]{1,0:T(8,128)(2,1)S(1)}, bf16[1376,128]{1,0:T(8,128)(2,1)S(1)}, u32[]{:S(2)}, u32[]{:S(2)}) collective-permute-start(bf16[1376,128]{1,0:T(8,128)(2,1)S(1)} %pad_maximum_fusion.own), channel_id=1, source_target_pairs={{0,24},{1,97},{2,26},{3,99},{4,28},{5,101},{6,30},{7,103},{8,0},{9... | collective-permute-start | bytes 1056776 | tf_op jit(solution)/shard_map/ppermute | solution.py:91
  129.4 15.7 %collective-permute-start.44 = (bf16[3840,128]{1,0:T(8,128)(2,1)S(1)}, bf16[3840,128]{1,0:T(8,128)(2,1)S(1)}, u32[]{:S(2)}, u32[]{:S(2)}) collective-permute-start(bf16[3840,128]{1,0:T(8,128)(2,1)S(1)} %get-tuple-element.174.refs_0_), channel_id=1, source_target_pairs={{0,64},{1,17},{2,66},{3,19},{4,68},{5,21},{6,70},{7,23},{8,72},{9,... | collective-permute-start | bytes 2949128 | tf_op jit(solution)/shard_map/ppermute | solution.py:91
  132.7 23.6 %collective-permute-start.40 = (bf16[3840,128]{1,0:T(8,128)(2,1)S(1)}, bf16[3840,128]{1,0:T(8,128)(2,1)S(1)}, u32[]{:S(2)}, u32[]{:S(2)}) collective-permute-start(bf16[3840,128]{1,0:T(8,128)(2,1)S(1)} %get-tuple-element.174.refs_0_), channel_id=1, source_target_pairs={{0,32},{1,9},{2,34},{3,11},{4,36},{5,13},{6,38},{7,15},{8,40},{9,1... | collective-permute-start | bytes 2949128 | tf_op jit(solution)/shard_map/ppermute | solution.py:91
  132.7 23.6 %collective-permute-start.41 = (bf16[3840,128]{1,0:T(8,128)(2,1)S(1)}, bf16[3840,128]{1,0:T(8,128)(2,1)S(1)}, u32[]{:S(2)}, u32[]{:S(2)}) collective-permute-start(bf16[3840,128]{1,0:T(8,128)(2,1)S(1)} %get-tuple-element.174.refs_0_), channel_id=1, source_target_pairs={{0,96},{1,25},{2,98},{3,27},{4,100},{5,29},{6,102},{7,31},{8,104},... | collective-permute-start | bytes 2949128 | tf_op jit(solution)/shard_map/ppermute | solution.py:91
  136.0 17.6 %collective-permute-start.42 = (bf16[1664,128]{1,0:T(8,128)(2,1)S(1)}, bf16[1664,128]{1,0:T(8,128)(2,1)S(1)}, u32[]{:S(2)}, u32[]{:S(2)}) collective-permute-start(bf16[1664,128]{1,0:T(8,128)(2,1)S(1)} %get-tuple-element.173.refs_1_), channel_id=1, source_target_pairs={{0,4},{1,5},{2,6},{3,7},{4,0},{5,1},{6,2},{7,3},{8,12},{9,13},{10,... | collective-permute-start | bytes 1277960 | tf_op jit(solution)/shard_map/ppermute | solution.py:639
  138.7 17.6 %collective-permute-start.43 = (bf16[1664,128]{1,0:T(8,128)(2,1)S(1)}, bf16[1664,128]{1,0:T(8,128)(2,1)S(1)}, u32[]{:S(2)}, u32[]{:S(2)}) collective-permute-start(bf16[1664,128]{1,0:T(8,128)(2,1)S(1)} %get-tuple-element.173.refs_1_), channel_id=1, source_target_pairs={{0,2},{1,7},{2,4},{3,1},{4,6},{5,3},{6,0},{7,5},{8,10},{9,15},{10,... | collective-permute-start | bytes 1277960 | tf_op jit(solution)/shard_map/ppermute | solution.py:640
  145.1 11.2 %collective-permute-start.45 = (bf16[1664,128]{1,0:T(8,128)(2,1)S(1)}, bf16[1664,128]{1,0:T(8,128)(2,1)S(1)}, u32[]{:S(2)}, u32[]{:S(2)}) collective-permute-start(bf16[1664,128]{1,0:T(8,128)(2,1)S(1)} %get-tuple-element.173.refs_1_), channel_id=1, source_target_pairs={{0,6},{1,3},{2,0},{3,5},{4,2},{5,7},{6,4},{7,1},{8,14},{9,11},{10,... | collective-permute-start | bytes 1277960 | tf_op jit(solution)/shard_map/ppermute | solution.py:651
  (28 other events, 113.0 us)

commit v2 on v1

--- a/solution.py
+++ b/solution.py
@@ -174,7 +174,7 @@
 
 def attend_body(
     far_two, far_one, normed, wide, query, wkv, gain, wo_m, wo_o, gain_two, cos, sin, pos_row,
-    normed_all, query_kept, kv, ctx_m, ctx_o, lse, after, normed_two,
+    normed_all, query_kept, kv, ctx_m, ctx_o, kept, after, normed_two,
 ):
     query_kept[...] = query[...]
     normed_all[512:, :] = normed[...]
@@ -193,8 +193,9 @@
         top = jnp.max(scores, axis=-1, keepdims=True)
         exps = jnp.exp(scores - top)
         total = jnp.sum(exps, axis=-1, keepdims=True)
-        lse[:, head * 128 : (head + 1) * 128] = jnp.broadcast_to(top + jnp.log(total), (256, 128))
-        probs = (exps * (1.0 / total)).astype(BF16)
+        probs = exps * (1.0 / total)
+        kept[head] = probs
+        probs = probs.astype(BF16)
         context = (ctx_m, ctx_o)[head // 2]
         at = head % 2 * HEAD
         context[:, at : at + HEAD] = dot(probs, kv[:, HEAD:]).astype(BF16)
@@ -289,11 +290,10 @@
 
 
 def attend_grad_body(
-    where, query, kv, lse, ga_low, wo_m, wo_o, cos, sin, pos_row,
+    where, query, kv, kept, ga_low, wo_m, wo_o, cos, sin,
     dq_m, dq_o, dkv, back_two, back_one, dkv_m, packed,
 ):
     dkv_o = packed.at[512:, :]
-    ok = allowed_pairs(pos_row)
     ga = ga_low[...]
     grad_k = None
     grad_v = None
@@ -305,8 +305,7 @@
             q = query[:, cols]
             gc = grad_context[:, head * HEAD : (head + 1) * HEAD]
             which = half * 2 + head
-            scores = jnp.where(ok, dot_nt(q, kv[:, :HEAD]), neg_fill)
-            probs = jnp.exp(scores - lse[:, which * 128 : which * 128 + 1])
+            probs = kept[which]
             part = dot_tn(probs.astype(BF16), gc)
             grad_v = part if grad_v is None else grad_v + part
             grad_probs = dot_nt(gc, kv[:, HEAD:])
@@ -548,32 +547,32 @@
         us=6, scalars=1,
     )
     first = (normed, far_one, far_two, out_other, gy_r)
-    gate_other = swap(after(w_gate, *first))
+    gate_other = swap(after(w_gate, out_other, query_other))
     up_other = swap(after(w_up, *first))
     down_other = swap(after(w_down, *first))
-    normed_all, query, kv, ctx_m, ctx_o, lse, after_attn, normed_two = call(
+    normed_all, query, kv, ctx_m, ctx_o, kept, after_attn, normed_two = call(
         "attend", attend_body,
         [
             ((3 * rows, D), BF16), ((rows, HEADS * HEAD), BF16), ((3 * rows, 2 * HEAD), BF16),
-            ((rows, MINE), BF16), ((rows, MINE), BF16), ((rows, 512), F32), ((rows, D), F32),
+            ((rows, MINE), BF16), ((rows, MINE), BF16), ((HEADS, rows, 3 * rows), F32), ((rows, D), F32),
             ((rows, D), BF16),
         ],
         [
-            far_two, far_one, normed, wide, query, wkv, gain_one, wo_near, out_other, gain_two,
+            far_two, far_one, normed, wide, query, wkv, after(gain_one, gate_other), wo_near,
+            out_other, gain_two,
             cos, sin, pos_row,
         ],
         us=5,
     )
-    normed_two_r = swap(normed_two)
     half_ffn = [((rows, FF // 2), BF16)] * 3
     hid_o, dg_o, du_o, total_o, grad_n_o = call(
         "ffn_other", ffn_other_body, [*half_ffn, ((rows, D), F32), ((rows, D), F32)],
         [normed_two, gy, gate_other, up_other, down_other],
         us=5,
     )
-    gain_two = after(gain_two, normed_two_r)
     hid_r, dg_r, du_r = swap(hid_o), swap(dg_o), swap(du_o)
-    ctx_r, normed_r = swap(after(ctx_o, hid_o)), swap(after(normed_all, hid_o))
+    normed_two_r, normed_r = swap(after(normed_two, hid_o)), swap(after(normed_all, hid_o))
+    ctx_r = swap(after(ctx_o, hid_r))
     out, hid_m, dg_m, du_m, grad_after, ga_low, grad_gain_two = call(
         "ffn", ffn_body,
         [((rows, D), BF16), *half_ffn, ((rows, D), F32), ((rows, D), BF16), ((1, D), F32)],
@@ -588,7 +587,7 @@
             ((3 * rows, HEAD), BF16), ((5 * rows, HEAD), BF16),
         ],
         [
-            where, query, kv, lse, ga_low, w_out, out_other, cos, sin, pos_row,
+            where, query, kv, kept, ga_low, w_out, out_other, cos, sin,
         ],
         us=0, scalars=1,
     )

time: 162 us -> 161 us (level)
  waiting for transfers between devices: 57.8 us -> 55.4 us
    ppermute x5, waiting for transfers between devices: 15.2 us -> 12.5 us  [swap_y(): lax.ppermute(v, ('ctx', 'fsdp'), chip_pairs(lambda x, z, y, c: (x, z, (pa...]
  transfers between devices with their start and end apart: 46 -> 46, of which waited for: 18 -> 20; matrix products, arithmetic and copies ran while one was open for 2% -> 2% of each run, Pallas kernels for 13% -> 14%
where the time goes in v2:
time: 161 us; the launch traced here: 159 us
  starting transfers between devices  59 us (37%)
  waiting for transfers between devices  55.4 us (34%)
  Pallas kernels  34.1 us (21%)
  local copies, waits for them, and re-layouts  5.78 us (4%)
  other arithmetic  3.83 us (2%)
    ppermute x12, waiting for transfers between devices, to_peers(): lax.ppermute(part, ('ctx', 'fsdp'), shift(by))  28.6 us
    pallas_call x10, Pallas kernels, call(): pl.pallas_call(body, out_shape=shapes, in_specs=[smem] * scalars + [whole...  26.6 us
    ppermute x12, starting transfers between devices, to_peers(): lax.ppermute(part, ('ctx', 'fsdp'), shift(by))  26 us
    ppermute x5, waiting for transfers between devices, swap_y(): lax.ppermute(v, ('ctx', 'fsdp'), chip_pairs(lambda x, z, y, c: (x, z, (pa...  12.5 us
    ppermute x4, starting transfers between devices, passed_along(): return lax.ppermute(shard, 'ctx', pairs)  10.4 us
    pallas_call x3, Pallas kernels, spread(): pl.pallas_call(functools.partial(spread_body, f_places, a_places, not sha...  7.48 us
    ppermute x5, starting transfers between devices, swap_y(): lax.ppermute(v, ('ctx', 'fsdp'), chip_pairs(lambda x, z, y, c: (x, z, (pa...  6.42 us
    ppermute x20, waiting for transfers between devices, swap(): return lax.ppermute(x, 'fsdp', [(0, 1), (1, 0)])  5.99 us
  transfers between devices with their start and end apart: 46, of which 20 were waited for; matrix products, arithmetic and copies ran while one was open for 2% of the time, Pallas kernels for 14%

profile of v2, /device:TPU:0, one launch (start us, length us, event | category | flops | bytes accessed | tf_op | source)
XLA Modules:
  0.0 159.2 jit_solution(10076914518487379959)
XLA Ops:
  0.6 5.2 %collective-permute-start = (bf16[256,640]{1,0:T(8,128)(2,1)}, bf16[256,640]{1,0:T(8,128)(2,1)S(1)}, u32[]{:S(2)}, u32[]{:S(2)}) collective-permute-start(bf16[256,640]{1,0:T(8,128)(2,1)} %bitcast.13), channel_id=1, source_target_pairs={{0,4},{2,6},{4,8},{6,10},{8,12},{10,14},{12,16},{14,18},{16,20},{1... | collective-permute-start | bytes 983048 | tf_op jit(solution)/shard_map/ppermute | solution.py:98
  5.9 2.6 %collective-permute-start.1 = (bf16[256,640]{1,0:T(8,128)(2,1)}, bf16[256,640]{1,0:T(8,128)(2,1)S(1)}, u32[]{:S(2)}, u32[]{:S(2)}) collective-permute-start(bf16[256,640]{1,0:T(8,128)(2,1)} %bitcast.14), channel_id=1, source_target_pairs={{0,2},{2,4},{4,6},{6,8},{8,10},{10,12},{12,14},{14,16},{16,18},{18... | collective-permute-start | bytes 983048 | tf_op jit(solution)/shard_map/ppermute | solution.py:98
  23.0 3.4 %attend.1 = (bf16[768,640]{1,0:T(8,128)(2,1)S(1)}, bf16[256,1024]{1,0:T(8,128)(2,1)S(1)}, bf16[768,512]{1,0:T(8,128)(2,1)S(1)}, bf16[256,512]{1,0:T(8,128)(2,1)S...) custom-call(bf16[256,640]{1,0:T(8,128)(2,1)S(1)} %collective-permute, ...), custom_call_target="tpu_custom_call" | custom-call | flops 5500000256 | bytes 1024 | tf_op jit(solution)/shard_map/attend/pallas_call | solution.py:118
  27.4 3.1 %ffn_other.1 = (bf16[256,1024]{1,0:T(8,128)(2,1)S(1)}, bf16[256,1024]{1,0:T(8,128)(2,1)S(1)}, bf16[256,1024]{1,0:T(8,128)(2,1)S(1)}, f32[256,640]{1,0:T(8,128)S(1)}, f32[256,640]{1,0:T(8,128)S(1)}) custom-call(bf16[256,640]{1,0:T(8,128)(2,1)S(1)} %get-tuple-element.140.normed_two.n, bf16[256,640]{1,0:T(8,128)(2,1)S(1)} %bitcast.10, ...), custom_call_target="tpu_custom_call" | custom-call | flops 5500000256 | bytes 1024 | tf_op jit(solution)/shard_map/ffn_other/pallas_call | solution.py:118
  31.8 4.2 %ffn.1 = (bf16[256,640]{1,0:T(8,128)(2,1)}, bf16[256,1024]{1,0:T(8,128)(2,1)S(1)}, bf16[256,1024]{1,0:T(8,128)(2,1)S(1)}, bf16[256,1024]{1,0:T(8,128)(2,1)S(1)},...) custom-call(f32[256,640]{1,0:T(8,128)S(1)} %get-tuple-element.115.after, ...), custom_call_target="tpu_custom_call" | custom-call | flops 4400000000 | bytes 1024 | tf_op jit(solution)/shard_map/ffn/pallas_call | solution.py:118
  35.9 4.2 %attend_grad.1 = (bf16[256,512]{1,0:T(8,128)(2,1)S(1)}, bf16[256,512]{1,0:T(8,128)(2,1)S(1)}, bf16[256,512]{1,0:T(8,128)(2,1)S(1)}, bf16[256,512]{1,0:T(8,128)(2...) custom-call(s32[4]{0:T(128)S(1)} %pad_add_fusion.where, ...), custom_call_target="tpu_custom_call" | custom-call | bytes 1024 | tf_op jit(solution)/shard_map/attend_grad/pallas_call | solution.py:118
  41.1 2.9 %ffn_grads.1 = (bf16[3840,128]{1,0:T(8,128)(2,1)S(1)}, bf16[3840,128]{1,0:T(8,128)(2,1)S(1)}, bf16[3840,128]{1,0:T(8,128)(2,1)S(1)}, bf16[3840,128]{1,0:T(8,128)(2,1)S(1)}) custom-call(s32[4]{0:T(128)S(1)} %pad_add_fusion.where, bf16[256,1024]{1,0:T(8,128)(2,1)S(1)} %get-tuple-element.134.hid_m, bf16[256,1024]{1,0:T(8,128)(2,1)S(1)} %collective-permute-done.11.hid_r, ...), custom_call_target="tpu_custom_call" | custom-call | flops 3300000000 | bytes 1024 | tf_op jit(solution)/shard_map/ffn_grads/pallas_call | solution.py:118
  44.1 3.8 %attend_grads.1 = (bf16[1664,128]{1,0:T(8,128)(2,1)S(1)}, bf16[1664,128]{1,0:T(8,128)(2,1)S(1)}, bf16[1664,128]{1,0:T(8,128)(2,1)S(1)}, bf16[1664,128]{1,0:T(8,128)(2,1)S(1)}) custom-call(s32[4]{0:T(128)S(1)} %pad_add_fusion.where, bf16[768,640]{1,0:T(8,128)(2,1)S(1)} %get-tuple-element.143.n, bf16[768,640]{1,0:T(8,128)(2,1)S(1)} %collective-permute-done.15.n_r, ...), custom_call_target="tpu_custom_call" | custom-call | bytes 1024 | tf_op jit(solution)/shard_map/attend_grads/pallas_call | solution.py:118
  48.9 4.5 %collective-permute-start.19 = (bf16[3840,128]{1,0:T(8,128)(2,1)S(1)}, bf16[3840,128]{1,0:T(8,128)(2,1)S(1)}, u32[]{:S(2)}, u32[]{:S(2)}) collective-permute-start(bf16[3840,128]{1,0:T(8,128)(2,1)S(1)} %get-tuple-element.152), channel_id=1, source_target_pairs={{0,64},{1,17},{2,66},{3,19},{4,68},{5,21},{6,70},{7,23},{8,72},{9,... | collective-permute-start | bytes 2949128 | tf_op jit(solution)/shard_map/ppermute | solution.py:91
  54.1 2.6 %collective-permute-start.21 = (bf16[3840,128]{1,0:T(8,128)(2,1)S(1)}, bf16[3840,128]{1,0:T(8,128)(2,1)S(1)}, u32[]{:S(2)}, u32[]{:S(2)}) collective-permute-start(bf16[3840,128]{1,0:T(8,128)(2,1)S(1)} %get-tuple-element.154), channel_id=1, source_target_pairs={{0,96},{1,25},{2,98},{3,27},{4,100},{5,29},{6,102},{7,31},{8,104},... | collective-permute-start | bytes 2949128 | tf_op jit(solution)/shard_map/ppermute | solution.py:91
  58.5 1.9 %collective-permute-start.24 = (bf16[1664,128]{1,0:T(8,128)(2,1)S(1)}, bf16[1664,128]{1,0:T(8,128)(2,1)S(1)}, u32[]{:S(2)}, u32[]{:S(2)}) collective-permute-start(bf16[1664,128]{1,0:T(8,128)(2,1)S(1)} %add_convert_fusion), channel_id=1, source_target_pairs={{0,6},{1,3},{2,4},{3,1},{4,2},{5,7},{6,0},{7,5},{8,14},{9,11},{10,... | collective-permute-start | bytes 1277960 | tf_op jit(solution)/shard_map/ppermute | solution.py:75
  60.4 8.4 %collective-permute-done.22.a_one = bf16[1664,128]{1,0:T(8,128)(2,1)S(1)} collective-permute-done((bf16[1664,128]{1,0:T(8,128)(2,1)S(1)}, bf16[1664,128]{1,0:T(8,128)(2,1)S(1)}, u32[]{:S(2)}, u32[]{:S(2)}) %collective-permute-start.22) | collective-permute-done | bytes 426016 | tf_op jit(solution)/shard_map/ppermute | solution.py:75
  68.7 7.3 %collective-permute-done.20.r_one = bf16[3840,128]{1,0:T(8,128)(2,1)S(1)} collective-permute-done((bf16[3840,128]{1,0:T(8,128)(2,1)S(1)}, bf16[3840,128]{1,0:T(8,128)(2,1)S(1)}, u32[]{:S(2)}, u32[]{:S(2)}) %collective-permute-start.20) | collective-permute-done | bytes 983072 | tf_op jit(solution)/shard_map/ppermute | solution.py:91
  77.9 2.2 %collective-permute-start.25 = (bf16[1376,128]{1,0:T(8,128)(2,1)S(1)}, bf16[1376,128]{1,0:T(8,128)(2,1)S(1)}, u32[]{:S(2)}, u32[]{:S(2)}) collective-permute-start(bf16[1376,128]{1,0:T(8,128)(2,1)S(1)} %get-tuple-element.159), channel_id=1, source_target_pairs={{0,16},{1,65},{2,18},{3,67},{4,20},{5,69},{6,22},{7,71},{8,24},{9,... | collective-permute-start | bytes 1056776 | tf_op jit(solution)/shard_map/ppermute | solution.py:91
  80.7 2.6 %collective-permute-start.27 = (bf16[1376,128]{1,0:T(8,128)(2,1)S(1)}, bf16[1376,128]{1,0:T(8,128)(2,1)S(1)}, u32[]{:S(2)}, u32[]{:S(2)}) collective-permute-start(bf16[1376,128]{1,0:T(8,128)(2,1)S(1)} %get-tuple-element.161), channel_id=1, source_target_pairs={{0,24},{1,97},{2,26},{3,99},{4,28},{5,101},{6,30},{7,103},{8,0},{9... | collective-permute-start | bytes 1056776 | tf_op jit(solution)/shard_map/ppermute | solution.py:91
  83.3 3.6 %collective-permute-done.25 = bf16[1376,128]{1,0:T(8,128)(2,1)S(1)} collective-permute-done((bf16[1376,128]{1,0:T(8,128)(2,1)S(1)}, bf16[1376,128]{1,0:T(8,128)(2,1)S(1)}, u32[]{:S(2)}, u32[]{:S(2)}) %collective-permute-start.25) | collective-permute-done | bytes 352288 | tf_op jit(solution)/shard_map/ppermute | solution.py:91
  86.9 3.7 %collective-permute-done.26 = bf16[1376,128]{1,0:T(8,128)(2,1)S(1)} collective-permute-done((bf16[1376,128]{1,0:T(8,128)(2,1)S(1)}, bf16[1376,128]{1,0:T(8,128)(2,1)S(1)}, u32[]{:S(2)}, u32[]{:S(2)}) %collective-permute-start.26) | collective-permute-done | bytes 352288 | tf_op jit(solution)/shard_map/ppermute | solution.py:91
  96.7 3.9 %collective-permute-done.30 = bf16[960,128]{1,0:T(8,128)(2,1)S(1)} collective-permute-done((bf16[960,128]{1,0:T(8,128)(2,1)S(1)}, bf16[960,128]{1,0:T(8,128)(2,1)S(1)}, u32[]{:S(2)}, u32[]{:S(2)}) %collective-permute-start.30) | collective-permute-done | bytes 245792 | tf_op jit(solution)/shard_map/ppermute | solution.py:75
  100.6 4.4 %collective-permute-start.33 = (bf16[416,128]{1,0:T(8,128)(2,1)S(1)}, bf16[416,128]{1,0:T(8,128)(2,1)S(1)}, u32[]{:S(2)}, u32[]{:S(2)}) collective-permute-start(bf16[416,128]{1,0:T(8,128)(2,1)S(1)} %add_convert_fusion.5), channel_id=1, source_target_pairs={{0,96},{1,25},{2,98},{3,27},{4,100},{5,29},{6,102},{7,31},{8,104},... | collective-permute-start | bytes 319496 | tf_op jit(solution)/shard_map/ppermute | solution.py:83
  106.7 4.4 %collective-permute-done.28.back_one = bf16[256,512]{1,0:T(8,128)(2,1)S(1)} collective-permute-done((bf16[256,512]{1,0:T(8,128)(2,1)S(1)}, bf16[256,512]{1,0:T(8,128)(2,1)S(1)}, u32[]{:S(2)}, u32[]{:S(2)}) %collective-permute-start.28) | collective-permute-done | bytes 262176 | tf_op jit(solution)/shard_map/ppermute | solution.py:98
  113.4 3.4 %collective-permute-start.36 = (bf16[1376,128]{1,0:T(8,128)(2,1)S(1)}, bf16[1376,128]{1,0:T(8,128)(2,1)S(1)}, u32[]{:S(2)}, u32[]{:S(2)}) collective-permute-start(bf16[1376,128]{1,0:T(8,128)(2,1)S(1)} %pad_maximum_fusion.own), channel_id=1, source_target_pairs={{0,16},{1,65},{2,18},{3,67},{4,20},{5,69},{6,22},{7,71},{8,24},{9,... | collective-permute-start | bytes 1056776 | tf_op jit(solution)/shard_map/ppermute | solution.py:91
  117.5 2.5 %collective-permute-start.38 = (bf16[1376,128]{1,0:T(8,128)(2,1)S(1)}, bf16[1376,128]{1,0:T(8,128)(2,1)S(1)}, u32[]{:S(2)}, u32[]{:S(2)}) collective-permute-start(bf16[1376,128]{1,0:T(8,128)(2,1)S(1)} %pad_maximum_fusion.own), channel_id=1, source_target_pairs={{0,24},{1,97},{2,26},{3,99},{4,28},{5,101},{6,30},{7,103},{8,0},{9... | collective-permute-start | bytes 1056776 | tf_op jit(solution)/shard_map/ppermute | solution.py:91
  120.0 2.3 %collective-permute-done.36.r_two = bf16[1376,128]{1,0:T(8,128)(2,1)S(1)} collective-permute-done((bf16[1376,128]{1,0:T(8,128)(2,1)S(1)}, bf16[1376,128]{1,0:T(8,128)(2,1)S(1)}, u32[]{:S(2)}, u32[]{:S(2)}) %collective-permute-start.36) | collective-permute-done | bytes 352288 | tf_op jit(solution)/shard_map/ppermute | solution.py:91
  122.3 3.7 %collective-permute-done.37.r_one = bf16[1376,128]{1,0:T(8,128)(2,1)S(1)} collective-permute-done((bf16[1376,128]{1,0:T(8,128)(2,1)S(1)}, bf16[1376,128]{1,0:T(8,128)(2,1)S(1)}, u32[]{:S(2)}, u32[]{:S(2)}) %collective-permute-start.37) | collective-permute-done | bytes 352288 | tf_op jit(solution)/shard_map/ppermute | solution.py:91
  128.5 3.1 %collective-permute-start.44 = (bf16[3840,128]{1,0:T(8,128)(2,1)S(1)}, bf16[3840,128]{1,0:T(8,128)(2,1)S(1)}, u32[]{:S(2)}, u32[]{:S(2)}) collective-permute-start(bf16[3840,128]{1,0:T(8,128)(2,1)S(1)} %get-tuple-element.176.refs_0_), channel_id=1, source_target_pairs={{0,64},{1,17},{2,66},{3,19},{4,68},{5,21},{6,70},{7,23},{8,72},{9,... | collective-permute-start | bytes 2949128 | tf_op jit(solution)/shard_map/ppermute | solution.py:91
  131.6 3.2 %collective-permute-start.41 = (bf16[3840,128]{1,0:T(8,128)(2,1)S(1)}, bf16[3840,128]{1,0:T(8,128)(2,1)S(1)}, u32[]{:S(2)}, u32[]{:S(2)}) collective-permute-start(bf16[3840,128]{1,0:T(8,128)(2,1)S(1)} %get-tuple-element.176.refs_0_), channel_id=1, source_target_pairs={{0,96},{1,25},{2,98},{3,27},{4,100},{5,29},{6,102},{7,31},{8,104},... | collective-permute-start | bytes 2949128 | tf_op jit(solution)/shard_map/ppermute | solution.py:91
  134.8 2.7 %collective-permute-start.42 = (bf16[1664,128]{1,0:T(8,128)(2,1)S(1)}, bf16[1664,128]{1,0:T(8,128)(2,1)S(1)}, u32[]{:S(2)}, u32[]{:S(2)}) collective-permute-start(bf16[1664,128]{1,0:T(8,128)(2,1)S(1)} %get-tuple-element.175.refs_1_), channel_id=1, source_target_pairs={{0,4},{1,5},{2,6},{3,7},{4,0},{5,1},{6,2},{7,3},{8,12},{9,13},{10,... | collective-permute-start | bytes 1277960 | tf_op jit(solution)/shard_map/ppermute | solution.py:638
  137.6 6.7 %collective-permute-done.44.refs_0_ = bf16[3840,128]{1,0:T(8,128)(2,1)S(1)} collective-permute-done((bf16[3840,128]{1,0:T(8,128)(2,1)S(1)}, bf16[3840,128]{1,0:T(8,128)(2,1)S(1)}, u32[]{:S(2)}, u32[]{:S(2)}) %collective-permute-start.44) | collective-permute-done | bytes 983072 | tf_op jit(solution)/shard_map/ppermute | solution.py:91
  144.2 2.5 %collective-permute-start.45 = (bf16[1664,128]{1,0:T(8,128)(2,1)S(1)}, bf16[1664,128]{1,0:T(8,128)(2,1)S(1)}, u32[]{:S(2)}, u32[]{:S(2)}) collective-permute-start(bf16[1664,128]{1,0:T(8,128)(2,1)S(1)} %get-tuple-element.175.refs_1_), channel_id=1, source_target_pairs={{0,6},{1,3},{2,0},{3,5},{4,2},{5,7},{6,4},{7,1},{8,14},{9,11},{10,... | collective-permute-start | bytes 1277960 | tf_op jit(solution)/shard_map/ppermute | solution.py:650
  148.5 2.2 %spread.3 = (f32[640,1024]{1,0:T(8,128)}, f32[640,1024]{1,0:T(8,128)}, f32[1024,640]{1,0:T(8,128)}, f32[640,512]{1,0:T(8,128)}, f32[640,128]{1,0:T(8,128)}, /*index=5*/f32[640,128]{1,0:T(8,128)}, f32[512,640]{1,0:T(8,128)}) custom-call(s32[4]{0:T(128)S(1)} %pad_add_fusion.where, bf16[3840,128]{1,0:T(8,128)(2,1)S(1)} %get-tuple-element.176.refs_0_, ...), custom_call_target="tpu_custom_call" | custom-call | flops 1024 | bytes 1024 | tf_op jit(solution)/shard_map/spread/pallas_call | solution.py:477
  152.6 2.4 %collective-permute-done.43.refs_3_ = bf16[1664,128]{1,0:T(8,128)(2,1)S(1)} collective-permute-done((bf16[1664,128]{1,0:T(8,128)(2,1)S(1)}, bf16[1664,128]{1,0:T(8,128)(2,1)S(1)}, u32[]{:S(2)}, u32[]{:S(2)}) %collective-permute-start.43) | collective-permute-done | bytes 426016 | tf_op jit(solution)/shard_map/ppermute | solution.py:639
  155.0 3.4 %spread.5 = (f32[640,1024]{1,0:T(8,128)}, f32[640,1024]{1,0:T(8,128)}, f32[1024,640]{1,0:T(8,128)}, f32[640,512]{1,0:T(8,128)}, f32[640,128]{1,0:T(8,128)}, /*index=5*/f32[640,128]{1,0:T(8,128)}, f32[512,640]{1,0:T(8,128)}) custom-call(s32[4]{0:T(128)S(1)} %pad_add_fusion.where, ...), custom_call_target="tpu_custom_call", output_to_operand_aliasing={{0}: (6, {}), {1}: (7, {}), {2}: (8, {}), {3}: (9, {}), {4}... | custom-call | flops 1024 | bytes 1024 | tf_op jit(solution)/shard_map/spread/pallas_call | solution.py:477
  (124 shorter events, 41.3 us)
Async XLA Ops:
  0.6 21.7 %collective-permute-start = (bf16[256,640]{1,0:T(8,128)(2,1)}, bf16[256,640]{1,0:T(8,128)(2,1)S(1)}, u32[]{:S(2)}, u32[]{:S(2)}) collective-permute-start(bf16[256,640]{1,0:T(8,128)(2,1)} %bitcast.13), channel_id=1, source_target_pairs={{0,4},{2,6},{4,8},{6,10},{8,12},{10,14},{12,16},{14,18},{16,20},{1... | collective-permute-start | bytes 983048 | tf_op jit(solution)/shard_map/ppermute | solution.py:98
  5.9 16.5 %collective-permute-start.1 = (bf16[256,640]{1,0:T(8,128)(2,1)}, bf16[256,640]{1,0:T(8,128)(2,1)S(1)}, u32[]{:S(2)}, u32[]{:S(2)}) collective-permute-start(bf16[256,640]{1,0:T(8,128)(2,1)} %bitcast.14), channel_id=1, source_target_pairs={{0,2},{2,4},{4,6},{6,8},{8,10},{10,12},{12,14},{14,16},{16,18},{18... | collective-permute-start | bytes 983048 | tf_op jit(solution)/shard_map/ppermute | solution.py:98
  13.1 9.3 %collective-permute-start.8 = (bf16[256,640]{1,0:T(8,128)(2,1)}, bf16[256,640]{1,0:T(8,128)(2,1)S(1)}, u32[]{:S(2)}, u32[]{:S(2)}) collective-permute-start(bf16[256,640]{1,0:T(8,128)(2,1)} %bitcast.9), channel_id=1, source_target_pairs={{0,1},{1,0},{2,3},{3,2},{4,5},{5,4},{6,7},{7,6},{8,9},{9,8},{10,11... | collective-permute-start | bytes 983048 | tf_op jit(solution)/shard_map/ppermute | solution.py:31
  15.6 7.4 %collective-permute-start.7 = (bf16[640,1024]{1,0:T(8,128)(2,1)}, bf16[640,1024]{1,0:T(8,128)(2,1)S(1)}, u32[]{:S(2)}, u32[]{:S(2)}) collective-permute-start(bf16[640,1024]{1,0:T(8,128)(2,1)} %wg.1), channel_id=1, source_target_pairs={{0,1},{1,0},{2,3},{3,2},{4,5},{5,4},{6,7},{7,6},{8,9},{9,8},{10,11... | collective-permute-start | bytes 3932168 | tf_op jit(solution)/shard_map/ppermute | solution.py:31
  30.5 10.0 %collective-permute-start.11 = (bf16[256,1024]{1,0:T(8,128)(2,1)S(1)}, bf16[256,1024]{1,0:T(8,128)(2,1)S(1)}, u32[]{:S(2)}, u32[]{:S(2)}) collective-permute-start(bf16[256,1024]{1,0:T(8,128)(2,1)S(1)} %get-tuple-element.135), channel_id=1, source_target_pairs={{0,1},{1,0},{2,3},{3,2},{4,5},{5,4},{6,7},{7,6},{8,9},{9,8},{10,11... | collective-permute-start | bytes 1572872 | tf_op jit(solution)/shard_map/ppermute | solution.py:31
  30.8 9.4 %collective-permute-start.14 = (bf16[256,640]{1,0:T(8,128)(2,1)S(1)}, bf16[256,640]{1,0:T(8,128)(2,1)S(1)}, u32[]{:S(2)}, u32[]{:S(2)}) collective-permute-start(bf16[256,640]{1,0:T(8,128)(2,1)S(1)} %get-tuple-element.140.normed_two.n), channel_id=1, source_target_pairs={{0,1},{1,0},{2,3},{3,2},{4,5},{5,4},{6,7},{7,6},{8,9},{9,8},{10,11... | collective-permute-start | bytes 983048 | tf_op jit(solution)/shard_map/ppermute | solution.py:31
  31.1 9.6 %collective-permute-start.12 = (bf16[256,1024]{1,0:T(8,128)(2,1)S(1)}, bf16[256,1024]{1,0:T(8,128)(2,1)S(1)}, u32[]{:S(2)}, u32[]{:S(2)}) collective-permute-start(bf16[256,1024]{1,0:T(8,128)(2,1)S(1)} %get-tuple-element.137), channel_id=1, source_target_pairs={{0,1},{1,0},{2,3},{3,2},{4,5},{5,4},{6,7},{7,6},{8,9},{9,8},{10,11... | collective-permute-start | bytes 1572872 | tf_op jit(solution)/shard_map/ppermute | solution.py:31
  31.3 9.8 %collective-permute-start.13 = (bf16[256,1024]{1,0:T(8,128)(2,1)S(1)}, bf16[256,1024]{1,0:T(8,128)(2,1)S(1)}, u32[]{:S(2)}, u32[]{:S(2)}) collective-permute-start(bf16[256,1024]{1,0:T(8,128)(2,1)S(1)} %get-tuple-element.139), channel_id=1, source_target_pairs={{0,1},{1,0},{2,3},{3,2},{4,5},{5,4},{6,7},{7,6},{8,9},{9,8},{10,11... | collective-permute-start | bytes 1572872 | tf_op jit(solution)/shard_map/ppermute | solution.py:31
  31.6 12.4 %collective-permute-start.15 = (bf16[768,640]{1,0:T(8,128)(2,1)S(1)}, bf16[768,640]{1,0:T(8,128)(2,1)S(1)}, u32[]{:S(2)}, u32[]{:S(2)}) collective-permute-start(bf16[768,640]{1,0:T(8,128)(2,1)S(1)} %get-tuple-element.143.n), channel_id=1, source_target_pairs={{0,1},{1,0},{2,3},{3,2},{4,5},{5,4},{6,7},{7,6},{8,9},{9,8},{10,11... | collective-permute-start | bytes 2949128 | tf_op jit(solution)/shard_map/ppermute | solution.py:31
  47.9 10.4 %collective-permute-start.23 = (bf16[1664,128]{1,0:T(8,128)(2,1)S(1)}, bf16[1664,128]{1,0:T(8,128)(2,1)S(1)}, u32[]{:S(2)}, u32[]{:S(2)}) collective-permute-start(bf16[1664,128]{1,0:T(8,128)(2,1)S(1)} %get-tuple-element.157), channel_id=1, source_target_pairs={{0,2},{1,7},{2,0},{3,5},{4,6},{5,3},{6,4},{7,1},{8,10},{9,15},{10,... | collective-permute-start | bytes 1277960 | tf_op jit(solution)/shard_map/ppermute | solution.py:75
  48.9 19.8 %collective-permute-start.19 = (bf16[3840,128]{1,0:T(8,128)(2,1)S(1)}, bf16[3840,128]{1,0:T(8,128)(2,1)S(1)}, u32[]{:S(2)}, u32[]{:S(2)}) collective-permute-start(bf16[3840,128]{1,0:T(8,128)(2,1)S(1)} %get-tuple-element.152), channel_id=1, source_target_pairs={{0,64},{1,17},{2,66},{3,19},{4,68},{5,21},{6,70},{7,23},{8,72},{9,... | collective-permute-start | bytes 2949128 | tf_op jit(solution)/shard_map/ppermute | solution.py:91
  53.4 22.6 %collective-permute-start.20 = (bf16[3840,128]{1,0:T(8,128)(2,1)S(1)}, bf16[3840,128]{1,0:T(8,128)(2,1)S(1)}, u32[]{:S(2)}, u32[]{:S(2)}) collective-permute-start(bf16[3840,128]{1,0:T(8,128)(2,1)S(1)} %get-tuple-element.153), channel_id=1, source_target_pairs={{0,32},{1,9},{2,34},{3,11},{4,36},{5,13},{6,38},{7,15},{8,40},{9,1... | collective-permute-start | bytes 2949128 | tf_op jit(solution)/shard_map/ppermute | solution.py:91
  54.1 22.6 %collective-permute-start.21 = (bf16[3840,128]{1,0:T(8,128)(2,1)S(1)}, bf16[3840,128]{1,0:T(8,128)(2,1)S(1)}, u32[]{:S(2)}, u32[]{:S(2)}) collective-permute-start(bf16[3840,128]{1,0:T(8,128)(2,1)S(1)} %get-tuple-element.154), channel_id=1, source_target_pairs={{0,96},{1,25},{2,98},{3,27},{4,100},{5,29},{6,102},{7,31},{8,104},... | collective-permute-start | bytes 2949128 | tf_op jit(solution)/shard_map/ppermute | solution.py:91
  56.6 12.1 %collective-permute-start.22 = (bf16[1664,128]{1,0:T(8,128)(2,1)S(1)}, bf16[1664,128]{1,0:T(8,128)(2,1)S(1)}, u32[]{:S(2)}, u32[]{:S(2)}) collective-permute-start(bf16[1664,128]{1,0:T(8,128)(2,1)S(1)} %get-tuple-element.155), channel_id=1, source_target_pairs={{0,2},{1,7},{2,0},{3,5},{4,6},{5,3},{6,4},{7,1},{8,10},{9,15},{10,... | collective-permute-start | bytes 1277960 | tf_op jit(solution)/shard_map/ppermute | solution.py:75
  58.5 18.2 %collective-permute-start.24 = (bf16[1664,128]{1,0:T(8,128)(2,1)S(1)}, bf16[1664,128]{1,0:T(8,128)(2,1)S(1)}, u32[]{:S(2)}, u32[]{:S(2)}) collective-permute-start(bf16[1664,128]{1,0:T(8,128)(2,1)S(1)} %add_convert_fusion), channel_id=1, source_target_pairs={{0,6},{1,3},{2,4},{3,1},{4,2},{5,7},{6,0},{7,5},{8,14},{9,11},{10,... | collective-permute-start | bytes 1277960 | tf_op jit(solution)/shard_map/ppermute | solution.py:75
  77.9 9.0 %collective-permute-start.25 = (bf16[1376,128]{1,0:T(8,128)(2,1)S(1)}, bf16[1376,128]{1,0:T(8,128)(2,1)S(1)}, u32[]{:S(2)}, u32[]{:S(2)}) collective-permute-start(bf16[1376,128]{1,0:T(8,128)(2,1)S(1)} %get-tuple-element.159), channel_id=1, source_target_pairs={{0,16},{1,65},{2,18},{3,67},{4,20},{5,69},{6,22},{7,71},{8,24},{9,... | collective-permute-start | bytes 1056776 | tf_op jit(solution)/shard_map/ppermute | solution.py:91
  80.0 10.5 %collective-permute-start.26 = (bf16[1376,128]{1,0:T(8,128)(2,1)S(1)}, bf16[1376,128]{1,0:T(8,128)(2,1)S(1)}, u32[]{:S(2)}, u32[]{:S(2)}) collective-permute-start(bf16[1376,128]{1,0:T(8,128)(2,1)S(1)} %get-tuple-element.160), channel_id=1, source_target_pairs={{0,8},{1,33},{2,10},{3,35},{4,12},{5,37},{6,14},{7,39},{8,16},{9,4... | collective-permute-start | bytes 1056776 | tf_op jit(solution)/shard_map/ppermute | solution.py:91
  80.7 9.9 %collective-permute-start.27 = (bf16[1376,128]{1,0:T(8,128)(2,1)S(1)}, bf16[1376,128]{1,0:T(8,128)(2,1)S(1)}, u32[]{:S(2)}, u32[]{:S(2)}) collective-permute-start(bf16[1376,128]{1,0:T(8,128)(2,1)S(1)} %get-tuple-element.161), channel_id=1, source_target_pairs={{0,24},{1,97},{2,26},{3,99},{4,28},{5,101},{6,30},{7,103},{8,0},{9... | collective-permute-start | bytes 1056776 | tf_op jit(solution)/shard_map/ppermute | solution.py:91
  92.2 8.3 %collective-permute-start.30 = (bf16[960,128]{1,0:T(8,128)(2,1)S(1)}, bf16[960,128]{1,0:T(8,128)(2,1)S(1)}, u32[]{:S(2)}, u32[]{:S(2)}) collective-permute-start(bf16[960,128]{1,0:T(8,128)(2,1)S(1)} %add_convert_fusion.3), channel_id=1, source_target_pairs={{0,2},{1,7},{2,0},{3,5},{4,6},{5,3},{6,4},{7,1},{8,10},{9,15},{10,... | collective-permute-start | bytes 737288 | tf_op jit(solution)/shard_map/ppermute | solution.py:75
  94.0 12.6 %collective-permute-start.29 = (bf16[256,512]{1,0:T(8,128)(2,1)S(1)}, bf16[256,512]{1,0:T(8,128)(2,1)S(1)}, u32[]{:S(2)}, u32[]{:S(2)}) collective-permute-start(bf16[256,512]{1,0:T(8,128)(2,1)S(1)} %get-tuple-element.164), channel_id=1, source_target_pairs={{4,0},{6,2},{8,4},{10,6},{12,8},{14,10},{16,12},{18,14},{20,16},{2... | collective-permute-start | bytes 786440 | tf_op jit(solution)/shard_map/ppermute | solution.py:98
  95.3 15.7 %collective-permute-start.28 = (bf16[256,512]{1,0:T(8,128)(2,1)S(1)}, bf16[256,512]{1,0:T(8,128)(2,1)S(1)}, u32[]{:S(2)}, u32[]{:S(2)}) collective-permute-start(bf16[256,512]{1,0:T(8,128)(2,1)S(1)} %get-tuple-element.162), channel_id=1, source_target_pairs={{2,0},{4,2},{6,4},{8,6},{10,8},{12,10},{14,12},{16,14},{18,16},{20... | collective-permute-start | bytes 786440 | tf_op jit(solution)/shard_map/ppermute | solution.py:98
  100.6 11.8 %collective-permute-start.33 = (bf16[416,128]{1,0:T(8,128)(2,1)S(1)}, bf16[416,128]{1,0:T(8,128)(2,1)S(1)}, u32[]{:S(2)}, u32[]{:S(2)}) collective-permute-start(bf16[416,128]{1,0:T(8,128)(2,1)S(1)} %add_convert_fusion.5), channel_id=1, source_target_pairs={{0,96},{1,25},{2,98},{3,27},{4,100},{5,29},{6,102},{7,31},{8,104},... | collective-permute-start | bytes 319496 | tf_op jit(solution)/shard_map/ppermute | solution.py:83
  105.1 7.6 %collective-permute-start.31 = (bf16[960,128]{1,0:T(8,128)(2,1)S(1)}, bf16[960,128]{1,0:T(8,128)(2,1)S(1)}, u32[]{:S(2)}, u32[]{:S(2)}) collective-permute-start(bf16[960,128]{1,0:T(8,128)(2,1)S(1)} %add_convert_fusion.2), channel_id=1, source_target_pairs={{0,6},{1,3},{2,4},{3,1},{4,2},{5,7},{6,0},{7,5},{8,14},{9,11},{10,... | collective-permute-start | bytes 737288 | tf_op jit(solution)/shard_map/ppermute | solution.py:75
  113.4 8.9 %collective-permute-start.36 = (bf16[1376,128]{1,0:T(8,128)(2,1)S(1)}, bf16[1376,128]{1,0:T(8,128)(2,1)S(1)}, u32[]{:S(2)}, u32[]{:S(2)}) collective-permute-start(bf16[1376,128]{1,0:T(8,128)(2,1)S(1)} %pad_maximum_fusion.own), channel_id=1, source_target_pairs={{0,16},{1,65},{2,18},{3,67},{4,20},{5,69},{6,22},{7,71},{8,24},{9,... | collective-permute-start | bytes 1056776 | tf_op jit(solution)/shard_map/ppermute | solution.py:91
  116.8 9.2 %collective-permute-start.37 = (bf16[1376,128]{1,0:T(8,128)(2,1)S(1)}, bf16[1376,128]{1,0:T(8,128)(2,1)S(1)}, u32[]{:S(2)}, u32[]{:S(2)}) collective-permute-start(bf16[1376,128]{1,0:T(8,128)(2,1)S(1)} %pad_maximum_fusion.own), channel_id=1, source_target_pairs={{0,8},{1,33},{2,10},{3,35},{4,12},{5,37},{6,14},{7,39},{8,16},{9,4... | collective-permute-start | bytes 1056776 | tf_op jit(solution)/shard_map/ppermute | solution.py:91
  117.5 9.1 %collective-permute-start.38 = (bf16[1376,128]{1,0:T(8,128)(2,1)S(1)}, bf16[1376,128]{1,0:T(8,128)(2,1)S(1)}, u32[]{:S(2)}, u32[]{:S(2)}) collective-permute-start(bf16[1376,128]{1,0:T(8,128)(2,1)S(1)} %pad_maximum_fusion.own), channel_id=1, source_target_pairs={{0,24},{1,97},{2,26},{3,99},{4,28},{5,101},{6,30},{7,103},{8,0},{9... | collective-permute-start | bytes 1056776 | tf_op jit(solution)/shard_map/ppermute | solution.py:91
  128.5 15.7 %collective-permute-start.44 = (bf16[3840,128]{1,0:T(8,128)(2,1)S(1)}, bf16[3840,128]{1,0:T(8,128)(2,1)S(1)}, u32[]{:S(2)}, u32[]{:S(2)}) collective-permute-start(bf16[3840,128]{1,0:T(8,128)(2,1)S(1)} %get-tuple-element.176.refs_0_), channel_id=1, source_target_pairs={{0,64},{1,17},{2,66},{3,19},{4,68},{5,21},{6,70},{7,23},{8,72},{9,... | collective-permute-start | bytes 2949128 | tf_op jit(solution)/shard_map/ppermute | solution.py:91
  131.6 23.4 %collective-permute-start.40 = (bf16[3840,128]{1,0:T(8,128)(2,1)S(1)}, bf16[3840,128]{1,0:T(8,128)(2,1)S(1)}, u32[]{:S(2)}, u32[]{:S(2)}) collective-permute-start(bf16[3840,128]{1,0:T(8,128)(2,1)S(1)} %get-tuple-element.176.refs_0_), channel_id=1, source_target_pairs={{0,32},{1,9},{2,34},{3,11},{4,36},{5,13},{6,38},{7,15},{8,40},{9,1... | collective-permute-start | bytes 2949128 | tf_op jit(solution)/shard_map/ppermute | solution.py:91
  131.6 23.4 %collective-permute-start.41 = (bf16[3840,128]{1,0:T(8,128)(2,1)S(1)}, bf16[3840,128]{1,0:T(8,128)(2,1)S(1)}, u32[]{:S(2)}, u32[]{:S(2)}) collective-permute-start(bf16[3840,128]{1,0:T(8,128)(2,1)S(1)} %get-tuple-element.176.refs_0_), channel_id=1, source_target_pairs={{0,96},{1,25},{2,98},{3,27},{4,100},{5,29},{6,102},{7,31},{8,104},... | collective-permute-start | bytes 2949128 | tf_op jit(solution)/shard_map/ppermute | solution.py:91
  134.8 17.8 %collective-permute-start.42 = (bf16[1664,128]{1,0:T(8,128)(2,1)S(1)}, bf16[1664,128]{1,0:T(8,128)(2,1)S(1)}, u32[]{:S(2)}, u32[]{:S(2)}) collective-permute-start(bf16[1664,128]{1,0:T(8,128)(2,1)S(1)} %get-tuple-element.175.refs_1_), channel_id=1, source_target_pairs={{0,4},{1,5},{2,6},{3,7},{4,0},{5,1},{6,2},{7,3},{8,12},{9,13},{10,... | collective-permute-start | bytes 1277960 | tf_op jit(solution)/shard_map/ppermute | solution.py:638
  137.6 17.5 %collective-permute-start.43 = (bf16[1664,128]{1,0:T(8,128)(2,1)S(1)}, bf16[1664,128]{1,0:T(8,128)(2,1)S(1)}, u32[]{:S(2)}, u32[]{:S(2)}) collective-permute-start(bf16[1664,128]{1,0:T(8,128)(2,1)S(1)} %get-tuple-element.175.refs_1_), channel_id=1, source_target_pairs={{0,2},{1,7},{2,4},{3,1},{4,6},{5,3},{6,0},{7,5},{8,10},{9,15},{10,... | collective-permute-start | bytes 1277960 | tf_op jit(solution)/shard_map/ppermute | solution.py:639
  144.2 10.8 %collective-permute-start.45 = (bf16[1664,128]{1,0:T(8,128)(2,1)S(1)}, bf16[1664,128]{1,0:T(8,128)(2,1)S(1)}, u32[]{:S(2)}, u32[]{:S(2)}) collective-permute-start(bf16[1664,128]{1,0:T(8,128)(2,1)S(1)} %get-tuple-element.175.refs_1_), channel_id=1, source_target_pairs={{0,6},{1,3},{2,0},{3,5},{4,2},{5,7},{6,4},{7,1},{8,14},{9,11},{10,... | collective-permute-start | bytes 1277960 | tf_op jit(solution)/shard_map/ppermute | solution.py:650
  (28 other events, 108.5 us)

commit v3 on v2

--- a/solution.py
+++ b/solution.py
@@ -370,8 +370,14 @@
 
 
 def token_grad_body(
-    tok, gain, grad_after, dq_m, dq_o, dkv, back_one, back_two, wq_m, wq_o, wkv, out
-):
+    where, tok, gain, grad_after, dq_m, dq_o, dkv, back_one, back_two, wq_m, wq_o, wkv, small,
+    small_r, out, gain_one_out, gain_two_out,
+):
+    sums = small[...].astype(F32) + small_r[...].astype(F32)
+    for at, target in ((0, gain_one_out), (5, gain_two_out)):
+        whole = jnp.concatenate([sums[at + b : at + b + 1, :] for b in range(5)], axis=1)
+        half = jnp.where(where[0] == 0, whole[:, : D // 2], whole[:, D // 2 :])
+        target[...] = half.reshape(D // 2)
     back = back_one[...].astype(F32) + back_two[...].astype(F32)
     own = (dkv[...].astype(F32) + back).astype(BF16)
     gn = dot_nt(dq_m[...], wq_m[...]) + dot_nt(dq_o[...], wq_o[...]) + dot_nt(own, wkv[...])
@@ -637,25 +643,23 @@
     f_got = to_peers([f_send] * 3, shift_first)
     a_two = lax.ppermute(a_send, everywhere, shift_y(2))
     a_one = lax.ppermute(a_send, everywhere, shift_apart(1))
-    grad_tokens = call(
-        "token_grad", token_grad_body, [((rows, D), F32)],
-        [
-            tok, gain_one, grad_after, dq_m, dq_o, dkv, back_one, back_two, w_query, query_other,
-            wkv,
-        ],
-        us=2,
-    )[0]
+    grad_tokens, g_gain_one, g_gain_two = call(
+        "token_grad", token_grad_body, [((rows, D), F32), ((half_d,), F32), ((half_d,), F32)],
+        [
+            where, tok, gain_one, grad_after, dq_m, dq_o, dkv, back_one, back_two, w_query,
+            query_other, wkv, small, small_r,
+        ],
+        us=2, scalars=1,
+    )
 
     shards = spread(where, [after(f_whole, grad_tokens)], (0,), [a_whole], ((0, 0),), [])
     a_other = lax.ppermute(after(a_send, f_got[0]), everywhere, shift_apart(-1))
-    shards = spread(where, f_got[:1], (2,), [], (), shards)
+    shards = spread(where, f_got[:1], (2,), [a_two], ((2, 0),), shards)
     g_gate, g_up, g_down, g_query, g_key, g_value, g_out = spread(
-        where, f_got[1:], (3, 1), [a_two, a_one, a_other], ((2, 0), (3, -2), (1, 2)), shards
-    )
-    g_gains = (after(small, g_key).astype(F32) + small_r.astype(F32))[:10].reshape(2, D)
-    g_gains = jnp.where(even, g_gains[:, :half_d], g_gains[:, half_d:])
+        where, f_got[1:], (3, 1), [a_one, a_other], ((3, -2), (1, 2)), shards
+    )
     return (
-        out[None], grad_tokens[None], g_gains[0], g_query, g_key, g_value, g_out, g_gains[1],
+        out[None], grad_tokens[None], g_gain_one, g_query, g_key, g_value, g_out, g_gain_two,
         g_gate, g_up, g_down,
     )
 

time: 161 us -> 160 us (level)
  no operation moved by 1% of the time
where the time goes in v3:
time: 160 us; the launch traced here: 158 us
  starting transfers between devices  59 us (37%)
  waiting for transfers between devices  54.6 us (34%)
  Pallas kernels  34.6 us (22%)
  local copies, waits for them, and re-layouts  5.16 us (3%)
  other arithmetic  3.76 us (2%)
    ppermute x12, waiting for transfers between devices, to_peers(): lax.ppermute(part, ('ctx', 'fsdp'), shift(by))  28.6 us
    pallas_call x10, Pallas kernels, call(): pl.pallas_call(body, out_shape=shapes, in_specs=[smem] * scalars + [whole...  27.1 us
    ppermute x12, starting transfers between devices, to_peers(): lax.ppermute(part, ('ctx', 'fsdp'), shift(by))  26 us
    ppermute x5, waiting for transfers between devices, swap_y(): lax.ppermute(v, ('ctx', 'fsdp'), chip_pairs(lambda x, z, y, c: (x, z, (pa...  12.5 us
    ppermute x4, starting transfers between devices, passed_along(): return lax.ppermute(shard, 'ctx', pairs)  10.4 us
    pallas_call x3, Pallas kernels, spread(): pl.pallas_call(functools.partial(spread_body, f_places, a_places, not sha...  7.51 us
    ppermute x5, starting transfers between devices, swap_y(): lax.ppermute(v, ('ctx', 'fsdp'), chip_pairs(lambda x, z, y, c: (x, z, (pa...  6.43 us
    ppermute x20, waiting for transfers between devices, swap(): return lax.ppermute(x, 'fsdp', [(0, 1), (1, 0)])  5.99 us
  transfers between devices with their start and end apart: 46, of which 20 were waited for; matrix products, arithmetic and copies ran while one was open for 2% of the time, Pallas kernels for 14%

profile of v3, /device:TPU:0, one launch (start us, length us, event | category | flops | bytes accessed | tf_op | source)
XLA Modules:
  0.0 158.4 jit_solution(7268609692443809690)
XLA Ops:
  0.6 5.2 %collective-permute-start = (bf16[256,640]{1,0:T(8,128)(2,1)}, bf16[256,640]{1,0:T(8,128)(2,1)S(1)}, u32[]{:S(2)}, u32[]{:S(2)}) collective-permute-start(bf16[256,640]{1,0:T(8,128)(2,1)} %bitcast.13), channel_id=1, source_target_pairs={{0,4},{2,6},{4,8},{6,10},{8,12},{10,14},{12,16},{14,18},{16,20},{1... | collective-permute-start | bytes 983048 | tf_op jit(solution)/shard_map/ppermute | solution.py:98
  5.9 2.6 %collective-permute-start.1 = (bf16[256,640]{1,0:T(8,128)(2,1)}, bf16[256,640]{1,0:T(8,128)(2,1)S(1)}, u32[]{:S(2)}, u32[]{:S(2)}) collective-permute-start(bf16[256,640]{1,0:T(8,128)(2,1)} %bitcast.14), channel_id=1, source_target_pairs={{0,2},{2,4},{4,6},{6,8},{8,10},{10,12},{12,14},{14,16},{16,18},{18... | collective-permute-start | bytes 983048 | tf_op jit(solution)/shard_map/ppermute | solution.py:98
  23.0 3.4 %attend.1 = (bf16[768,640]{1,0:T(8,128)(2,1)S(1)}, bf16[256,1024]{1,0:T(8,128)(2,1)S(1)}, bf16[768,512]{1,0:T(8,128)(2,1)S(1)}, bf16[256,512]{1,0:T(8,128)(2,1)S...) custom-call(bf16[256,640]{1,0:T(8,128)(2,1)S(1)} %collective-permute, ...), custom_call_target="tpu_custom_call" | custom-call | flops 5500000256 | bytes 1024 | tf_op jit(solution)/shard_map/attend/pallas_call | solution.py:118
  27.4 3.1 %ffn_other.1 = (bf16[256,1024]{1,0:T(8,128)(2,1)S(1)}, bf16[256,1024]{1,0:T(8,128)(2,1)S(1)}, bf16[256,1024]{1,0:T(8,128)(2,1)S(1)}, f32[256,640]{1,0:T(8,128)S(1)}, f32[256,640]{1,0:T(8,128)S(1)}) custom-call(bf16[256,640]{1,0:T(8,128)(2,1)S(1)} %get-tuple-element.142.normed_two.n, bf16[256,640]{1,0:T(8,128)(2,1)S(1)} %bitcast.10, ...), custom_call_target="tpu_custom_call" | custom-call | flops 5500000256 | bytes 1024 | tf_op jit(solution)/shard_map/ffn_other/pallas_call | solution.py:118
  31.8 4.2 %ffn.1 = (bf16[256,640]{1,0:T(8,128)(2,1)}, bf16[256,1024]{1,0:T(8,128)(2,1)S(1)}, bf16[256,1024]{1,0:T(8,128)(2,1)S(1)}, bf16[256,1024]{1,0:T(8,128)(2,1)S(1)},...) custom-call(f32[256,640]{1,0:T(8,128)S(1)} %get-tuple-element.117.after, ...), custom_call_target="tpu_custom_call" | custom-call | flops 4400000000 | bytes 1024 | tf_op jit(solution)/shard_map/ffn/pallas_call | solution.py:118
  35.9 4.2 %attend_grad.1 = (bf16[256,512]{1,0:T(8,128)(2,1)S(1)}, bf16[256,512]{1,0:T(8,128)(2,1)S(1)}, bf16[256,512]{1,0:T(8,128)(2,1)S(1)}, bf16[256,512]{1,0:T(8,128)(2...) custom-call(s32[4]{0:T(128)S(1)} %pad_add_fusion.where, ...), custom_call_target="tpu_custom_call" | custom-call | bytes 1024 | tf_op jit(solution)/shard_map/attend_grad/pallas_call | solution.py:118
  41.1 2.9 %ffn_grads.1 = (bf16[3840,128]{1,0:T(8,128)(2,1)S(1)}, bf16[3840,128]{1,0:T(8,128)(2,1)S(1)}, bf16[3840,128]{1,0:T(8,128)(2,1)S(1)}, bf16[3840,128]{1,0:T(8,128)(2,1)S(1)}) custom-call(s32[4]{0:T(128)S(1)} %pad_add_fusion.where, bf16[256,1024]{1,0:T(8,128)(2,1)S(1)} %get-tuple-element.136.hid_m, bf16[256,1024]{1,0:T(8,128)(2,1)S(1)} %collective-permute-done.11.hid_r, ...), custom_call_target="tpu_custom_call" | custom-call | flops 3300000000 | bytes 1024 | tf_op jit(solution)/shard_map/ffn_grads/pallas_call | solution.py:118
  44.1 3.8 %attend_grads.1 = (bf16[1664,128]{1,0:T(8,128)(2,1)S(1)}, bf16[1664,128]{1,0:T(8,128)(2,1)S(1)}, bf16[1664,128]{1,0:T(8,128)(2,1)S(1)}, bf16[1664,128]{1,0:T(8,128)(2,1)S(1)}) custom-call(s32[4]{0:T(128)S(1)} %pad_add_fusion.where, bf16[768,640]{1,0:T(8,128)(2,1)S(1)} %get-tuple-element.145.n, bf16[768,640]{1,0:T(8,128)(2,1)S(1)} %collective-permute-done.15.n_r, ...), custom_call_target="tpu_custom_call" | custom-call | bytes 1024 | tf_op jit(solution)/shard_map/attend_grads/pallas_call | solution.py:118
  48.9 4.5 %collective-permute-start.19 = (bf16[3840,128]{1,0:T(8,128)(2,1)S(1)}, bf16[3840,128]{1,0:T(8,128)(2,1)S(1)}, u32[]{:S(2)}, u32[]{:S(2)}) collective-permute-start(bf16[3840,128]{1,0:T(8,128)(2,1)S(1)} %get-tuple-element.154), channel_id=1, source_target_pairs={{0,64},{1,17},{2,66},{3,19},{4,68},{5,21},{6,70},{7,23},{8,72},{9,... | collective-permute-start | bytes 2949128 | tf_op jit(solution)/shard_map/ppermute | solution.py:91
  54.1 2.6 %collective-permute-start.21 = (bf16[3840,128]{1,0:T(8,128)(2,1)S(1)}, bf16[3840,128]{1,0:T(8,128)(2,1)S(1)}, u32[]{:S(2)}, u32[]{:S(2)}) collective-permute-start(bf16[3840,128]{1,0:T(8,128)(2,1)S(1)} %get-tuple-element.156), channel_id=1, source_target_pairs={{0,96},{1,25},{2,98},{3,27},{4,100},{5,29},{6,102},{7,31},{8,104},... | collective-permute-start | bytes 2949128 | tf_op jit(solution)/shard_map/ppermute | solution.py:91
  60.4 8.4 %collective-permute-done.22.a_one = bf16[1664,128]{1,0:T(8,128)(2,1)S(1)} collective-permute-done((bf16[1664,128]{1,0:T(8,128)(2,1)S(1)}, bf16[1664,128]{1,0:T(8,128)(2,1)S(1)}, u32[]{:S(2)}, u32[]{:S(2)}) %collective-permute-start.22) | collective-permute-done | bytes 426016 | tf_op jit(solution)/shard_map/ppermute | solution.py:75
  68.7 7.3 %collective-permute-done.20.r_one = bf16[3840,128]{1,0:T(8,128)(2,1)S(1)} collective-permute-done((bf16[3840,128]{1,0:T(8,128)(2,1)S(1)}, bf16[3840,128]{1,0:T(8,128)(2,1)S(1)}, u32[]{:S(2)}, u32[]{:S(2)}) %collective-permute-start.20) | collective-permute-done | bytes 983072 | tf_op jit(solution)/shard_map/ppermute | solution.py:91
  77.9 2.2 %collective-permute-start.25 = (bf16[1376,128]{1,0:T(8,128)(2,1)S(1)}, bf16[1376,128]{1,0:T(8,128)(2,1)S(1)}, u32[]{:S(2)}, u32[]{:S(2)}) collective-permute-start(bf16[1376,128]{1,0:T(8,128)(2,1)S(1)} %get-tuple-element.161), channel_id=1, source_target_pairs={{0,16},{1,65},{2,18},{3,67},{4,20},{5,69},{6,22},{7,71},{8,24},{9,... | collective-permute-start | bytes 1056776 | tf_op jit(solution)/shard_map/ppermute | solution.py:91
  80.7 2.6 %collective-permute-start.27 = (bf16[1376,128]{1,0:T(8,128)(2,1)S(1)}, bf16[1376,128]{1,0:T(8,128)(2,1)S(1)}, u32[]{:S(2)}, u32[]{:S(2)}) collective-permute-start(bf16[1376,128]{1,0:T(8,128)(2,1)S(1)} %get-tuple-element.163), channel_id=1, source_target_pairs={{0,24},{1,97},{2,26},{3,99},{4,28},{5,101},{6,30},{7,103},{8,0},{9... | collective-permute-start | bytes 1056776 | tf_op jit(solution)/shard_map/ppermute | solution.py:91
  83.3 3.6 %collective-permute-done.25 = bf16[1376,128]{1,0:T(8,128)(2,1)S(1)} collective-permute-done((bf16[1376,128]{1,0:T(8,128)(2,1)S(1)}, bf16[1376,128]{1,0:T(8,128)(2,1)S(1)}, u32[]{:S(2)}, u32[]{:S(2)}) %collective-permute-start.25) | collective-permute-done | bytes 352288 | tf_op jit(solution)/shard_map/ppermute | solution.py:91
  86.9 3.7 %collective-permute-done.26 = bf16[1376,128]{1,0:T(8,128)(2,1)S(1)} collective-permute-done((bf16[1376,128]{1,0:T(8,128)(2,1)S(1)}, bf16[1376,128]{1,0:T(8,128)(2,1)S(1)}, u32[]{:S(2)}, u32[]{:S(2)}) %collective-permute-start.26) | collective-permute-done | bytes 352288 | tf_op jit(solution)/shard_map/ppermute | solution.py:91
  96.7 3.9 %collective-permute-done.30 = bf16[960,128]{1,0:T(8,128)(2,1)S(1)} collective-permute-done((bf16[960,128]{1,0:T(8,128)(2,1)S(1)}, bf16[960,128]{1,0:T(8,128)(2,1)S(1)}, u32[]{:S(2)}, u32[]{:S(2)}) %collective-permute-start.30) | collective-permute-done | bytes 245792 | tf_op jit(solution)/shard_map/ppermute | solution.py:75
  100.6 4.4 %collective-permute-start.33 = (bf16[416,128]{1,0:T(8,128)(2,1)S(1)}, bf16[416,128]{1,0:T(8,128)(2,1)S(1)}, u32[]{:S(2)}, u32[]{:S(2)}) collective-permute-start(bf16[416,128]{1,0:T(8,128)(2,1)S(1)} %add_convert_fusion.5), channel_id=1, source_target_pairs={{0,96},{1,25},{2,98},{3,27},{4,100},{5,29},{6,102},{7,31},{8,104},... | collective-permute-start | bytes 319496 | tf_op jit(solution)/shard_map/ppermute | solution.py:83
  106.6 4.4 %collective-permute-done.28.back_one = bf16[256,512]{1,0:T(8,128)(2,1)S(1)} collective-permute-done((bf16[256,512]{1,0:T(8,128)(2,1)S(1)}, bf16[256,512]{1,0:T(8,128)(2,1)S(1)}, u32[]{:S(2)}, u32[]{:S(2)}) %collective-permute-start.28) | collective-permute-done | bytes 262176 | tf_op jit(solution)/shard_map/ppermute | solution.py:98
  113.4 3.4 %collective-permute-start.36 = (bf16[1376,128]{1,0:T(8,128)(2,1)S(1)}, bf16[1376,128]{1,0:T(8,128)(2,1)S(1)}, u32[]{:S(2)}, u32[]{:S(2)}) collective-permute-start(bf16[1376,128]{1,0:T(8,128)(2,1)S(1)} %pad_maximum_fusion.own), channel_id=1, source_target_pairs={{0,16},{1,65},{2,18},{3,67},{4,20},{5,69},{6,22},{7,71},{8,24},{9,... | collective-permute-start | bytes 1056776 | tf_op jit(solution)/shard_map/ppermute | solution.py:91
  117.5 2.5 %collective-permute-start.38 = (bf16[1376,128]{1,0:T(8,128)(2,1)S(1)}, bf16[1376,128]{1,0:T(8,128)(2,1)S(1)}, u32[]{:S(2)}, u32[]{:S(2)}) collective-permute-start(bf16[1376,128]{1,0:T(8,128)(2,1)S(1)} %pad_maximum_fusion.own), channel_id=1, source_target_pairs={{0,24},{1,97},{2,26},{3,99},{4,28},{5,101},{6,30},{7,103},{8,0},{9... | collective-permute-start | bytes 1056776 | tf_op jit(solution)/shard_map/ppermute | solution.py:91
  120.0 2.3 %collective-permute-done.36.r_two = bf16[1376,128]{1,0:T(8,128)(2,1)S(1)} collective-permute-done((bf16[1376,128]{1,0:T(8,128)(2,1)S(1)}, bf16[1376,128]{1,0:T(8,128)(2,1)S(1)}, u32[]{:S(2)}, u32[]{:S(2)}) %collective-permute-start.36) | collective-permute-done | bytes 352288 | tf_op jit(solution)/shard_map/ppermute | solution.py:91
  122.3 3.7 %collective-permute-done.37.r_one = bf16[1376,128]{1,0:T(8,128)(2,1)S(1)} collective-permute-done((bf16[1376,128]{1,0:T(8,128)(2,1)S(1)}, bf16[1376,128]{1,0:T(8,128)(2,1)S(1)}, u32[]{:S(2)}, u32[]{:S(2)}) %collective-permute-start.37) | collective-permute-done | bytes 352288 | tf_op jit(solution)/shard_map/ppermute | solution.py:91
  128.5 3.1 %collective-permute-start.43 = (bf16[3840,128]{1,0:T(8,128)(2,1)S(1)}, bf16[3840,128]{1,0:T(8,128)(2,1)S(1)}, u32[]{:S(2)}, u32[]{:S(2)}) collective-permute-start(bf16[3840,128]{1,0:T(8,128)(2,1)S(1)} %get-tuple-element.180.refs_0_), channel_id=1, source_target_pairs={{0,64},{1,17},{2,66},{3,19},{4,68},{5,21},{6,70},{7,23},{8,72},{9,... | collective-permute-start | bytes 2949128 | tf_op jit(solution)/shard_map/ppermute | solution.py:91
  131.6 3.2 %collective-permute-start.41 = (bf16[3840,128]{1,0:T(8,128)(2,1)S(1)}, bf16[3840,128]{1,0:T(8,128)(2,1)S(1)}, u32[]{:S(2)}, u32[]{:S(2)}) collective-permute-start(bf16[3840,128]{1,0:T(8,128)(2,1)S(1)} %get-tuple-element.180.refs_0_), channel_id=1, source_target_pairs={{0,96},{1,25},{2,98},{3,27},{4,100},{5,29},{6,102},{7,31},{8,104},... | collective-permute-start | bytes 2949128 | tf_op jit(solution)/shard_map/ppermute | solution.py:91
  134.8 2.7 %collective-permute-start.45 = (bf16[1664,128]{1,0:T(8,128)(2,1)S(1)}, bf16[1664,128]{1,0:T(8,128)(2,1)S(1)}, u32[]{:S(2)}, u32[]{:S(2)}) collective-permute-start(bf16[1664,128]{1,0:T(8,128)(2,1)S(1)} %get-tuple-element.179.refs_1_), channel_id=1, source_target_pairs={{0,4},{1,5},{2,6},{3,7},{4,0},{5,1},{6,2},{7,3},{8,12},{9,13},{10,... | collective-permute-start | bytes 1277960 | tf_op jit(solution)/shard_map/ppermute | solution.py:644
  137.6 6.7 %collective-permute-done.43.refs_0_ = bf16[3840,128]{1,0:T(8,128)(2,1)S(1)} collective-permute-done((bf16[3840,128]{1,0:T(8,128)(2,1)S(1)}, bf16[3840,128]{1,0:T(8,128)(2,1)S(1)}, u32[]{:S(2)}, u32[]{:S(2)}) %collective-permute-start.43) | collective-permute-done | bytes 983072 | tf_op jit(solution)/shard_map/ppermute | solution.py:91
  144.2 2.5 %collective-permute-start.44 = (bf16[1664,128]{1,0:T(8,128)(2,1)S(1)}, bf16[1664,128]{1,0:T(8,128)(2,1)S(1)}, u32[]{:S(2)}, u32[]{:S(2)}) collective-permute-start(bf16[1664,128]{1,0:T(8,128)(2,1)S(1)} %get-tuple-element.179.refs_1_), channel_id=1, source_target_pairs={{0,6},{1,3},{2,0},{3,5},{4,2},{5,7},{6,4},{7,1},{8,14},{9,11},{10,... | collective-permute-start | bytes 1277960 | tf_op jit(solution)/shard_map/ppermute | solution.py:656
  146.7 2.3 %token_grad.1 = (f32[256,640]{1,0:T(8,128)}, f32[320]{0:T(512)}, f32[320]{0:T(512)}) custom-call(s32[4]{0:T(128)S(1)} %pad_add_fusion.where, bf16[256,640]{1,0:T(8,128)(2,1)S(1)} %bitcast.16, f32[1,640]{1,0:T(1,128)S(1)} %maximum_convert_fusion.1.gain, f32[256,640]{1,0:T(8,128)S(1)} %get-tuple-element.125.grad_after, ...), custom_call_target="tpu_custom_call" | custom-call | flops 2200000000 | bytes 1024 | tf_op jit(solution)/shard_map/token_grad/pallas_call | solution.py:118
  149.1 2.2 %spread.3 = (f32[640,1024]{1,0:T(8,128)}, f32[640,1024]{1,0:T(8,128)}, f32[1024,640]{1,0:T(8,128)}, f32[640,512]{1,0:T(8,128)}, f32[640,128]{1,0:T(8,128)}, /*index=5*/f32[640,128]{1,0:T(8,128)}, f32[512,640]{1,0:T(8,128)}) custom-call(s32[4]{0:T(128)S(1)} %pad_add_fusion.where, bf16[3840,128]{1,0:T(8,128)(2,1)S(1)} %get-tuple-element.180.refs_0_, ...), custom_call_target="tpu_custom_call" | custom-call | flops 1024 | bytes 1024 | tf_op jit(solution)/shard_map/spread/pallas_call | solution.py:483
  151.3 2.2 %spread.4 = (f32[640,1024]{1,0:T(8,128)}, f32[640,1024]{1,0:T(8,128)}, f32[1024,640]{1,0:T(8,128)}, f32[640,512]{1,0:T(8,128)}, f32[640,128]{1,0:T(8,128)}, /*index=5*/f32[640,128]{1,0:T(8,128)}, f32[512,640]{1,0:T(8,128)}) custom-call(s32[4]{0:T(128)S(1)} %pad_add_fusion.where, ...), custom_call_target="tpu_custom_call", output_to_operand_aliasing={{0}: (3, {}), {1}: (4, {}), {2}: (5, {}), {3}: (6, {}), {4}... | custom-call | flops 1024 | bytes 1024 | tf_op jit(solution)/shard_map/spread/pallas_call | solution.py:483
  155.0 3.1 %spread.5 = (f32[640,1024]{1,0:T(8,128)}, f32[640,1024]{1,0:T(8,128)}, f32[1024,640]{1,0:T(8,128)}, f32[640,512]{1,0:T(8,128)}, f32[640,128]{1,0:T(8,128)}, /*index=5*/f32[640,128]{1,0:T(8,128)}, f32[512,640]{1,0:T(8,128)}) custom-call(s32[4]{0:T(128)S(1)} %pad_add_fusion.where, ...), custom_call_target="tpu_custom_call", output_to_operand_aliasing={{0}: (5, {}), {1}: (6, {}), {2}: (7, {}), {3}: (8, {}), {4}... | custom-call | flops 1024 | bytes 1024 | tf_op jit(solution)/shard_map/spread/pallas_call | solution.py:483
  (120 shorter events, 40.3 us)
Async XLA Ops:
  0.6 21.7 %collective-permute-start = (bf16[256,640]{1,0:T(8,128)(2,1)}, bf16[256,640]{1,0:T(8,128)(2,1)S(1)}, u32[]{:S(2)}, u32[]{:S(2)}) collective-permute-start(bf16[256,640]{1,0:T(8,128)(2,1)} %bitcast.13), channel_id=1, source_target_pairs={{0,4},{2,6},{4,8},{6,10},{8,12},{10,14},{12,16},{14,18},{16,20},{1... | collective-permute-start | bytes 983048 | tf_op jit(solution)/shard_map/ppermute | solution.py:98
  5.9 16.5 %collective-permute-start.1 = (bf16[256,640]{1,0:T(8,128)(2,1)}, bf16[256,640]{1,0:T(8,128)(2,1)S(1)}, u32[]{:S(2)}, u32[]{:S(2)}) collective-permute-start(bf16[256,640]{1,0:T(8,128)(2,1)} %bitcast.14), channel_id=1, source_target_pairs={{0,2},{2,4},{4,6},{6,8},{8,10},{10,12},{12,14},{14,16},{16,18},{18... | collective-permute-start | bytes 983048 | tf_op jit(solution)/shard_map/ppermute | solution.py:98
  13.1 9.3 %collective-permute-start.8 = (bf16[256,640]{1,0:T(8,128)(2,1)}, bf16[256,640]{1,0:T(8,128)(2,1)S(1)}, u32[]{:S(2)}, u32[]{:S(2)}) collective-permute-start(bf16[256,640]{1,0:T(8,128)(2,1)} %bitcast.9), channel_id=1, source_target_pairs={{0,1},{1,0},{2,3},{3,2},{4,5},{5,4},{6,7},{7,6},{8,9},{9,8},{10,11... | collective-permute-start | bytes 983048 | tf_op jit(solution)/shard_map/ppermute | solution.py:31
  15.6 7.4 %collective-permute-start.7 = (bf16[640,1024]{1,0:T(8,128)(2,1)}, bf16[640,1024]{1,0:T(8,128)(2,1)S(1)}, u32[]{:S(2)}, u32[]{:S(2)}) collective-permute-start(bf16[640,1024]{1,0:T(8,128)(2,1)} %wg.1), channel_id=1, source_target_pairs={{0,1},{1,0},{2,3},{3,2},{4,5},{5,4},{6,7},{7,6},{8,9},{9,8},{10,11... | collective-permute-start | bytes 3932168 | tf_op jit(solution)/shard_map/ppermute | solution.py:31
  30.5 10.0 %collective-permute-start.11 = (bf16[256,1024]{1,0:T(8,128)(2,1)S(1)}, bf16[256,1024]{1,0:T(8,128)(2,1)S(1)}, u32[]{:S(2)}, u32[]{:S(2)}) collective-permute-start(bf16[256,1024]{1,0:T(8,128)(2,1)S(1)} %get-tuple-element.137), channel_id=1, source_target_pairs={{0,1},{1,0},{2,3},{3,2},{4,5},{5,4},{6,7},{7,6},{8,9},{9,8},{10,11... | collective-permute-start | bytes 1572872 | tf_op jit(solution)/shard_map/ppermute | solution.py:31
  30.8 9.4 %collective-permute-start.14 = (bf16[256,640]{1,0:T(8,128)(2,1)S(1)}, bf16[256,640]{1,0:T(8,128)(2,1)S(1)}, u32[]{:S(2)}, u32[]{:S(2)}) collective-permute-start(bf16[256,640]{1,0:T(8,128)(2,1)S(1)} %get-tuple-element.142.normed_two.n), channel_id=1, source_target_pairs={{0,1},{1,0},{2,3},{3,2},{4,5},{5,4},{6,7},{7,6},{8,9},{9,8},{10,11... | collective-permute-start | bytes 983048 | tf_op jit(solution)/shard_map/ppermute | solution.py:31
  31.1 9.6 %collective-permute-start.12 = (bf16[256,1024]{1,0:T(8,128)(2,1)S(1)}, bf16[256,1024]{1,0:T(8,128)(2,1)S(1)}, u32[]{:S(2)}, u32[]{:S(2)}) collective-permute-start(bf16[256,1024]{1,0:T(8,128)(2,1)S(1)} %get-tuple-element.139), channel_id=1, source_target_pairs={{0,1},{1,0},{2,3},{3,2},{4,5},{5,4},{6,7},{7,6},{8,9},{9,8},{10,11... | collective-permute-start | bytes 1572872 | tf_op jit(solution)/shard_map/ppermute | solution.py:31
  31.3 9.8 %collective-permute-start.13 = (bf16[256,1024]{1,0:T(8,128)(2,1)S(1)}, bf16[256,1024]{1,0:T(8,128)(2,1)S(1)}, u32[]{:S(2)}, u32[]{:S(2)}) collective-permute-start(bf16[256,1024]{1,0:T(8,128)(2,1)S(1)} %get-tuple-element.141), channel_id=1, source_target_pairs={{0,1},{1,0},{2,3},{3,2},{4,5},{5,4},{6,7},{7,6},{8,9},{9,8},{10,11... | collective-permute-start | bytes 1572872 | tf_op jit(solution)/shard_map/ppermute | solution.py:31
  31.6 12.4 %collective-permute-start.15 = (bf16[768,640]{1,0:T(8,128)(2,1)S(1)}, bf16[768,640]{1,0:T(8,128)(2,1)S(1)}, u32[]{:S(2)}, u32[]{:S(2)}) collective-permute-start(bf16[768,640]{1,0:T(8,128)(2,1)S(1)} %get-tuple-element.145.n), channel_id=1, source_target_pairs={{0,1},{1,0},{2,3},{3,2},{4,5},{5,4},{6,7},{7,6},{8,9},{9,8},{10,11... | collective-permute-start | bytes 2949128 | tf_op jit(solution)/shard_map/ppermute | solution.py:31
  47.9 10.4 %collective-permute-start.23 = (bf16[1664,128]{1,0:T(8,128)(2,1)S(1)}, bf16[1664,128]{1,0:T(8,128)(2,1)S(1)}, u32[]{:S(2)}, u32[]{:S(2)}) collective-permute-start(bf16[1664,128]{1,0:T(8,128)(2,1)S(1)} %get-tuple-element.159), channel_id=1, source_target_pairs={{0,2},{1,7},{2,0},{3,5},{4,6},{5,3},{6,4},{7,1},{8,10},{9,15},{10,... | collective-permute-start | bytes 1277960 | tf_op jit(solution)/shard_map/ppermute | solution.py:75
  48.9 19.8 %collective-permute-start.19 = (bf16[3840,128]{1,0:T(8,128)(2,1)S(1)}, bf16[3840,128]{1,0:T(8,128)(2,1)S(1)}, u32[]{:S(2)}, u32[]{:S(2)}) collective-permute-start(bf16[3840,128]{1,0:T(8,128)(2,1)S(1)} %get-tuple-element.154), channel_id=1, source_target_pairs={{0,64},{1,17},{2,66},{3,19},{4,68},{5,21},{6,70},{7,23},{8,72},{9,... | collective-permute-start | bytes 2949128 | tf_op jit(solution)/shard_map/ppermute | solution.py:91
  53.4 22.6 %collective-permute-start.20 = (bf16[3840,128]{1,0:T(8,128)(2,1)S(1)}, bf16[3840,128]{1,0:T(8,128)(2,1)S(1)}, u32[]{:S(2)}, u32[]{:S(2)}) collective-permute-start(bf16[3840,128]{1,0:T(8,128)(2,1)S(1)} %get-tuple-element.155), channel_id=1, source_target_pairs={{0,32},{1,9},{2,34},{3,11},{4,36},{5,13},{6,38},{7,15},{8,40},{9,1... | collective-permute-start | bytes 2949128 | tf_op jit(solution)/shard_map/ppermute | solution.py:91
  54.1 22.6 %collective-permute-start.21 = (bf16[3840,128]{1,0:T(8,128)(2,1)S(1)}, bf16[3840,128]{1,0:T(8,128)(2,1)S(1)}, u32[]{:S(2)}, u32[]{:S(2)}) collective-permute-start(bf16[3840,128]{1,0:T(8,128)(2,1)S(1)} %get-tuple-element.156), channel_id=1, source_target_pairs={{0,96},{1,25},{2,98},{3,27},{4,100},{5,29},{6,102},{7,31},{8,104},... | collective-permute-start | bytes 2949128 | tf_op jit(solution)/shard_map/ppermute | solution.py:91
  56.6 12.1 %collective-permute-start.22 = (bf16[1664,128]{1,0:T(8,128)(2,1)S(1)}, bf16[1664,128]{1,0:T(8,128)(2,1)S(1)}, u32[]{:S(2)}, u32[]{:S(2)}) collective-permute-start(bf16[1664,128]{1,0:T(8,128)(2,1)S(1)} %get-tuple-element.157), channel_id=1, source_target_pairs={{0,2},{1,7},{2,0},{3,5},{4,6},{5,3},{6,4},{7,1},{8,10},{9,15},{10,... | collective-permute-start | bytes 1277960 | tf_op jit(solution)/shard_map/ppermute | solution.py:75
  58.5 18.2 %collective-permute-start.24 = (bf16[1664,128]{1,0:T(8,128)(2,1)S(1)}, bf16[1664,128]{1,0:T(8,128)(2,1)S(1)}, u32[]{:S(2)}, u32[]{:S(2)}) collective-permute-start(bf16[1664,128]{1,0:T(8,128)(2,1)S(1)} %add_convert_fusion), channel_id=1, source_target_pairs={{0,6},{1,3},{2,4},{3,1},{4,2},{5,7},{6,0},{7,5},{8,14},{9,11},{10,... | collective-permute-start | bytes 1277960 | tf_op jit(solution)/shard_map/ppermute | solution.py:75
  77.9 9.0 %collective-permute-start.25 = (bf16[1376,128]{1,0:T(8,128)(2,1)S(1)}, bf16[1376,128]{1,0:T(8,128)(2,1)S(1)}, u32[]{:S(2)}, u32[]{:S(2)}) collective-permute-start(bf16[1376,128]{1,0:T(8,128)(2,1)S(1)} %get-tuple-element.161), channel_id=1, source_target_pairs={{0,16},{1,65},{2,18},{3,67},{4,20},{5,69},{6,22},{7,71},{8,24},{9,... | collective-permute-start | bytes 1056776 | tf_op jit(solution)/shard_map/ppermute | solution.py:91
  80.0 10.5 %collective-permute-start.26 = (bf16[1376,128]{1,0:T(8,128)(2,1)S(1)}, bf16[1376,128]{1,0:T(8,128)(2,1)S(1)}, u32[]{:S(2)}, u32[]{:S(2)}) collective-permute-start(bf16[1376,128]{1,0:T(8,128)(2,1)S(1)} %get-tuple-element.162), channel_id=1, source_target_pairs={{0,8},{1,33},{2,10},{3,35},{4,12},{5,37},{6,14},{7,39},{8,16},{9,4... | collective-permute-start | bytes 1056776 | tf_op jit(solution)/shard_map/ppermute | solution.py:91
  80.7 9.9 %collective-permute-start.27 = (bf16[1376,128]{1,0:T(8,128)(2,1)S(1)}, bf16[1376,128]{1,0:T(8,128)(2,1)S(1)}, u32[]{:S(2)}, u32[]{:S(2)}) collective-permute-start(bf16[1376,128]{1,0:T(8,128)(2,1)S(1)} %get-tuple-element.163), channel_id=1, source_target_pairs={{0,24},{1,97},{2,26},{3,99},{4,28},{5,101},{6,30},{7,103},{8,0},{9... | collective-permute-start | bytes 1056776 | tf_op jit(solution)/shard_map/ppermute | solution.py:91
  92.2 8.3 %collective-permute-start.30 = (bf16[960,128]{1,0:T(8,128)(2,1)S(1)}, bf16[960,128]{1,0:T(8,128)(2,1)S(1)}, u32[]{:S(2)}, u32[]{:S(2)}) collective-permute-start(bf16[960,128]{1,0:T(8,128)(2,1)S(1)} %add_convert_fusion.3), channel_id=1, source_target_pairs={{0,2},{1,7},{2,0},{3,5},{4,6},{5,3},{6,4},{7,1},{8,10},{9,15},{10,... | collective-permute-start | bytes 737288 | tf_op jit(solution)/shard_map/ppermute | solution.py:75
  94.0 12.6 %collective-permute-start.29 = (bf16[256,512]{1,0:T(8,128)(2,1)S(1)}, bf16[256,512]{1,0:T(8,128)(2,1)S(1)}, u32[]{:S(2)}, u32[]{:S(2)}) collective-permute-start(bf16[256,512]{1,0:T(8,128)(2,1)S(1)} %get-tuple-element.166), channel_id=1, source_target_pairs={{4,0},{6,2},{8,4},{10,6},{12,8},{14,10},{16,12},{18,14},{20,16},{2... | collective-permute-start | bytes 786440 | tf_op jit(solution)/shard_map/ppermute | solution.py:98
  95.3 15.7 %collective-permute-start.28 = (bf16[256,512]{1,0:T(8,128)(2,1)S(1)}, bf16[256,512]{1,0:T(8,128)(2,1)S(1)}, u32[]{:S(2)}, u32[]{:S(2)}) collective-permute-start(bf16[256,512]{1,0:T(8,128)(2,1)S(1)} %get-tuple-element.164), channel_id=1, source_target_pairs={{2,0},{4,2},{6,4},{8,6},{10,8},{12,10},{14,12},{16,14},{18,16},{20... | collective-permute-start | bytes 786440 | tf_op jit(solution)/shard_map/ppermute | solution.py:98
  100.6 11.7 %collective-permute-start.33 = (bf16[416,128]{1,0:T(8,128)(2,1)S(1)}, bf16[416,128]{1,0:T(8,128)(2,1)S(1)}, u32[]{:S(2)}, u32[]{:S(2)}) collective-permute-start(bf16[416,128]{1,0:T(8,128)(2,1)S(1)} %add_convert_fusion.5), channel_id=1, source_target_pairs={{0,96},{1,25},{2,98},{3,27},{4,100},{5,29},{6,102},{7,31},{8,104},... | collective-permute-start | bytes 319496 | tf_op jit(solution)/shard_map/ppermute | solution.py:83
  105.1 7.6 %collective-permute-start.31 = (bf16[960,128]{1,0:T(8,128)(2,1)S(1)}, bf16[960,128]{1,0:T(8,128)(2,1)S(1)}, u32[]{:S(2)}, u32[]{:S(2)}) collective-permute-start(bf16[960,128]{1,0:T(8,128)(2,1)S(1)} %add_convert_fusion.2), channel_id=1, source_target_pairs={{0,6},{1,3},{2,4},{3,1},{4,2},{5,7},{6,0},{7,5},{8,14},{9,11},{10,... | collective-permute-start | bytes 737288 | tf_op jit(solution)/shard_map/ppermute | solution.py:75
  113.4 8.9 %collective-permute-start.36 = (bf16[1376,128]{1,0:T(8,128)(2,1)S(1)}, bf16[1376,128]{1,0:T(8,128)(2,1)S(1)}, u32[]{:S(2)}, u32[]{:S(2)}) collective-permute-start(bf16[1376,128]{1,0:T(8,128)(2,1)S(1)} %pad_maximum_fusion.own), channel_id=1, source_target_pairs={{0,16},{1,65},{2,18},{3,67},{4,20},{5,69},{6,22},{7,71},{8,24},{9,... | collective-permute-start | bytes 1056776 | tf_op jit(solution)/shard_map/ppermute | solution.py:91
  116.8 9.2 %collective-permute-start.37 = (bf16[1376,128]{1,0:T(8,128)(2,1)S(1)}, bf16[1376,128]{1,0:T(8,128)(2,1)S(1)}, u32[]{:S(2)}, u32[]{:S(2)}) collective-permute-start(bf16[1376,128]{1,0:T(8,128)(2,1)S(1)} %pad_maximum_fusion.own), channel_id=1, source_target_pairs={{0,8},{1,33},{2,10},{3,35},{4,12},{5,37},{6,14},{7,39},{8,16},{9,4... | collective-permute-start | bytes 1056776 | tf_op jit(solution)/shard_map/ppermute | solution.py:91
  117.5 9.1 %collective-permute-start.38 = (bf16[1376,128]{1,0:T(8,128)(2,1)S(1)}, bf16[1376,128]{1,0:T(8,128)(2,1)S(1)}, u32[]{:S(2)}, u32[]{:S(2)}) collective-permute-start(bf16[1376,128]{1,0:T(8,128)(2,1)S(1)} %pad_maximum_fusion.own), channel_id=1, source_target_pairs={{0,24},{1,97},{2,26},{3,99},{4,28},{5,101},{6,30},{7,103},{8,0},{9... | collective-permute-start | bytes 1056776 | tf_op jit(solution)/shard_map/ppermute | solution.py:91
  128.5 15.7 %collective-permute-start.43 = (bf16[3840,128]{1,0:T(8,128)(2,1)S(1)}, bf16[3840,128]{1,0:T(8,128)(2,1)S(1)}, u32[]{:S(2)}, u32[]{:S(2)}) collective-permute-start(bf16[3840,128]{1,0:T(8,128)(2,1)S(1)} %get-tuple-element.180.refs_0_), channel_id=1, source_target_pairs={{0,64},{1,17},{2,66},{3,19},{4,68},{5,21},{6,70},{7,23},{8,72},{9,... | collective-permute-start | bytes 2949128 | tf_op jit(solution)/shard_map/ppermute | solution.py:91
  131.6 23.4 %collective-permute-start.40 = (bf16[3840,128]{1,0:T(8,128)(2,1)S(1)}, bf16[3840,128]{1,0:T(8,128)(2,1)S(1)}, u32[]{:S(2)}, u32[]{:S(2)}) collective-permute-start(bf16[3840,128]{1,0:T(8,128)(2,1)S(1)} %get-tuple-element.180.refs_0_), channel_id=1, source_target_pairs={{0,32},{1,9},{2,34},{3,11},{4,36},{5,13},{6,38},{7,15},{8,40},{9,1... | collective-permute-start | bytes 2949128 | tf_op jit(solution)/shard_map/ppermute | solution.py:91
  131.6 23.4 %collective-permute-start.41 = (bf16[3840,128]{1,0:T(8,128)(2,1)S(1)}, bf16[3840,128]{1,0:T(8,128)(2,1)S(1)}, u32[]{:S(2)}, u32[]{:S(2)}) collective-permute-start(bf16[3840,128]{1,0:T(8,128)(2,1)S(1)} %get-tuple-element.180.refs_0_), channel_id=1, source_target_pairs={{0,96},{1,25},{2,98},{3,27},{4,100},{5,29},{6,102},{7,31},{8,104},... | collective-permute-start | bytes 2949128 | tf_op jit(solution)/shard_map/ppermute | solution.py:91
  134.8 16.4 %collective-permute-start.45 = (bf16[1664,128]{1,0:T(8,128)(2,1)S(1)}, bf16[1664,128]{1,0:T(8,128)(2,1)S(1)}, u32[]{:S(2)}, u32[]{:S(2)}) collective-permute-start(bf16[1664,128]{1,0:T(8,128)(2,1)S(1)} %get-tuple-element.179.refs_1_), channel_id=1, source_target_pairs={{0,4},{1,5},{2,6},{3,7},{4,0},{5,1},{6,2},{7,3},{8,12},{9,13},{10,... | collective-permute-start | bytes 1277960 | tf_op jit(solution)/shard_map/ppermute | solution.py:644
  137.6 17.5 %collective-permute-start.42 = (bf16[1664,128]{1,0:T(8,128)(2,1)S(1)}, bf16[1664,128]{1,0:T(8,128)(2,1)S(1)}, u32[]{:S(2)}, u32[]{:S(2)}) collective-permute-start(bf16[1664,128]{1,0:T(8,128)(2,1)S(1)} %get-tuple-element.179.refs_1_), channel_id=1, source_target_pairs={{0,2},{1,7},{2,4},{3,1},{4,6},{5,3},{6,0},{7,5},{8,10},{9,15},{10,... | collective-permute-start | bytes 1277960 | tf_op jit(solution)/shard_map/ppermute | solution.py:645
  144.2 10.8 %collective-permute-start.44 = (bf16[1664,128]{1,0:T(8,128)(2,1)S(1)}, bf16[1664,128]{1,0:T(8,128)(2,1)S(1)}, u32[]{:S(2)}, u32[]{:S(2)}) collective-permute-start(bf16[1664,128]{1,0:T(8,128)(2,1)S(1)} %get-tuple-element.179.refs_1_), channel_id=1, source_target_pairs={{0,6},{1,3},{2,0},{3,5},{4,2},{5,7},{6,4},{7,1},{8,14},{9,11},{10,... | collective-permute-start | bytes 1277960 | tf_op jit(solution)/shard_map/ppermute | solution.py:656
  (28 other events, 108.5 us)

commit v4 on v3

--- a/solution.py
+++ b/solution.py
@@ -204,7 +204,7 @@
     normed_two[...] = (h * inv_rms(h) * gain_two[...]).astype(BF16)
 
 
-FFN_STEP = 512
+FFN_STEP = 1024
 
 
 def ffn_half(n, y, wg, wu, wd, hid, dg, du):

time: 160 us -> 160 us (level)
  no operation moved by 1% of the time
where the time goes in v4:
time: 160 us; the launch traced here: 158 us
  starting transfers between devices  59.5 us (37%)
  waiting for transfers between devices  54.3 us (34%)
  Pallas kernels  34.4 us (22%)
  local copies, waits for them, and re-layouts  5.16 us (3%)
  other arithmetic  3.76 us (2%)
    ppermute x12, waiting for transfers between devices, to_peers(): lax.ppermute(part, ('ctx', 'fsdp'), shift(by))  28.1 us
    pallas_call x10, Pallas kernels, call(): pl.pallas_call(body, out_shape=shapes, in_specs=[smem] * scalars + [whole...  26.9 us
    ppermute x12, starting transfers between devices, to_peers(): lax.ppermute(part, ('ctx', 'fsdp'), shift(by))  25.8 us
    ppermute x5, waiting for transfers between devices, swap_y(): lax.ppermute(v, ('ctx', 'fsdp'), chip_pairs(lambda x, z, y, c: (x, z, (pa...  12.2 us
    ppermute x4, starting transfers between devices, passed_along(): return lax.ppermute(shard, 'ctx', pairs)  10.4 us
    pallas_call x3, Pallas kernels, spread(): pl.pallas_call(functools.partial(spread_body, f_places, a_places, not sha...  7.51 us
    ppermute x5, starting transfers between devices, swap_y(): lax.ppermute(v, ('ctx', 'fsdp'), chip_pairs(lambda x, z, y, c: (x, z, (pa...  6.88 us
    ppermute x4, waiting for transfers between devices, passed_along(): return lax.ppermute(shard, 'ctx', pairs)  6.17 us
  transfers between devices with their start and end apart: 46, of which 20 were waited for; matrix products, arithmetic and copies ran while one was open for 2% of the time, Pallas kernels for 14%

profile of v4, /device:TPU:0, one launch (start us, length us, event | category | flops | bytes accessed | tf_op | source)
XLA Modules:
  0.0 158.3 jit_solution(10492701341222794073)
XLA Ops:
  0.6 5.2 %collective-permute-start = (bf16[256,640]{1,0:T(8,128)(2,1)}, bf16[256,640]{1,0:T(8,128)(2,1)S(1)}, u32[]{:S(2)}, u32[]{:S(2)}) collective-permute-start(bf16[256,640]{1,0:T(8,128)(2,1)} %bitcast.13), channel_id=1, source_target_pairs={{0,4},{2,6},{4,8},{6,10},{8,12},{10,14},{12,16},{14,18},{16,20},{1... | collective-permute-start | bytes 983048 | tf_op jit(solution)/shard_map/ppermute | solution.py:98
  5.9 2.6 %collective-permute-start.1 = (bf16[256,640]{1,0:T(8,128)(2,1)}, bf16[256,640]{1,0:T(8,128)(2,1)S(1)}, u32[]{:S(2)}, u32[]{:S(2)}) collective-permute-start(bf16[256,640]{1,0:T(8,128)(2,1)} %bitcast.14), channel_id=1, source_target_pairs={{0,2},{2,4},{4,6},{6,8},{8,10},{10,12},{12,14},{14,16},{16,18},{18... | collective-permute-start | bytes 983048 | tf_op jit(solution)/shard_map/ppermute | solution.py:98
  23.0 3.4 %attend.1 = (bf16[768,640]{1,0:T(8,128)(2,1)S(1)}, bf16[256,1024]{1,0:T(8,128)(2,1)S(1)}, bf16[768,512]{1,0:T(8,128)(2,1)S(1)}, bf16[256,512]{1,0:T(8,128)(2,1)S...) custom-call(bf16[256,640]{1,0:T(8,128)(2,1)S(1)} %collective-permute, ...), custom_call_target="tpu_custom_call" | custom-call | flops 5500000256 | bytes 1024 | tf_op jit(solution)/shard_map/attend/pallas_call | solution.py:118
  27.4 3.0 %ffn_other.1 = (bf16[256,1024]{1,0:T(8,128)(2,1)S(1)}, bf16[256,1024]{1,0:T(8,128)(2,1)S(1)}, bf16[256,1024]{1,0:T(8,128)(2,1)S(1)}, f32[256,640]{1,0:T(8,128)S(1)}, f32[256,640]{1,0:T(8,128)S(1)}) custom-call(bf16[256,640]{1,0:T(8,128)(2,1)S(1)} %get-tuple-element.142.normed_two.n, bf16[256,640]{1,0:T(8,128)(2,1)S(1)} %bitcast.10, ...), custom_call_target="tpu_custom_call" | custom-call | flops 5500000256 | bytes 1024 | tf_op jit(solution)/shard_map/ffn_other/pallas_call | solution.py:118
  31.6 4.0 %ffn.1 = (bf16[256,640]{1,0:T(8,128)(2,1)}, bf16[256,1024]{1,0:T(8,128)(2,1)S(1)}, bf16[256,1024]{1,0:T(8,128)(2,1)S(1)}, bf16[256,1024]{1,0:T(8,128)(2,1)S(1)},...) custom-call(f32[256,640]{1,0:T(8,128)S(1)} %get-tuple-element.117.after, ...), custom_call_target="tpu_custom_call" | custom-call | flops 4400000000 | bytes 1024 | tf_op jit(solution)/shard_map/ffn/pallas_call | solution.py:118
  35.7 4.2 %attend_grad.1 = (bf16[256,512]{1,0:T(8,128)(2,1)S(1)}, bf16[256,512]{1,0:T(8,128)(2,1)S(1)}, bf16[256,512]{1,0:T(8,128)(2,1)S(1)}, bf16[256,512]{1,0:T(8,128)(2...) custom-call(s32[4]{0:T(128)S(1)} %pad_add_fusion.where, ...), custom_call_target="tpu_custom_call" | custom-call | bytes 1024 | tf_op jit(solution)/shard_map/attend_grad/pallas_call | solution.py:118
  40.8 2.9 %ffn_grads.1 = (bf16[3840,128]{1,0:T(8,128)(2,1)S(1)}, bf16[3840,128]{1,0:T(8,128)(2,1)S(1)}, bf16[3840,128]{1,0:T(8,128)(2,1)S(1)}, bf16[3840,128]{1,0:T(8,128)(2,1)S(1)}) custom-call(s32[4]{0:T(128)S(1)} %pad_add_fusion.where, bf16[256,1024]{1,0:T(8,128)(2,1)S(1)} %get-tuple-element.136.hid_m, bf16[256,1024]{1,0:T(8,128)(2,1)S(1)} %collective-permute-done.11.hid_r, ...), custom_call_target="tpu_custom_call" | custom-call | flops 3300000000 | bytes 1024 | tf_op jit(solution)/shard_map/ffn_grads/pallas_call | solution.py:118
  43.8 3.8 %attend_grads.1 = (bf16[1664,128]{1,0:T(8,128)(2,1)S(1)}, bf16[1664,128]{1,0:T(8,128)(2,1)S(1)}, bf16[1664,128]{1,0:T(8,128)(2,1)S(1)}, bf16[1664,128]{1,0:T(8,128)(2,1)S(1)}) custom-call(s32[4]{0:T(128)S(1)} %pad_add_fusion.where, bf16[768,640]{1,0:T(8,128)(2,1)S(1)} %get-tuple-element.145.n, bf16[768,640]{1,0:T(8,128)(2,1)S(1)} %collective-permute-done.15.n_r, ...), custom_call_target="tpu_custom_call" | custom-call | bytes 1024 | tf_op jit(solution)/shard_map/attend_grads/pallas_call | solution.py:118
  48.6 4.2 %collective-permute-start.19 = (bf16[3840,128]{1,0:T(8,128)(2,1)S(1)}, bf16[3840,128]{1,0:T(8,128)(2,1)S(1)}, u32[]{:S(2)}, u32[]{:S(2)}) collective-permute-start(bf16[3840,128]{1,0:T(8,128)(2,1)S(1)} %get-tuple-element.154), channel_id=1, source_target_pairs={{0,64},{1,17},{2,66},{3,19},{4,68},{5,21},{6,70},{7,23},{8,72},{9,... | collective-permute-start | bytes 2949128 | tf_op jit(solution)/shard_map/ppermute | solution.py:91
  53.6 2.6 %collective-permute-start.21 = (bf16[3840,128]{1,0:T(8,128)(2,1)S(1)}, bf16[3840,128]{1,0:T(8,128)(2,1)S(1)}, u32[]{:S(2)}, u32[]{:S(2)}) collective-permute-start(bf16[3840,128]{1,0:T(8,128)(2,1)S(1)} %get-tuple-element.156), channel_id=1, source_target_pairs={{0,96},{1,25},{2,98},{3,27},{4,100},{5,29},{6,102},{7,31},{8,104},... | collective-permute-start | bytes 2949128 | tf_op jit(solution)/shard_map/ppermute | solution.py:91
  60.1 8.1 %collective-permute-done.22.a_one = bf16[1664,128]{1,0:T(8,128)(2,1)S(1)} collective-permute-done((bf16[1664,128]{1,0:T(8,128)(2,1)S(1)}, bf16[1664,128]{1,0:T(8,128)(2,1)S(1)}, u32[]{:S(2)}, u32[]{:S(2)}) %collective-permute-start.22) | collective-permute-done | bytes 426016 | tf_op jit(solution)/shard_map/ppermute | solution.py:75
  68.2 7.3 %collective-permute-done.20.r_one = bf16[3840,128]{1,0:T(8,128)(2,1)S(1)} collective-permute-done((bf16[3840,128]{1,0:T(8,128)(2,1)S(1)}, bf16[3840,128]{1,0:T(8,128)(2,1)S(1)}, u32[]{:S(2)}, u32[]{:S(2)}) %collective-permute-start.20) | collective-permute-done | bytes 983072 | tf_op jit(solution)/shard_map/ppermute | solution.py:91
  77.4 2.4 %collective-permute-start.25 = (bf16[1376,128]{1,0:T(8,128)(2,1)S(1)}, bf16[1376,128]{1,0:T(8,128)(2,1)S(1)}, u32[]{:S(2)}, u32[]{:S(2)}) collective-permute-start(bf16[1376,128]{1,0:T(8,128)(2,1)S(1)} %get-tuple-element.161), channel_id=1, source_target_pairs={{0,16},{1,65},{2,18},{3,67},{4,20},{5,69},{6,22},{7,71},{8,24},{9,... | collective-permute-start | bytes 1056776 | tf_op jit(solution)/shard_map/ppermute | solution.py:91
  80.2 2.8 %collective-permute-start.27 = (bf16[1376,128]{1,0:T(8,128)(2,1)S(1)}, bf16[1376,128]{1,0:T(8,128)(2,1)S(1)}, u32[]{:S(2)}, u32[]{:S(2)}) collective-permute-start(bf16[1376,128]{1,0:T(8,128)(2,1)S(1)} %get-tuple-element.163), channel_id=1, source_target_pairs={{0,24},{1,97},{2,26},{3,99},{4,28},{5,101},{6,30},{7,103},{8,0},{9... | collective-permute-start | bytes 1056776 | tf_op jit(solution)/shard_map/ppermute | solution.py:91
  83.0 3.4 %collective-permute-done.25 = bf16[1376,128]{1,0:T(8,128)(2,1)S(1)} collective-permute-done((bf16[1376,128]{1,0:T(8,128)(2,1)S(1)}, bf16[1376,128]{1,0:T(8,128)(2,1)S(1)}, u32[]{:S(2)}, u32[]{:S(2)}) %collective-permute-start.25) | collective-permute-done | bytes 352288 | tf_op jit(solution)/shard_map/ppermute | solution.py:91
  86.4 3.7 %collective-permute-done.26 = bf16[1376,128]{1,0:T(8,128)(2,1)S(1)} collective-permute-done((bf16[1376,128]{1,0:T(8,128)(2,1)S(1)}, bf16[1376,128]{1,0:T(8,128)(2,1)S(1)}, u32[]{:S(2)}, u32[]{:S(2)}) %collective-permute-start.26) | collective-permute-done | bytes 352288 | tf_op jit(solution)/shard_map/ppermute | solution.py:91
  96.4 3.9 %collective-permute-done.30 = bf16[960,128]{1,0:T(8,128)(2,1)S(1)} collective-permute-done((bf16[960,128]{1,0:T(8,128)(2,1)S(1)}, bf16[960,128]{1,0:T(8,128)(2,1)S(1)}, u32[]{:S(2)}, u32[]{:S(2)}) %collective-permute-start.30) | collective-permute-done | bytes 245792 | tf_op jit(solution)/shard_map/ppermute | solution.py:75
  100.3 4.2 %collective-permute-start.33 = (bf16[416,128]{1,0:T(8,128)(2,1)S(1)}, bf16[416,128]{1,0:T(8,128)(2,1)S(1)}, u32[]{:S(2)}, u32[]{:S(2)}) collective-permute-start(bf16[416,128]{1,0:T(8,128)(2,1)S(1)} %add_convert_fusion.5), channel_id=1, source_target_pairs={{0,96},{1,25},{2,98},{3,27},{4,100},{5,29},{6,102},{7,31},{8,104},... | collective-permute-start | bytes 319496 | tf_op jit(solution)/shard_map/ppermute | solution.py:83
  104.6 2.3 %collective-permute-done.29.back_two = bf16[256,512]{1,0:T(8,128)(2,1)S(1)} collective-permute-done((bf16[256,512]{1,0:T(8,128)(2,1)S(1)}, bf16[256,512]{1,0:T(8,128)(2,1)S(1)}, u32[]{:S(2)}, u32[]{:S(2)}) %collective-permute-start.29) | collective-permute-done | bytes 262176 | tf_op jit(solution)/shard_map/ppermute | solution.py:98
  106.9 3.9 %collective-permute-done.28.back_one = bf16[256,512]{1,0:T(8,128)(2,1)S(1)} collective-permute-done((bf16[256,512]{1,0:T(8,128)(2,1)S(1)}, bf16[256,512]{1,0:T(8,128)(2,1)S(1)}, u32[]{:S(2)}, u32[]{:S(2)}) %collective-permute-start.28) | collective-permute-done | bytes 262176 | tf_op jit(solution)/shard_map/ppermute | solution.py:98
  113.1 3.2 %collective-permute-start.36 = (bf16[1376,128]{1,0:T(8,128)(2,1)S(1)}, bf16[1376,128]{1,0:T(8,128)(2,1)S(1)}, u32[]{:S(2)}, u32[]{:S(2)}) collective-permute-start(bf16[1376,128]{1,0:T(8,128)(2,1)S(1)} %pad_maximum_fusion.own), channel_id=1, source_target_pairs={{0,16},{1,65},{2,18},{3,67},{4,20},{5,69},{6,22},{7,71},{8,24},{9,... | collective-permute-start | bytes 1056776 | tf_op jit(solution)/shard_map/ppermute | solution.py:91
  117.0 2.4 %collective-permute-start.38 = (bf16[1376,128]{1,0:T(8,128)(2,1)S(1)}, bf16[1376,128]{1,0:T(8,128)(2,1)S(1)}, u32[]{:S(2)}, u32[]{:S(2)}) collective-permute-start(bf16[1376,128]{1,0:T(8,128)(2,1)S(1)} %pad_maximum_fusion.own), channel_id=1, source_target_pairs={{0,24},{1,97},{2,26},{3,99},{4,28},{5,101},{6,30},{7,103},{8,0},{9... | collective-permute-start | bytes 1056776 | tf_op jit(solution)/shard_map/ppermute | solution.py:91
  119.5 2.6 %collective-permute-done.36.r_two = bf16[1376,128]{1,0:T(8,128)(2,1)S(1)} collective-permute-done((bf16[1376,128]{1,0:T(8,128)(2,1)S(1)}, bf16[1376,128]{1,0:T(8,128)(2,1)S(1)}, u32[]{:S(2)}, u32[]{:S(2)}) %collective-permute-start.36) | collective-permute-done | bytes 352288 | tf_op jit(solution)/shard_map/ppermute | solution.py:91
  122.0 3.7 %collective-permute-done.37.r_one = bf16[1376,128]{1,0:T(8,128)(2,1)S(1)} collective-permute-done((bf16[1376,128]{1,0:T(8,128)(2,1)S(1)}, bf16[1376,128]{1,0:T(8,128)(2,1)S(1)}, u32[]{:S(2)}, u32[]{:S(2)}) %collective-permute-start.37) | collective-permute-done | bytes 352288 | tf_op jit(solution)/shard_map/ppermute | solution.py:91
  128.0 3.1 %collective-permute-start.43 = (bf16[3840,128]{1,0:T(8,128)(2,1)S(1)}, bf16[3840,128]{1,0:T(8,128)(2,1)S(1)}, u32[]{:S(2)}, u32[]{:S(2)}) collective-permute-start(bf16[3840,128]{1,0:T(8,128)(2,1)S(1)} %get-tuple-element.180.refs_0_), channel_id=1, source_target_pairs={{0,64},{1,17},{2,66},{3,19},{4,68},{5,21},{6,70},{7,23},{8,72},{9,... | collective-permute-start | bytes 2949128 | tf_op jit(solution)/shard_map/ppermute | solution.py:91
  131.1 3.2 %collective-permute-start.41 = (bf16[3840,128]{1,0:T(8,128)(2,1)S(1)}, bf16[3840,128]{1,0:T(8,128)(2,1)S(1)}, u32[]{:S(2)}, u32[]{:S(2)}) collective-permute-start(bf16[3840,128]{1,0:T(8,128)(2,1)S(1)} %get-tuple-element.180.refs_0_), channel_id=1, source_target_pairs={{0,96},{1,25},{2,98},{3,27},{4,100},{5,29},{6,102},{7,31},{8,104},... | collective-permute-start | bytes 2949128 | tf_op jit(solution)/shard_map/ppermute | solution.py:91
  134.3 2.9 %collective-permute-start.45 = (bf16[1664,128]{1,0:T(8,128)(2,1)S(1)}, bf16[1664,128]{1,0:T(8,128)(2,1)S(1)}, u32[]{:S(2)}, u32[]{:S(2)}) collective-permute-start(bf16[1664,128]{1,0:T(8,128)(2,1)S(1)} %get-tuple-element.179.refs_1_), channel_id=1, source_target_pairs={{0,4},{1,5},{2,6},{3,7},{4,0},{5,1},{6,2},{7,3},{8,12},{9,13},{10,... | collective-permute-start | bytes 1277960 | tf_op jit(solution)/shard_map/ppermute | solution.py:644
  137.3 6.4 %collective-permute-done.43.refs_0_ = bf16[3840,128]{1,0:T(8,128)(2,1)S(1)} collective-permute-done((bf16[3840,128]{1,0:T(8,128)(2,1)S(1)}, bf16[3840,128]{1,0:T(8,128)(2,1)S(1)}, u32[]{:S(2)}, u32[]{:S(2)}) %collective-permute-start.43) | collective-permute-done | bytes 983072 | tf_op jit(solution)/shard_map/ppermute | solution.py:91
  143.7 2.7 %collective-permute-start.44 = (bf16[1664,128]{1,0:T(8,128)(2,1)S(1)}, bf16[1664,128]{1,0:T(8,128)(2,1)S(1)}, u32[]{:S(2)}, u32[]{:S(2)}) collective-permute-start(bf16[1664,128]{1,0:T(8,128)(2,1)S(1)} %get-tuple-element.179.refs_1_), channel_id=1, source_target_pairs={{0,6},{1,3},{2,0},{3,5},{4,2},{5,7},{6,4},{7,1},{8,14},{9,11},{10,... | collective-permute-start | bytes 1277960 | tf_op jit(solution)/shard_map/ppermute | solution.py:656
  146.5 2.3 %token_grad.1 = (f32[256,640]{1,0:T(8,128)}, f32[320]{0:T(512)}, f32[320]{0:T(512)}) custom-call(s32[4]{0:T(128)S(1)} %pad_add_fusion.where, bf16[256,640]{1,0:T(8,128)(2,1)S(1)} %bitcast.16, f32[1,640]{1,0:T(1,128)S(1)} %maximum_convert_fusion.1.gain, f32[256,640]{1,0:T(8,128)S(1)} %get-tuple-element.125.grad_after, ...), custom_call_target="tpu_custom_call" | custom-call | flops 2200000000 | bytes 1024 | tf_op jit(solution)/shard_map/token_grad/pallas_call | solution.py:118
  151.0 2.2 %spread.4 = (f32[640,1024]{1,0:T(8,128)}, f32[640,1024]{1,0:T(8,128)}, f32[1024,640]{1,0:T(8,128)}, f32[640,512]{1,0:T(8,128)}, f32[640,128]{1,0:T(8,128)}, /*index=5*/f32[640,128]{1,0:T(8,128)}, f32[512,640]{1,0:T(8,128)}) custom-call(s32[4]{0:T(128)S(1)} %pad_add_fusion.where, ...), custom_call_target="tpu_custom_call", output_to_operand_aliasing={{0}: (3, {}), {1}: (4, {}), {2}: (5, {}), {3}: (6, {}), {4}... | custom-call | flops 1024 | bytes 1024 | tf_op jit(solution)/shard_map/spread/pallas_call | solution.py:483
  155.0 3.1 %spread.5 = (f32[640,1024]{1,0:T(8,128)}, f32[640,1024]{1,0:T(8,128)}, f32[1024,640]{1,0:T(8,128)}, f32[640,512]{1,0:T(8,128)}, f32[640,128]{1,0:T(8,128)}, /*index=5*/f32[640,128]{1,0:T(8,128)}, f32[512,640]{1,0:T(8,128)}) custom-call(s32[4]{0:T(128)S(1)} %pad_add_fusion.where, ...), custom_call_target="tpu_custom_call", output_to_operand_aliasing={{0}: (5, {}), {1}: (6, {}), {2}: (7, {}), {3}: (8, {}), {4}... | custom-call | flops 1024 | bytes 1024 | tf_op jit(solution)/shard_map/spread/pallas_call | solution.py:483
  (120 shorter events, 41.2 us)
Async XLA Ops:
  0.6 21.7 %collective-permute-start = (bf16[256,640]{1,0:T(8,128)(2,1)}, bf16[256,640]{1,0:T(8,128)(2,1)S(1)}, u32[]{:S(2)}, u32[]{:S(2)}) collective-permute-start(bf16[256,640]{1,0:T(8,128)(2,1)} %bitcast.13), channel_id=1, source_target_pairs={{0,4},{2,6},{4,8},{6,10},{8,12},{10,14},{12,16},{14,18},{16,20},{1... | collective-permute-start | bytes 983048 | tf_op jit(solution)/shard_map/ppermute | solution.py:98
  5.9 16.5 %collective-permute-start.1 = (bf16[256,640]{1,0:T(8,128)(2,1)}, bf16[256,640]{1,0:T(8,128)(2,1)S(1)}, u32[]{:S(2)}, u32[]{:S(2)}) collective-permute-start(bf16[256,640]{1,0:T(8,128)(2,1)} %bitcast.14), channel_id=1, source_target_pairs={{0,2},{2,4},{4,6},{6,8},{8,10},{10,12},{12,14},{14,16},{16,18},{18... | collective-permute-start | bytes 983048 | tf_op jit(solution)/shard_map/ppermute | solution.py:98
  13.1 9.3 %collective-permute-start.8 = (bf16[256,640]{1,0:T(8,128)(2,1)}, bf16[256,640]{1,0:T(8,128)(2,1)S(1)}, u32[]{:S(2)}, u32[]{:S(2)}) collective-permute-start(bf16[256,640]{1,0:T(8,128)(2,1)} %bitcast.9), channel_id=1, source_target_pairs={{0,1},{1,0},{2,3},{3,2},{4,5},{5,4},{6,7},{7,6},{8,9},{9,8},{10,11... | collective-permute-start | bytes 983048 | tf_op jit(solution)/shard_map/ppermute | solution.py:31
  15.6 7.4 %collective-permute-start.7 = (bf16[640,1024]{1,0:T(8,128)(2,1)}, bf16[640,1024]{1,0:T(8,128)(2,1)S(1)}, u32[]{:S(2)}, u32[]{:S(2)}) collective-permute-start(bf16[640,1024]{1,0:T(8,128)(2,1)} %wg.1), channel_id=1, source_target_pairs={{0,1},{1,0},{2,3},{3,2},{4,5},{5,4},{6,7},{7,6},{8,9},{9,8},{10,11... | collective-permute-start | bytes 3932168 | tf_op jit(solution)/shard_map/ppermute | solution.py:31
  30.4 9.9 %collective-permute-start.11 = (bf16[256,1024]{1,0:T(8,128)(2,1)S(1)}, bf16[256,1024]{1,0:T(8,128)(2,1)S(1)}, u32[]{:S(2)}, u32[]{:S(2)}) collective-permute-start(bf16[256,1024]{1,0:T(8,128)(2,1)S(1)} %get-tuple-element.137), channel_id=1, source_target_pairs={{0,1},{1,0},{2,3},{3,2},{4,5},{5,4},{6,7},{7,6},{8,9},{9,8},{10,11... | collective-permute-start | bytes 1572872 | tf_op jit(solution)/shard_map/ppermute | solution.py:31
  30.6 9.3 %collective-permute-start.14 = (bf16[256,640]{1,0:T(8,128)(2,1)S(1)}, bf16[256,640]{1,0:T(8,128)(2,1)S(1)}, u32[]{:S(2)}, u32[]{:S(2)}) collective-permute-start(bf16[256,640]{1,0:T(8,128)(2,1)S(1)} %get-tuple-element.142.normed_two.n), channel_id=1, source_target_pairs={{0,1},{1,0},{2,3},{3,2},{4,5},{5,4},{6,7},{7,6},{8,9},{9,8},{10,11... | collective-permute-start | bytes 983048 | tf_op jit(solution)/shard_map/ppermute | solution.py:31
  31.0 9.5 %collective-permute-start.12 = (bf16[256,1024]{1,0:T(8,128)(2,1)S(1)}, bf16[256,1024]{1,0:T(8,128)(2,1)S(1)}, u32[]{:S(2)}, u32[]{:S(2)}) collective-permute-start(bf16[256,1024]{1,0:T(8,128)(2,1)S(1)} %get-tuple-element.139), channel_id=1, source_target_pairs={{0,1},{1,0},{2,3},{3,2},{4,5},{5,4},{6,7},{7,6},{8,9},{9,8},{10,11... | collective-permute-start | bytes 1572872 | tf_op jit(solution)/shard_map/ppermute | solution.py:31
  31.1 9.7 %collective-permute-start.13 = (bf16[256,1024]{1,0:T(8,128)(2,1)S(1)}, bf16[256,1024]{1,0:T(8,128)(2,1)S(1)}, u32[]{:S(2)}, u32[]{:S(2)}) collective-permute-start(bf16[256,1024]{1,0:T(8,128)(2,1)S(1)} %get-tuple-element.141), channel_id=1, source_target_pairs={{0,1},{1,0},{2,3},{3,2},{4,5},{5,4},{6,7},{7,6},{8,9},{9,8},{10,11... | collective-permute-start | bytes 1572872 | tf_op jit(solution)/shard_map/ppermute | solution.py:31
  31.5 12.3 %collective-permute-start.15 = (bf16[768,640]{1,0:T(8,128)(2,1)S(1)}, bf16[768,640]{1,0:T(8,128)(2,1)S(1)}, u32[]{:S(2)}, u32[]{:S(2)}) collective-permute-start(bf16[768,640]{1,0:T(8,128)(2,1)S(1)} %get-tuple-element.145.n), channel_id=1, source_target_pairs={{0,1},{1,0},{2,3},{3,2},{4,5},{5,4},{6,7},{7,6},{8,9},{9,8},{10,11... | collective-permute-start | bytes 2949128 | tf_op jit(solution)/shard_map/ppermute | solution.py:31
  47.6 10.4 %collective-permute-start.23 = (bf16[1664,128]{1,0:T(8,128)(2,1)S(1)}, bf16[1664,128]{1,0:T(8,128)(2,1)S(1)}, u32[]{:S(2)}, u32[]{:S(2)}) collective-permute-start(bf16[1664,128]{1,0:T(8,128)(2,1)S(1)} %get-tuple-element.159), channel_id=1, source_target_pairs={{0,2},{1,7},{2,0},{3,5},{4,6},{5,3},{6,4},{7,1},{8,10},{9,15},{10,... | collective-permute-start | bytes 1277960 | tf_op jit(solution)/shard_map/ppermute | solution.py:75
  48.6 19.6 %collective-permute-start.19 = (bf16[3840,128]{1,0:T(8,128)(2,1)S(1)}, bf16[3840,128]{1,0:T(8,128)(2,1)S(1)}, u32[]{:S(2)}, u32[]{:S(2)}) collective-permute-start(bf16[3840,128]{1,0:T(8,128)(2,1)S(1)} %get-tuple-element.154), channel_id=1, source_target_pairs={{0,64},{1,17},{2,66},{3,19},{4,68},{5,21},{6,70},{7,23},{8,72},{9,... | collective-permute-start | bytes 2949128 | tf_op jit(solution)/shard_map/ppermute | solution.py:91
  52.9 22.6 %collective-permute-start.20 = (bf16[3840,128]{1,0:T(8,128)(2,1)S(1)}, bf16[3840,128]{1,0:T(8,128)(2,1)S(1)}, u32[]{:S(2)}, u32[]{:S(2)}) collective-permute-start(bf16[3840,128]{1,0:T(8,128)(2,1)S(1)} %get-tuple-element.155), channel_id=1, source_target_pairs={{0,32},{1,9},{2,34},{3,11},{4,36},{5,13},{6,38},{7,15},{8,40},{9,1... | collective-permute-start | bytes 2949128 | tf_op jit(solution)/shard_map/ppermute | solution.py:91
  53.6 22.6 %collective-permute-start.21 = (bf16[3840,128]{1,0:T(8,128)(2,1)S(1)}, bf16[3840,128]{1,0:T(8,128)(2,1)S(1)}, u32[]{:S(2)}, u32[]{:S(2)}) collective-permute-start(bf16[3840,128]{1,0:T(8,128)(2,1)S(1)} %get-tuple-element.156), channel_id=1, source_target_pairs={{0,96},{1,25},{2,98},{3,27},{4,100},{5,29},{6,102},{7,31},{8,104},... | collective-permute-start | bytes 2949128 | tf_op jit(solution)/shard_map/ppermute | solution.py:91
  56.1 12.1 %collective-permute-start.22 = (bf16[1664,128]{1,0:T(8,128)(2,1)S(1)}, bf16[1664,128]{1,0:T(8,128)(2,1)S(1)}, u32[]{:S(2)}, u32[]{:S(2)}) collective-permute-start(bf16[1664,128]{1,0:T(8,128)(2,1)S(1)} %get-tuple-element.157), channel_id=1, source_target_pairs={{0,2},{1,7},{2,0},{3,5},{4,6},{5,3},{6,4},{7,1},{8,10},{9,15},{10,... | collective-permute-start | bytes 1277960 | tf_op jit(solution)/shard_map/ppermute | solution.py:75
  58.2 18.0 %collective-permute-start.24 = (bf16[1664,128]{1,0:T(8,128)(2,1)S(1)}, bf16[1664,128]{1,0:T(8,128)(2,1)S(1)}, u32[]{:S(2)}, u32[]{:S(2)}) collective-permute-start(bf16[1664,128]{1,0:T(8,128)(2,1)S(1)} %add_convert_fusion), channel_id=1, source_target_pairs={{0,6},{1,3},{2,4},{3,1},{4,2},{5,7},{6,0},{7,5},{8,14},{9,11},{10,... | collective-permute-start | bytes 1277960 | tf_op jit(solution)/shard_map/ppermute | solution.py:75
  77.4 9.0 %collective-permute-start.25 = (bf16[1376,128]{1,0:T(8,128)(2,1)S(1)}, bf16[1376,128]{1,0:T(8,128)(2,1)S(1)}, u32[]{:S(2)}, u32[]{:S(2)}) collective-permute-start(bf16[1376,128]{1,0:T(8,128)(2,1)S(1)} %get-tuple-element.161), channel_id=1, source_target_pairs={{0,16},{1,65},{2,18},{3,67},{4,20},{5,69},{6,22},{7,71},{8,24},{9,... | collective-permute-start | bytes 1056776 | tf_op jit(solution)/shard_map/ppermute | solution.py:91
  79.8 10.3 %collective-permute-start.26 = (bf16[1376,128]{1,0:T(8,128)(2,1)S(1)}, bf16[1376,128]{1,0:T(8,128)(2,1)S(1)}, u32[]{:S(2)}, u32[]{:S(2)}) collective-permute-start(bf16[1376,128]{1,0:T(8,128)(2,1)S(1)} %get-tuple-element.162), channel_id=1, source_target_pairs={{0,8},{1,33},{2,10},{3,35},{4,12},{5,37},{6,14},{7,39},{8,16},{9,4... | collective-permute-start | bytes 1056776 | tf_op jit(solution)/shard_map/ppermute | solution.py:91
  80.2 9.9 %collective-permute-start.27 = (bf16[1376,128]{1,0:T(8,128)(2,1)S(1)}, bf16[1376,128]{1,0:T(8,128)(2,1)S(1)}, u32[]{:S(2)}, u32[]{:S(2)}) collective-permute-start(bf16[1376,128]{1,0:T(8,128)(2,1)S(1)} %get-tuple-element.163), channel_id=1, source_target_pairs={{0,24},{1,97},{2,26},{3,99},{4,28},{5,101},{6,30},{7,103},{8,0},{9... | collective-permute-start | bytes 1056776 | tf_op jit(solution)/shard_map/ppermute | solution.py:91
  91.7 8.5 %collective-permute-start.30 = (bf16[960,128]{1,0:T(8,128)(2,1)S(1)}, bf16[960,128]{1,0:T(8,128)(2,1)S(1)}, u32[]{:S(2)}, u32[]{:S(2)}) collective-permute-start(bf16[960,128]{1,0:T(8,128)(2,1)S(1)} %add_convert_fusion.3), channel_id=1, source_target_pairs={{0,2},{1,7},{2,0},{3,5},{4,6},{5,3},{6,4},{7,1},{8,10},{9,15},{10,... | collective-permute-start | bytes 737288 | tf_op jit(solution)/shard_map/ppermute | solution.py:75
  93.7 13.1 %collective-permute-start.29 = (bf16[256,512]{1,0:T(8,128)(2,1)S(1)}, bf16[256,512]{1,0:T(8,128)(2,1)S(1)}, u32[]{:S(2)}, u32[]{:S(2)}) collective-permute-start(bf16[256,512]{1,0:T(8,128)(2,1)S(1)} %get-tuple-element.166), channel_id=1, source_target_pairs={{4,0},{6,2},{8,4},{10,6},{12,8},{14,10},{16,12},{18,14},{20,16},{2... | collective-permute-start | bytes 786440 | tf_op jit(solution)/shard_map/ppermute | solution.py:98
  95.0 15.7 %collective-permute-start.28 = (bf16[256,512]{1,0:T(8,128)(2,1)S(1)}, bf16[256,512]{1,0:T(8,128)(2,1)S(1)}, u32[]{:S(2)}, u32[]{:S(2)}) collective-permute-start(bf16[256,512]{1,0:T(8,128)(2,1)S(1)} %get-tuple-element.164), channel_id=1, source_target_pairs={{2,0},{4,2},{6,4},{8,6},{10,8},{12,10},{14,12},{16,14},{18,16},{20... | collective-permute-start | bytes 786440 | tf_op jit(solution)/shard_map/ppermute | solution.py:98
  100.3 11.7 %collective-permute-start.33 = (bf16[416,128]{1,0:T(8,128)(2,1)S(1)}, bf16[416,128]{1,0:T(8,128)(2,1)S(1)}, u32[]{:S(2)}, u32[]{:S(2)}) collective-permute-start(bf16[416,128]{1,0:T(8,128)(2,1)S(1)} %add_convert_fusion.5), channel_id=1, source_target_pairs={{0,96},{1,25},{2,98},{3,27},{4,100},{5,29},{6,102},{7,31},{8,104},... | collective-permute-start | bytes 319496 | tf_op jit(solution)/shard_map/ppermute | solution.py:83
  104.6 7.8 %collective-permute-start.31 = (bf16[960,128]{1,0:T(8,128)(2,1)S(1)}, bf16[960,128]{1,0:T(8,128)(2,1)S(1)}, u32[]{:S(2)}, u32[]{:S(2)}) collective-permute-start(bf16[960,128]{1,0:T(8,128)(2,1)S(1)} %add_convert_fusion.2), channel_id=1, source_target_pairs={{0,6},{1,3},{2,4},{3,1},{4,2},{5,7},{6,0},{7,5},{8,14},{9,11},{10,... | collective-permute-start | bytes 737288 | tf_op jit(solution)/shard_map/ppermute | solution.py:75
  113.1 8.9 %collective-permute-start.36 = (bf16[1376,128]{1,0:T(8,128)(2,1)S(1)}, bf16[1376,128]{1,0:T(8,128)(2,1)S(1)}, u32[]{:S(2)}, u32[]{:S(2)}) collective-permute-start(bf16[1376,128]{1,0:T(8,128)(2,1)S(1)} %pad_maximum_fusion.own), channel_id=1, source_target_pairs={{0,16},{1,65},{2,18},{3,67},{4,20},{5,69},{6,22},{7,71},{8,24},{9,... | collective-permute-start | bytes 1056776 | tf_op jit(solution)/shard_map/ppermute | solution.py:91
  116.2 9.5 %collective-permute-start.37 = (bf16[1376,128]{1,0:T(8,128)(2,1)S(1)}, bf16[1376,128]{1,0:T(8,128)(2,1)S(1)}, u32[]{:S(2)}, u32[]{:S(2)}) collective-permute-start(bf16[1376,128]{1,0:T(8,128)(2,1)S(1)} %pad_maximum_fusion.own), channel_id=1, source_target_pairs={{0,8},{1,33},{2,10},{3,35},{4,12},{5,37},{6,14},{7,39},{8,16},{9,4... | collective-permute-start | bytes 1056776 | tf_op jit(solution)/shard_map/ppermute | solution.py:91
  117.0 9.1 %collective-permute-start.38 = (bf16[1376,128]{1,0:T(8,128)(2,1)S(1)}, bf16[1376,128]{1,0:T(8,128)(2,1)S(1)}, u32[]{:S(2)}, u32[]{:S(2)}) collective-permute-start(bf16[1376,128]{1,0:T(8,128)(2,1)S(1)} %pad_maximum_fusion.own), channel_id=1, source_target_pairs={{0,24},{1,97},{2,26},{3,99},{4,28},{5,101},{6,30},{7,103},{8,0},{9... | collective-permute-start | bytes 1056776 | tf_op jit(solution)/shard_map/ppermute | solution.py:91
  128.0 15.7 %collective-permute-start.43 = (bf16[3840,128]{1,0:T(8,128)(2,1)S(1)}, bf16[3840,128]{1,0:T(8,128)(2,1)S(1)}, u32[]{:S(2)}, u32[]{:S(2)}) collective-permute-start(bf16[3840,128]{1,0:T(8,128)(2,1)S(1)} %get-tuple-element.180.refs_0_), channel_id=1, source_target_pairs={{0,64},{1,17},{2,66},{3,19},{4,68},{5,21},{6,70},{7,23},{8,72},{9,... | collective-permute-start | bytes 2949128 | tf_op jit(solution)/shard_map/ppermute | solution.py:91
  131.1 23.8 %collective-permute-start.40 = (bf16[3840,128]{1,0:T(8,128)(2,1)S(1)}, bf16[3840,128]{1,0:T(8,128)(2,1)S(1)}, u32[]{:S(2)}, u32[]{:S(2)}) collective-permute-start(bf16[3840,128]{1,0:T(8,128)(2,1)S(1)} %get-tuple-element.180.refs_0_), channel_id=1, source_target_pairs={{0,32},{1,9},{2,34},{3,11},{4,36},{5,13},{6,38},{7,15},{8,40},{9,1... | collective-permute-start | bytes 2949128 | tf_op jit(solution)/shard_map/ppermute | solution.py:91
  131.1 23.8 %collective-permute-start.41 = (bf16[3840,128]{1,0:T(8,128)(2,1)S(1)}, bf16[3840,128]{1,0:T(8,128)(2,1)S(1)}, u32[]{:S(2)}, u32[]{:S(2)}) collective-permute-start(bf16[3840,128]{1,0:T(8,128)(2,1)S(1)} %get-tuple-element.180.refs_0_), channel_id=1, source_target_pairs={{0,96},{1,25},{2,98},{3,27},{4,100},{5,29},{6,102},{7,31},{8,104},... | collective-permute-start | bytes 2949128 | tf_op jit(solution)/shard_map/ppermute | solution.py:91
  134.3 16.6 %collective-permute-start.45 = (bf16[1664,128]{1,0:T(8,128)(2,1)S(1)}, bf16[1664,128]{1,0:T(8,128)(2,1)S(1)}, u32[]{:S(2)}, u32[]{:S(2)}) collective-permute-start(bf16[1664,128]{1,0:T(8,128)(2,1)S(1)} %get-tuple-element.179.refs_1_), channel_id=1, source_target_pairs={{0,4},{1,5},{2,6},{3,7},{4,0},{5,1},{6,2},{7,3},{8,12},{9,13},{10,... | collective-permute-start | bytes 1277960 | tf_op jit(solution)/shard_map/ppermute | solution.py:644
  137.3 17.7 %collective-permute-start.42 = (bf16[1664,128]{1,0:T(8,128)(2,1)S(1)}, bf16[1664,128]{1,0:T(8,128)(2,1)S(1)}, u32[]{:S(2)}, u32[]{:S(2)}) collective-permute-start(bf16[1664,128]{1,0:T(8,128)(2,1)S(1)} %get-tuple-element.179.refs_1_), channel_id=1, source_target_pairs={{0,2},{1,7},{2,4},{3,1},{4,6},{5,3},{6,0},{7,5},{8,10},{9,15},{10,... | collective-permute-start | bytes 1277960 | tf_op jit(solution)/shard_map/ppermute | solution.py:645
  143.7 11.2 %collective-permute-start.44 = (bf16[1664,128]{1,0:T(8,128)(2,1)S(1)}, bf16[1664,128]{1,0:T(8,128)(2,1)S(1)}, u32[]{:S(2)}, u32[]{:S(2)}) collective-permute-start(bf16[1664,128]{1,0:T(8,128)(2,1)S(1)} %get-tuple-element.179.refs_1_), channel_id=1, source_target_pairs={{0,6},{1,3},{2,0},{3,5},{4,2},{5,7},{6,4},{7,1},{8,14},{9,11},{10,... | collective-permute-start | bytes 1277960 | tf_op jit(solution)/shard_map/ppermute | solution.py:656
  (28 other events, 108.4 us)

commit v5 on v4

--- a/solution.py
+++ b/solution.py
@@ -604,7 +604,10 @@
         scalars=1, scratch=[pltpu.VMEM((D, 512), BF16)],
         us=3,
     )
-    f_got = to_peers(f_chunks[1:], shift_first)
+    f_got = [
+        lax.ppermute(f_chunks[i], ("ctx", "fsdp"), shift_first(by)) for i, by in ((2, 1), (3, -1), (1, 2))
+    ]
+    f_got = [f_got[2], f_got[0], f_got[1]]
 
     a_chunks = call(
         "attend_grads", attend_grads_body, [((A_ROWS, 128), BF16)] * 4,

time: 160 us -> 160 us (level)
    ppermute x12 -> x9, waiting for transfers between devices: 28.1 us -> 20.2 us  [to_peers(): lax.ppermute(part, ('ctx', 'fsdp'), shift(by))]
    ppermute x0 -> x3, waiting for transfers between devices: none -> 7.96 us  [local(): lax.ppermute(f_chunks[i], ('ctx', 'fsdp'), shift_first(by))]
    ppermute x0 -> x3, starting transfers between devices: none -> 7.49 us  [local(): lax.ppermute(f_chunks[i], ('ctx', 'fsdp'), shift_first(by))]
    ppermute x12 -> x9, starting transfers between devices: 25.8 us -> 18.3 us  [to_peers(): lax.ppermute(part, ('ctx', 'fsdp'), shift(by))]
where the time goes in v5:
time: 160 us; the launch traced here: 158 us
  starting transfers between devices  59.5 us (37%)
  waiting for transfers between devices  54.3 us (34%)
  Pallas kernels  34.4 us (22%)
  local copies, waits for them, and re-layouts  5.16 us (3%)
  other arithmetic  3.76 us (2%)
    pallas_call x10, Pallas kernels, call(): pl.pallas_call(body, out_shape=shapes, in_specs=[smem] * scalars + [whole...  26.9 us
    ppermute x9, waiting for transfers between devices, to_peers(): lax.ppermute(part, ('ctx', 'fsdp'), shift(by))  20.2 us
    ppermute x9, starting transfers between devices, to_peers(): lax.ppermute(part, ('ctx', 'fsdp'), shift(by))  18.3 us
    ppermute x5, waiting for transfers between devices, swap_y(): lax.ppermute(v, ('ctx', 'fsdp'), chip_pairs(lambda x, z, y, c: (x, z, (pa...  12.2 us
    ppermute x4, starting transfers between devices, passed_along(): return lax.ppermute(shard, 'ctx', pairs)  10.4 us
    ppermute x3, waiting for transfers between devices, local(): lax.ppermute(f_chunks[i], ('ctx', 'fsdp'), shift_first(by))  7.96 us
    pallas_call x3, Pallas kernels, spread(): pl.pallas_call(functools.partial(spread_body, f_places, a_places, not sha...  7.51 us
    ppermute x3, starting transfers between devices, local(): lax.ppermute(f_chunks[i], ('ctx', 'fsdp'), shift_first(by))  7.49 us
  transfers between devices with their start and end apart: 46, of which 20 were waited for; matrix products, arithmetic and copies ran while one was open for 2% of the time, Pallas kernels for 14%

profile of v5, /device:TPU:0, one launch (start us, length us, event | category | flops | bytes accessed | tf_op | source)
XLA Modules:
  0.0 158.3 jit_solution(10492701341222794073)
XLA Ops:
  0.6 5.2 %collective-permute-start = (bf16[256,640]{1,0:T(8,128)(2,1)}, bf16[256,640]{1,0:T(8,128)(2,1)S(1)}, u32[]{:S(2)}, u32[]{:S(2)}) collective-permute-start(bf16[256,640]{1,0:T(8,128)(2,1)} %bitcast.13), channel_id=1, source_target_pairs={{0,4},{2,6},{4,8},{6,10},{8,12},{10,14},{12,16},{14,18},{16,20},{1... | collective-permute-start | bytes 983048 | tf_op jit(solution)/shard_map/ppermute | solution.py:98
  5.9 2.6 %collective-permute-start.1 = (bf16[256,640]{1,0:T(8,128)(2,1)}, bf16[256,640]{1,0:T(8,128)(2,1)S(1)}, u32[]{:S(2)}, u32[]{:S(2)}) collective-permute-start(bf16[256,640]{1,0:T(8,128)(2,1)} %bitcast.14), channel_id=1, source_target_pairs={{0,2},{2,4},{4,6},{6,8},{8,10},{10,12},{12,14},{14,16},{16,18},{18... | collective-permute-start | bytes 983048 | tf_op jit(solution)/shard_map/ppermute | solution.py:98
  23.0 3.4 %attend.1 = (bf16[768,640]{1,0:T(8,128)(2,1)S(1)}, bf16[256,1024]{1,0:T(8,128)(2,1)S(1)}, bf16[768,512]{1,0:T(8,128)(2,1)S(1)}, bf16[256,512]{1,0:T(8,128)(2,1)S...) custom-call(bf16[256,640]{1,0:T(8,128)(2,1)S(1)} %collective-permute, ...), custom_call_target="tpu_custom_call" | custom-call | flops 5500000256 | bytes 1024 | tf_op jit(solution)/shard_map/attend/pallas_call | solution.py:118
  27.4 3.0 %ffn_other.1 = (bf16[256,1024]{1,0:T(8,128)(2,1)S(1)}, bf16[256,1024]{1,0:T(8,128)(2,1)S(1)}, bf16[256,1024]{1,0:T(8,128)(2,1)S(1)}, f32[256,640]{1,0:T(8,128)S(1)}, f32[256,640]{1,0:T(8,128)S(1)}) custom-call(bf16[256,640]{1,0:T(8,128)(2,1)S(1)} %get-tuple-element.142.normed_two.n, bf16[256,640]{1,0:T(8,128)(2,1)S(1)} %bitcast.10, ...), custom_call_target="tpu_custom_call" | custom-call | flops 5500000256 | bytes 1024 | tf_op jit(solution)/shard_map/ffn_other/pallas_call | solution.py:118
  31.6 4.0 %ffn.1 = (bf16[256,640]{1,0:T(8,128)(2,1)}, bf16[256,1024]{1,0:T(8,128)(2,1)S(1)}, bf16[256,1024]{1,0:T(8,128)(2,1)S(1)}, bf16[256,1024]{1,0:T(8,128)(2,1)S(1)},...) custom-call(f32[256,640]{1,0:T(8,128)S(1)} %get-tuple-element.117.after, ...), custom_call_target="tpu_custom_call" | custom-call | flops 4400000000 | bytes 1024 | tf_op jit(solution)/shard_map/ffn/pallas_call | solution.py:118
  35.7 4.2 %attend_grad.1 = (bf16[256,512]{1,0:T(8,128)(2,1)S(1)}, bf16[256,512]{1,0:T(8,128)(2,1)S(1)}, bf16[256,512]{1,0:T(8,128)(2,1)S(1)}, bf16[256,512]{1,0:T(8,128)(2...) custom-call(s32[4]{0:T(128)S(1)} %pad_add_fusion.where, ...), custom_call_target="tpu_custom_call" | custom-call | bytes 1024 | tf_op jit(solution)/shard_map/attend_grad/pallas_call | solution.py:118
  40.8 2.9 %ffn_grads.1 = (bf16[3840,128]{1,0:T(8,128)(2,1)S(1)}, bf16[3840,128]{1,0:T(8,128)(2,1)S(1)}, bf16[3840,128]{1,0:T(8,128)(2,1)S(1)}, bf16[3840,128]{1,0:T(8,128)(2,1)S(1)}) custom-call(s32[4]{0:T(128)S(1)} %pad_add_fusion.where, bf16[256,1024]{1,0:T(8,128)(2,1)S(1)} %get-tuple-element.136.hid_m, bf16[256,1024]{1,0:T(8,128)(2,1)S(1)} %collective-permute-done.11.hid_r, ...), custom_call_target="tpu_custom_call" | custom-call | flops 3300000000 | bytes 1024 | tf_op jit(solution)/shard_map/ffn_grads/pallas_call | solution.py:118
  43.8 3.8 %attend_grads.1 = (bf16[1664,128]{1,0:T(8,128)(2,1)S(1)}, bf16[1664,128]{1,0:T(8,128)(2,1)S(1)}, bf16[1664,128]{1,0:T(8,128)(2,1)S(1)}, bf16[1664,128]{1,0:T(8,128)(2,1)S(1)}) custom-call(s32[4]{0:T(128)S(1)} %pad_add_fusion.where, bf16[768,640]{1,0:T(8,128)(2,1)S(1)} %get-tuple-element.145.n, bf16[768,640]{1,0:T(8,128)(2,1)S(1)} %collective-permute-done.15.n_r, ...), custom_call_target="tpu_custom_call" | custom-call | bytes 1024 | tf_op jit(solution)/shard_map/attend_grads/pallas_call | solution.py:118
  48.6 4.2 %collective-permute-start.19 = (bf16[3840,128]{1,0:T(8,128)(2,1)S(1)}, bf16[3840,128]{1,0:T(8,128)(2,1)S(1)}, u32[]{:S(2)}, u32[]{:S(2)}) collective-permute-start(bf16[3840,128]{1,0:T(8,128)(2,1)S(1)} %get-tuple-element.154), channel_id=1, source_target_pairs={{0,64},{1,17},{2,66},{3,19},{4,68},{5,21},{6,70},{7,23},{8,72},{9,... | collective-permute-start | bytes 2949128 | tf_op jit(solution)/shard_map/ppermute | solution.py:608
  53.6 2.6 %collective-permute-start.21 = (bf16[3840,128]{1,0:T(8,128)(2,1)S(1)}, bf16[3840,128]{1,0:T(8,128)(2,1)S(1)}, u32[]{:S(2)}, u32[]{:S(2)}) collective-permute-start(bf16[3840,128]{1,0:T(8,128)(2,1)S(1)} %get-tuple-element.156), channel_id=1, source_target_pairs={{0,96},{1,25},{2,98},{3,27},{4,100},{5,29},{6,102},{7,31},{8,104},... | collective-permute-start | bytes 2949128 | tf_op jit(solution)/shard_map/ppermute | solution.py:608
  60.1 8.1 %collective-permute-done.22.a_one = bf16[1664,128]{1,0:T(8,128)(2,1)S(1)} collective-permute-done((bf16[1664,128]{1,0:T(8,128)(2,1)S(1)}, bf16[1664,128]{1,0:T(8,128)(2,1)S(1)}, u32[]{:S(2)}, u32[]{:S(2)}) %collective-permute-start.22) | collective-permute-done | bytes 426016 | tf_op jit(solution)/shard_map/ppermute | solution.py:75
  68.2 7.3 %collective-permute-done.20.r_one = bf16[3840,128]{1,0:T(8,128)(2,1)S(1)} collective-permute-done((bf16[3840,128]{1,0:T(8,128)(2,1)S(1)}, bf16[3840,128]{1,0:T(8,128)(2,1)S(1)}, u32[]{:S(2)}, u32[]{:S(2)}) %collective-permute-start.20) | collective-permute-done | bytes 983072 | tf_op jit(solution)/shard_map/ppermute | solution.py:608
  77.4 2.4 %collective-permute-start.25 = (bf16[1376,128]{1,0:T(8,128)(2,1)S(1)}, bf16[1376,128]{1,0:T(8,128)(2,1)S(1)}, u32[]{:S(2)}, u32[]{:S(2)}) collective-permute-start(bf16[1376,128]{1,0:T(8,128)(2,1)S(1)} %get-tuple-element.161), channel_id=1, source_target_pairs={{0,16},{1,65},{2,18},{3,67},{4,20},{5,69},{6,22},{7,71},{8,24},{9,... | collective-permute-start | bytes 1056776 | tf_op jit(solution)/shard_map/ppermute | solution.py:91
  80.2 2.8 %collective-permute-start.27 = (bf16[1376,128]{1,0:T(8,128)(2,1)S(1)}, bf16[1376,128]{1,0:T(8,128)(2,1)S(1)}, u32[]{:S(2)}, u32[]{:S(2)}) collective-permute-start(bf16[1376,128]{1,0:T(8,128)(2,1)S(1)} %get-tuple-element.163), channel_id=1, source_target_pairs={{0,24},{1,97},{2,26},{3,99},{4,28},{5,101},{6,30},{7,103},{8,0},{9... | collective-permute-start | bytes 1056776 | tf_op jit(solution)/shard_map/ppermute | solution.py:91
  83.0 3.4 %collective-permute-done.25 = bf16[1376,128]{1,0:T(8,128)(2,1)S(1)} collective-permute-done((bf16[1376,128]{1,0:T(8,128)(2,1)S(1)}, bf16[1376,128]{1,0:T(8,128)(2,1)S(1)}, u32[]{:S(2)}, u32[]{:S(2)}) %collective-permute-start.25) | collective-permute-done | bytes 352288 | tf_op jit(solution)/shard_map/ppermute | solution.py:91
  86.4 3.7 %collective-permute-done.26 = bf16[1376,128]{1,0:T(8,128)(2,1)S(1)} collective-permute-done((bf16[1376,128]{1,0:T(8,128)(2,1)S(1)}, bf16[1376,128]{1,0:T(8,128)(2,1)S(1)}, u32[]{:S(2)}, u32[]{:S(2)}) %collective-permute-start.26) | collective-permute-done | bytes 352288 | tf_op jit(solution)/shard_map/ppermute | solution.py:91
  96.4 3.9 %collective-permute-done.30 = bf16[960,128]{1,0:T(8,128)(2,1)S(1)} collective-permute-done((bf16[960,128]{1,0:T(8,128)(2,1)S(1)}, bf16[960,128]{1,0:T(8,128)(2,1)S(1)}, u32[]{:S(2)}, u32[]{:S(2)}) %collective-permute-start.30) | collective-permute-done | bytes 245792 | tf_op jit(solution)/shard_map/ppermute | solution.py:75
  100.3 4.2 %collective-permute-start.33 = (bf16[416,128]{1,0:T(8,128)(2,1)S(1)}, bf16[416,128]{1,0:T(8,128)(2,1)S(1)}, u32[]{:S(2)}, u32[]{:S(2)}) collective-permute-start(bf16[416,128]{1,0:T(8,128)(2,1)S(1)} %add_convert_fusion.5), channel_id=1, source_target_pairs={{0,96},{1,25},{2,98},{3,27},{4,100},{5,29},{6,102},{7,31},{8,104},... | collective-permute-start | bytes 319496 | tf_op jit(solution)/shard_map/ppermute | solution.py:83
  104.6 2.3 %collective-permute-done.29.back_two = bf16[256,512]{1,0:T(8,128)(2,1)S(1)} collective-permute-done((bf16[256,512]{1,0:T(8,128)(2,1)S(1)}, bf16[256,512]{1,0:T(8,128)(2,1)S(1)}, u32[]{:S(2)}, u32[]{:S(2)}) %collective-permute-start.29) | collective-permute-done | bytes 262176 | tf_op jit(solution)/shard_map/ppermute | solution.py:98
  106.9 3.9 %collective-permute-done.28.back_one = bf16[256,512]{1,0:T(8,128)(2,1)S(1)} collective-permute-done((bf16[256,512]{1,0:T(8,128)(2,1)S(1)}, bf16[256,512]{1,0:T(8,128)(2,1)S(1)}, u32[]{:S(2)}, u32[]{:S(2)}) %collective-permute-start.28) | collective-permute-done | bytes 262176 | tf_op jit(solution)/shard_map/ppermute | solution.py:98
  113.1 3.2 %collective-permute-start.36 = (bf16[1376,128]{1,0:T(8,128)(2,1)S(1)}, bf16[1376,128]{1,0:T(8,128)(2,1)S(1)}, u32[]{:S(2)}, u32[]{:S(2)}) collective-permute-start(bf16[1376,128]{1,0:T(8,128)(2,1)S(1)} %pad_maximum_fusion.own), channel_id=1, source_target_pairs={{0,16},{1,65},{2,18},{3,67},{4,20},{5,69},{6,22},{7,71},{8,24},{9,... | collective-permute-start | bytes 1056776 | tf_op jit(solution)/shard_map/ppermute | solution.py:91
  117.0 2.4 %collective-permute-start.38 = (bf16[1376,128]{1,0:T(8,128)(2,1)S(1)}, bf16[1376,128]{1,0:T(8,128)(2,1)S(1)}, u32[]{:S(2)}, u32[]{:S(2)}) collective-permute-start(bf16[1376,128]{1,0:T(8,128)(2,1)S(1)} %pad_maximum_fusion.own), channel_id=1, source_target_pairs={{0,24},{1,97},{2,26},{3,99},{4,28},{5,101},{6,30},{7,103},{8,0},{9... | collective-permute-start | bytes 1056776 | tf_op jit(solution)/shard_map/ppermute | solution.py:91
  119.5 2.6 %collective-permute-done.36.r_two = bf16[1376,128]{1,0:T(8,128)(2,1)S(1)} collective-permute-done((bf16[1376,128]{1,0:T(8,128)(2,1)S(1)}, bf16[1376,128]{1,0:T(8,128)(2,1)S(1)}, u32[]{:S(2)}, u32[]{:S(2)}) %collective-permute-start.36) | collective-permute-done | bytes 352288 | tf_op jit(solution)/shard_map/ppermute | solution.py:91
  122.0 3.7 %collective-permute-done.37.r_one = bf16[1376,128]{1,0:T(8,128)(2,1)S(1)} collective-permute-done((bf16[1376,128]{1,0:T(8,128)(2,1)S(1)}, bf16[1376,128]{1,0:T(8,128)(2,1)S(1)}, u32[]{:S(2)}, u32[]{:S(2)}) %collective-permute-start.37) | collective-permute-done | bytes 352288 | tf_op jit(solution)/shard_map/ppermute | solution.py:91
  128.0 3.1 %collective-permute-start.43 = (bf16[3840,128]{1,0:T(8,128)(2,1)S(1)}, bf16[3840,128]{1,0:T(8,128)(2,1)S(1)}, u32[]{:S(2)}, u32[]{:S(2)}) collective-permute-start(bf16[3840,128]{1,0:T(8,128)(2,1)S(1)} %get-tuple-element.180.refs_0_), channel_id=1, source_target_pairs={{0,64},{1,17},{2,66},{3,19},{4,68},{5,21},{6,70},{7,23},{8,72},{9,... | collective-permute-start | bytes 2949128 | tf_op jit(solution)/shard_map/ppermute | solution.py:91
  131.1 3.2 %collective-permute-start.41 = (bf16[3840,128]{1,0:T(8,128)(2,1)S(1)}, bf16[3840,128]{1,0:T(8,128)(2,1)S(1)}, u32[]{:S(2)}, u32[]{:S(2)}) collective-permute-start(bf16[3840,128]{1,0:T(8,128)(2,1)S(1)} %get-tuple-element.180.refs_0_), channel_id=1, source_target_pairs={{0,96},{1,25},{2,98},{3,27},{4,100},{5,29},{6,102},{7,31},{8,104},... | collective-permute-start | bytes 2949128 | tf_op jit(solution)/shard_map/ppermute | solution.py:91
  134.3 2.9 %collective-permute-start.45 = (bf16[1664,128]{1,0:T(8,128)(2,1)S(1)}, bf16[1664,128]{1,0:T(8,128)(2,1)S(1)}, u32[]{:S(2)}, u32[]{:S(2)}) collective-permute-start(bf16[1664,128]{1,0:T(8,128)(2,1)S(1)} %get-tuple-element.179.refs_1_), channel_id=1, source_target_pairs={{0,4},{1,5},{2,6},{3,7},{4,0},{5,1},{6,2},{7,3},{8,12},{9,13},{10,... | collective-permute-start | bytes 1277960 | tf_op jit(solution)/shard_map/ppermute | solution.py:647
  137.3 6.4 %collective-permute-done.43.refs_0_ = bf16[3840,128]{1,0:T(8,128)(2,1)S(1)} collective-permute-done((bf16[3840,128]{1,0:T(8,128)(2,1)S(1)}, bf16[3840,128]{1,0:T(8,128)(2,1)S(1)}, u32[]{:S(2)}, u32[]{:S(2)}) %collective-permute-start.43) | collective-permute-done | bytes 983072 | tf_op jit(solution)/shard_map/ppermute | solution.py:91
  143.7 2.7 %collective-permute-start.44 = (bf16[1664,128]{1,0:T(8,128)(2,1)S(1)}, bf16[1664,128]{1,0:T(8,128)(2,1)S(1)}, u32[]{:S(2)}, u32[]{:S(2)}) collective-permute-start(bf16[1664,128]{1,0:T(8,128)(2,1)S(1)} %get-tuple-element.179.refs_1_), channel_id=1, source_target_pairs={{0,6},{1,3},{2,0},{3,5},{4,2},{5,7},{6,4},{7,1},{8,14},{9,11},{10,... | collective-permute-start | bytes 1277960 | tf_op jit(solution)/shard_map/ppermute | solution.py:659
  146.5 2.3 %token_grad.1 = (f32[256,640]{1,0:T(8,128)}, f32[320]{0:T(512)}, f32[320]{0:T(512)}) custom-call(s32[4]{0:T(128)S(1)} %pad_add_fusion.where, bf16[256,640]{1,0:T(8,128)(2,1)S(1)} %bitcast.16, f32[1,640]{1,0:T(1,128)S(1)} %maximum_convert_fusion.1.gain, f32[256,640]{1,0:T(8,128)S(1)} %get-tuple-element.125.grad_after, ...), custom_call_target="tpu_custom_call" | custom-call | flops 2200000000 | bytes 1024 | tf_op jit(solution)/shard_map/token_grad/pallas_call | solution.py:118
  151.0 2.2 %spread.4 = (f32[640,1024]{1,0:T(8,128)}, f32[640,1024]{1,0:T(8,128)}, f32[1024,640]{1,0:T(8,128)}, f32[640,512]{1,0:T(8,128)}, f32[640,128]{1,0:T(8,128)}, /*index=5*/f32[640,128]{1,0:T(8,128)}, f32[512,640]{1,0:T(8,128)}) custom-call(s32[4]{0:T(128)S(1)} %pad_add_fusion.where, ...), custom_call_target="tpu_custom_call", output_to_operand_aliasing={{0}: (3, {}), {1}: (4, {}), {2}: (5, {}), {3}: (6, {}), {4}... | custom-call | flops 1024 | bytes 1024 | tf_op jit(solution)/shard_map/spread/pallas_call | solution.py:483
  155.0 3.1 %spread.5 = (f32[640,1024]{1,0:T(8,128)}, f32[640,1024]{1,0:T(8,128)}, f32[1024,640]{1,0:T(8,128)}, f32[640,512]{1,0:T(8,128)}, f32[640,128]{1,0:T(8,128)}, /*index=5*/f32[640,128]{1,0:T(8,128)}, f32[512,640]{1,0:T(8,128)}) custom-call(s32[4]{0:T(128)S(1)} %pad_add_fusion.where, ...), custom_call_target="tpu_custom_call", output_to_operand_aliasing={{0}: (5, {}), {1}: (6, {}), {2}: (7, {}), {3}: (8, {}), {4}... | custom-call | flops 1024 | bytes 1024 | tf_op jit(solution)/shard_map/spread/pallas_call | solution.py:483
  (120 shorter events, 41.2 us)
Async XLA Ops:
  0.6 21.7 %collective-permute-start = (bf16[256,640]{1,0:T(8,128)(2,1)}, bf16[256,640]{1,0:T(8,128)(2,1)S(1)}, u32[]{:S(2)}, u32[]{:S(2)}) collective-permute-start(bf16[256,640]{1,0:T(8,128)(2,1)} %bitcast.13), channel_id=1, source_target_pairs={{0,4},{2,6},{4,8},{6,10},{8,12},{10,14},{12,16},{14,18},{16,20},{1... | collective-permute-start | bytes 983048 | tf_op jit(solution)/shard_map/ppermute | solution.py:98
  5.9 16.5 %collective-permute-start.1 = (bf16[256,640]{1,0:T(8,128)(2,1)}, bf16[256,640]{1,0:T(8,128)(2,1)S(1)}, u32[]{:S(2)}, u32[]{:S(2)}) collective-permute-start(bf16[256,640]{1,0:T(8,128)(2,1)} %bitcast.14), channel_id=1, source_target_pairs={{0,2},{2,4},{4,6},{6,8},{8,10},{10,12},{12,14},{14,16},{16,18},{18... | collective-permute-start | bytes 983048 | tf_op jit(solution)/shard_map/ppermute | solution.py:98
  13.1 9.3 %collective-permute-start.8 = (bf16[256,640]{1,0:T(8,128)(2,1)}, bf16[256,640]{1,0:T(8,128)(2,1)S(1)}, u32[]{:S(2)}, u32[]{:S(2)}) collective-permute-start(bf16[256,640]{1,0:T(8,128)(2,1)} %bitcast.9), channel_id=1, source_target_pairs={{0,1},{1,0},{2,3},{3,2},{4,5},{5,4},{6,7},{7,6},{8,9},{9,8},{10,11... | collective-permute-start | bytes 983048 | tf_op jit(solution)/shard_map/ppermute | solution.py:31
  15.6 7.4 %collective-permute-start.7 = (bf16[640,1024]{1,0:T(8,128)(2,1)}, bf16[640,1024]{1,0:T(8,128)(2,1)S(1)}, u32[]{:S(2)}, u32[]{:S(2)}) collective-permute-start(bf16[640,1024]{1,0:T(8,128)(2,1)} %wg.1), channel_id=1, source_target_pairs={{0,1},{1,0},{2,3},{3,2},{4,5},{5,4},{6,7},{7,6},{8,9},{9,8},{10,11... | collective-permute-start | bytes 3932168 | tf_op jit(solution)/shard_map/ppermute | solution.py:31
  30.4 9.9 %collective-permute-start.11 = (bf16[256,1024]{1,0:T(8,128)(2,1)S(1)}, bf16[256,1024]{1,0:T(8,128)(2,1)S(1)}, u32[]{:S(2)}, u32[]{:S(2)}) collective-permute-start(bf16[256,1024]{1,0:T(8,128)(2,1)S(1)} %get-tuple-element.137), channel_id=1, source_target_pairs={{0,1},{1,0},{2,3},{3,2},{4,5},{5,4},{6,7},{7,6},{8,9},{9,8},{10,11... | collective-permute-start | bytes 1572872 | tf_op jit(solution)/shard_map/ppermute | solution.py:31
  30.6 9.3 %collective-permute-start.14 = (bf16[256,640]{1,0:T(8,128)(2,1)S(1)}, bf16[256,640]{1,0:T(8,128)(2,1)S(1)}, u32[]{:S(2)}, u32[]{:S(2)}) collective-permute-start(bf16[256,640]{1,0:T(8,128)(2,1)S(1)} %get-tuple-element.142.normed_two.n), channel_id=1, source_target_pairs={{0,1},{1,0},{2,3},{3,2},{4,5},{5,4},{6,7},{7,6},{8,9},{9,8},{10,11... | collective-permute-start | bytes 983048 | tf_op jit(solution)/shard_map/ppermute | solution.py:31
  31.0 9.5 %collective-permute-start.12 = (bf16[256,1024]{1,0:T(8,128)(2,1)S(1)}, bf16[256,1024]{1,0:T(8,128)(2,1)S(1)}, u32[]{:S(2)}, u32[]{:S(2)}) collective-permute-start(bf16[256,1024]{1,0:T(8,128)(2,1)S(1)} %get-tuple-element.139), channel_id=1, source_target_pairs={{0,1},{1,0},{2,3},{3,2},{4,5},{5,4},{6,7},{7,6},{8,9},{9,8},{10,11... | collective-permute-start | bytes 1572872 | tf_op jit(solution)/shard_map/ppermute | solution.py:31
  31.1 9.7 %collective-permute-start.13 = (bf16[256,1024]{1,0:T(8,128)(2,1)S(1)}, bf16[256,1024]{1,0:T(8,128)(2,1)S(1)}, u32[]{:S(2)}, u32[]{:S(2)}) collective-permute-start(bf16[256,1024]{1,0:T(8,128)(2,1)S(1)} %get-tuple-element.141), channel_id=1, source_target_pairs={{0,1},{1,0},{2,3},{3,2},{4,5},{5,4},{6,7},{7,6},{8,9},{9,8},{10,11... | collective-permute-start | bytes 1572872 | tf_op jit(solution)/shard_map/ppermute | solution.py:31
  31.5 12.3 %collective-permute-start.15 = (bf16[768,640]{1,0:T(8,128)(2,1)S(1)}, bf16[768,640]{1,0:T(8,128)(2,1)S(1)}, u32[]{:S(2)}, u32[]{:S(2)}) collective-permute-start(bf16[768,640]{1,0:T(8,128)(2,1)S(1)} %get-tuple-element.145.n), channel_id=1, source_target_pairs={{0,1},{1,0},{2,3},{3,2},{4,5},{5,4},{6,7},{7,6},{8,9},{9,8},{10,11... | collective-permute-start | bytes 2949128 | tf_op jit(solution)/shard_map/ppermute | solution.py:31
  47.6 10.4 %collective-permute-start.23 = (bf16[1664,128]{1,0:T(8,128)(2,1)S(1)}, bf16[1664,128]{1,0:T(8,128)(2,1)S(1)}, u32[]{:S(2)}, u32[]{:S(2)}) collective-permute-start(bf16[1664,128]{1,0:T(8,128)(2,1)S(1)} %get-tuple-element.159), channel_id=1, source_target_pairs={{0,2},{1,7},{2,0},{3,5},{4,6},{5,3},{6,4},{7,1},{8,10},{9,15},{10,... | collective-permute-start | bytes 1277960 | tf_op jit(solution)/shard_map/ppermute | solution.py:75
  48.6 19.6 %collective-permute-start.19 = (bf16[3840,128]{1,0:T(8,128)(2,1)S(1)}, bf16[3840,128]{1,0:T(8,128)(2,1)S(1)}, u32[]{:S(2)}, u32[]{:S(2)}) collective-permute-start(bf16[3840,128]{1,0:T(8,128)(2,1)S(1)} %get-tuple-element.154), channel_id=1, source_target_pairs={{0,64},{1,17},{2,66},{3,19},{4,68},{5,21},{6,70},{7,23},{8,72},{9,... | collective-permute-start | bytes 2949128 | tf_op jit(solution)/shard_map/ppermute | solution.py:608
  52.9 22.6 %collective-permute-start.20 = (bf16[3840,128]{1,0:T(8,128)(2,1)S(1)}, bf16[3840,128]{1,0:T(8,128)(2,1)S(1)}, u32[]{:S(2)}, u32[]{:S(2)}) collective-permute-start(bf16[3840,128]{1,0:T(8,128)(2,1)S(1)} %get-tuple-element.155), channel_id=1, source_target_pairs={{0,32},{1,9},{2,34},{3,11},{4,36},{5,13},{6,38},{7,15},{8,40},{9,1... | collective-permute-start | bytes 2949128 | tf_op jit(solution)/shard_map/ppermute | solution.py:608
  53.6 22.6 %collective-permute-start.21 = (bf16[3840,128]{1,0:T(8,128)(2,1)S(1)}, bf16[3840,128]{1,0:T(8,128)(2,1)S(1)}, u32[]{:S(2)}, u32[]{:S(2)}) collective-permute-start(bf16[3840,128]{1,0:T(8,128)(2,1)S(1)} %get-tuple-element.156), channel_id=1, source_target_pairs={{0,96},{1,25},{2,98},{3,27},{4,100},{5,29},{6,102},{7,31},{8,104},... | collective-permute-start | bytes 2949128 | tf_op jit(solution)/shard_map/ppermute | solution.py:608
  56.1 12.1 %collective-permute-start.22 = (bf16[1664,128]{1,0:T(8,128)(2,1)S(1)}, bf16[1664,128]{1,0:T(8,128)(2,1)S(1)}, u32[]{:S(2)}, u32[]{:S(2)}) collective-permute-start(bf16[1664,128]{1,0:T(8,128)(2,1)S(1)} %get-tuple-element.157), channel_id=1, source_target_pairs={{0,2},{1,7},{2,0},{3,5},{4,6},{5,3},{6,4},{7,1},{8,10},{9,15},{10,... | collective-permute-start | bytes 1277960 | tf_op jit(solution)/shard_map/ppermute | solution.py:75
  58.2 18.0 %collective-permute-start.24 = (bf16[1664,128]{1,0:T(8,128)(2,1)S(1)}, bf16[1664,128]{1,0:T(8,128)(2,1)S(1)}, u32[]{:S(2)}, u32[]{:S(2)}) collective-permute-start(bf16[1664,128]{1,0:T(8,128)(2,1)S(1)} %add_convert_fusion), channel_id=1, source_target_pairs={{0,6},{1,3},{2,4},{3,1},{4,2},{5,7},{6,0},{7,5},{8,14},{9,11},{10,... | collective-permute-start | bytes 1277960 | tf_op jit(solution)/shard_map/ppermute | solution.py:75
  77.4 9.0 %collective-permute-start.25 = (bf16[1376,128]{1,0:T(8,128)(2,1)S(1)}, bf16[1376,128]{1,0:T(8,128)(2,1)S(1)}, u32[]{:S(2)}, u32[]{:S(2)}) collective-permute-start(bf16[1376,128]{1,0:T(8,128)(2,1)S(1)} %get-tuple-element.161), channel_id=1, source_target_pairs={{0,16},{1,65},{2,18},{3,67},{4,20},{5,69},{6,22},{7,71},{8,24},{9,... | collective-permute-start | bytes 1056776 | tf_op jit(solution)/shard_map/ppermute | solution.py:91
  79.8 10.3 %collective-permute-start.26 = (bf16[1376,128]{1,0:T(8,128)(2,1)S(1)}, bf16[1376,128]{1,0:T(8,128)(2,1)S(1)}, u32[]{:S(2)}, u32[]{:S(2)}) collective-permute-start(bf16[1376,128]{1,0:T(8,128)(2,1)S(1)} %get-tuple-element.162), channel_id=1, source_target_pairs={{0,8},{1,33},{2,10},{3,35},{4,12},{5,37},{6,14},{7,39},{8,16},{9,4... | collective-permute-start | bytes 1056776 | tf_op jit(solution)/shard_map/ppermute | solution.py:91
  80.2 9.9 %collective-permute-start.27 = (bf16[1376,128]{1,0:T(8,128)(2,1)S(1)}, bf16[1376,128]{1,0:T(8,128)(2,1)S(1)}, u32[]{:S(2)}, u32[]{:S(2)}) collective-permute-start(bf16[1376,128]{1,0:T(8,128)(2,1)S(1)} %get-tuple-element.163), channel_id=1, source_target_pairs={{0,24},{1,97},{2,26},{3,99},{4,28},{5,101},{6,30},{7,103},{8,0},{9... | collective-permute-start | bytes 1056776 | tf_op jit(solution)/shard_map/ppermute | solution.py:91
  91.7 8.5 %collective-permute-start.30 = (bf16[960,128]{1,0:T(8,128)(2,1)S(1)}, bf16[960,128]{1,0:T(8,128)(2,1)S(1)}, u32[]{:S(2)}, u32[]{:S(2)}) collective-permute-start(bf16[960,128]{1,0:T(8,128)(2,1)S(1)} %add_convert_fusion.3), channel_id=1, source_target_pairs={{0,2},{1,7},{2,0},{3,5},{4,6},{5,3},{6,4},{7,1},{8,10},{9,15},{10,... | collective-permute-start | bytes 737288 | tf_op jit(solution)/shard_map/ppermute | solution.py:75
  93.7 13.1 %collective-permute-start.29 = (bf16[256,512]{1,0:T(8,128)(2,1)S(1)}, bf16[256,512]{1,0:T(8,128)(2,1)S(1)}, u32[]{:S(2)}, u32[]{:S(2)}) collective-permute-start(bf16[256,512]{1,0:T(8,128)(2,1)S(1)} %get-tuple-element.166), channel_id=1, source_target_pairs={{4,0},{6,2},{8,4},{10,6},{12,8},{14,10},{16,12},{18,14},{20,16},{2... | collective-permute-start | bytes 786440 | tf_op jit(solution)/shard_map/ppermute | solution.py:98
  95.0 15.7 %collective-permute-start.28 = (bf16[256,512]{1,0:T(8,128)(2,1)S(1)}, bf16[256,512]{1,0:T(8,128)(2,1)S(1)}, u32[]{:S(2)}, u32[]{:S(2)}) collective-permute-start(bf16[256,512]{1,0:T(8,128)(2,1)S(1)} %get-tuple-element.164), channel_id=1, source_target_pairs={{2,0},{4,2},{6,4},{8,6},{10,8},{12,10},{14,12},{16,14},{18,16},{20... | collective-permute-start | bytes 786440 | tf_op jit(solution)/shard_map/ppermute | solution.py:98
  100.3 11.7 %collective-permute-start.33 = (bf16[416,128]{1,0:T(8,128)(2,1)S(1)}, bf16[416,128]{1,0:T(8,128)(2,1)S(1)}, u32[]{:S(2)}, u32[]{:S(2)}) collective-permute-start(bf16[416,128]{1,0:T(8,128)(2,1)S(1)} %add_convert_fusion.5), channel_id=1, source_target_pairs={{0,96},{1,25},{2,98},{3,27},{4,100},{5,29},{6,102},{7,31},{8,104},... | collective-permute-start | bytes 319496 | tf_op jit(solution)/shard_map/ppermute | solution.py:83
  104.6 7.8 %collective-permute-start.31 = (bf16[960,128]{1,0:T(8,128)(2,1)S(1)}, bf16[960,128]{1,0:T(8,128)(2,1)S(1)}, u32[]{:S(2)}, u32[]{:S(2)}) collective-permute-start(bf16[960,128]{1,0:T(8,128)(2,1)S(1)} %add_convert_fusion.2), channel_id=1, source_target_pairs={{0,6},{1,3},{2,4},{3,1},{4,2},{5,7},{6,0},{7,5},{8,14},{9,11},{10,... | collective-permute-start | bytes 737288 | tf_op jit(solution)/shard_map/ppermute | solution.py:75
  113.1 8.9 %collective-permute-start.36 = (bf16[1376,128]{1,0:T(8,128)(2,1)S(1)}, bf16[1376,128]{1,0:T(8,128)(2,1)S(1)}, u32[]{:S(2)}, u32[]{:S(2)}) collective-permute-start(bf16[1376,128]{1,0:T(8,128)(2,1)S(1)} %pad_maximum_fusion.own), channel_id=1, source_target_pairs={{0,16},{1,65},{2,18},{3,67},{4,20},{5,69},{6,22},{7,71},{8,24},{9,... | collective-permute-start | bytes 1056776 | tf_op jit(solution)/shard_map/ppermute | solution.py:91
  116.2 9.5 %collective-permute-start.37 = (bf16[1376,128]{1,0:T(8,128)(2,1)S(1)}, bf16[1376,128]{1,0:T(8,128)(2,1)S(1)}, u32[]{:S(2)}, u32[]{:S(2)}) collective-permute-start(bf16[1376,128]{1,0:T(8,128)(2,1)S(1)} %pad_maximum_fusion.own), channel_id=1, source_target_pairs={{0,8},{1,33},{2,10},{3,35},{4,12},{5,37},{6,14},{7,39},{8,16},{9,4... | collective-permute-start | bytes 1056776 | tf_op jit(solution)/shard_map/ppermute | solution.py:91
  117.0 9.1 %collective-permute-start.38 = (bf16[1376,128]{1,0:T(8,128)(2,1)S(1)}, bf16[1376,128]{1,0:T(8,128)(2,1)S(1)}, u32[]{:S(2)}, u32[]{:S(2)}) collective-permute-start(bf16[1376,128]{1,0:T(8,128)(2,1)S(1)} %pad_maximum_fusion.own), channel_id=1, source_target_pairs={{0,24},{1,97},{2,26},{3,99},{4,28},{5,101},{6,30},{7,103},{8,0},{9... | collective-permute-start | bytes 1056776 | tf_op jit(solution)/shard_map/ppermute | solution.py:91
  128.0 15.7 %collective-permute-start.43 = (bf16[3840,128]{1,0:T(8,128)(2,1)S(1)}, bf16[3840,128]{1,0:T(8,128)(2,1)S(1)}, u32[]{:S(2)}, u32[]{:S(2)}) collective-permute-start(bf16[3840,128]{1,0:T(8,128)(2,1)S(1)} %get-tuple-element.180.refs_0_), channel_id=1, source_target_pairs={{0,64},{1,17},{2,66},{3,19},{4,68},{5,21},{6,70},{7,23},{8,72},{9,... | collective-permute-start | bytes 2949128 | tf_op jit(solution)/shard_map/ppermute | solution.py:91
  131.1 23.8 %collective-permute-start.40 = (bf16[3840,128]{1,0:T(8,128)(2,1)S(1)}, bf16[3840,128]{1,0:T(8,128)(2,1)S(1)}, u32[]{:S(2)}, u32[]{:S(2)}) collective-permute-start(bf16[3840,128]{1,0:T(8,128)(2,1)S(1)} %get-tuple-element.180.refs_0_), channel_id=1, source_target_pairs={{0,32},{1,9},{2,34},{3,11},{4,36},{5,13},{6,38},{7,15},{8,40},{9,1... | collective-permute-start | bytes 2949128 | tf_op jit(solution)/shard_map/ppermute | solution.py:91
  131.1 23.8 %collective-permute-start.41 = (bf16[3840,128]{1,0:T(8,128)(2,1)S(1)}, bf16[3840,128]{1,0:T(8,128)(2,1)S(1)}, u32[]{:S(2)}, u32[]{:S(2)}) collective-permute-start(bf16[3840,128]{1,0:T(8,128)(2,1)S(1)} %get-tuple-element.180.refs_0_), channel_id=1, source_target_pairs={{0,96},{1,25},{2,98},{3,27},{4,100},{5,29},{6,102},{7,31},{8,104},... | collective-permute-start | bytes 2949128 | tf_op jit(solution)/shard_map/ppermute | solution.py:91
  134.3 16.6 %collective-permute-start.45 = (bf16[1664,128]{1,0:T(8,128)(2,1)S(1)}, bf16[1664,128]{1,0:T(8,128)(2,1)S(1)}, u32[]{:S(2)}, u32[]{:S(2)}) collective-permute-start(bf16[1664,128]{1,0:T(8,128)(2,1)S(1)} %get-tuple-element.179.refs_1_), channel_id=1, source_target_pairs={{0,4},{1,5},{2,6},{3,7},{4,0},{5,1},{6,2},{7,3},{8,12},{9,13},{10,... | collective-permute-start | bytes 1277960 | tf_op jit(solution)/shard_map/ppermute | solution.py:647
  137.3 17.7 %collective-permute-start.42 = (bf16[1664,128]{1,0:T(8,128)(2,1)S(1)}, bf16[1664,128]{1,0:T(8,128)(2,1)S(1)}, u32[]{:S(2)}, u32[]{:S(2)}) collective-permute-start(bf16[1664,128]{1,0:T(8,128)(2,1)S(1)} %get-tuple-element.179.refs_1_), channel_id=1, source_target_pairs={{0,2},{1,7},{2,4},{3,1},{4,6},{5,3},{6,0},{7,5},{8,10},{9,15},{10,... | collective-permute-start | bytes 1277960 | tf_op jit(solution)/shard_map/ppermute | solution.py:648
  143.7 11.2 %collective-permute-start.44 = (bf16[1664,128]{1,0:T(8,128)(2,1)S(1)}, bf16[1664,128]{1,0:T(8,128)(2,1)S(1)}, u32[]{:S(2)}, u32[]{:S(2)}) collective-permute-start(bf16[1664,128]{1,0:T(8,128)(2,1)S(1)} %get-tuple-element.179.refs_1_), channel_id=1, source_target_pairs={{0,6},{1,3},{2,0},{3,5},{4,2},{5,7},{6,4},{7,1},{8,14},{9,11},{10,... | collective-permute-start | bytes 1277960 | tf_op jit(solution)/shard_map/ppermute | solution.py:659
  (28 other events, 108.4 us)
